TPU v7x, 256 devices: a whole 4x4x8 slice. The times are simulated.
256 devices in a mesh: tower: 16 (over x, y), shard: 16 (over z, core).
Axes of the slice: x: 4, y: 4, z: 8, core: 2. Of those that a mesh axis runs over, the one named last changes fastest.
Arguments:
- pooled: bfloat16 [16, 6144, 48, 128], P('tower', None, 'shard'), may hold values from -6 to 6
- cross_down: bfloat16 [16, 2, 4096, 512], P('tower', None, 'shard'), may hold values from -0.09375 to 0.09375
- cross_up: bfloat16 [16, 2, 512, 4096], P('tower', None, None, 'shard'), may hold values from -0.25 to 0.25
- cross_bias: bfloat16 [16, 2, 4096], P('tower'), may hold values from -3 to 3
- comp_weight: bfloat16 [16, 4096, 256], P('tower', 'shard'), may hold values from -0.09375 to 0.09375
- comp_bias: bfloat16 [16, 256], P('tower'), may hold values from -3 to 3
- over_weight: bfloat16 [4096, 1024], P('tower', 'shard'), may hold values from -0.09375 to 0.09375
- over_bias: bfloat16 [1024], replicated, may hold values from -3 to 3
- table_tower: int32 [512], replicated, may hold values from 0 to 15, as said below
- table_owner: int32 [512], replicated, may hold values from 0 to 15, as said below
Outputs:
- scores: bfloat16 [16, 384, 1024], P('shard', 'tower')
Inputs may be any that keep to these rules, and one draw needn't show every extreme that they name: `table_tower`: each value names exactly 32 tables. `table_owner`: among the tables of one tower no value is named by more than 3 tables, and in every tower some value is named by exactly 3.
All inputs are finite; a program needn't handle non-finite values.
Results may differ from a plain program's by a relative error of at most 0.014.
Values may be sent and summed in bfloat16 or wider, within the bound.
No kernel may reach another device: no remote copies, remote signals or barrier semaphores. Data moves between devices by JAX's collectives and lax.ppermute only.
A program may use at most 128 MiB of HBM per device.

v0:
```python
import jax
import jax.numpy as jnp
from jax import lax
from jax.sharding import PartitionSpec as P


def slot_order(table_tower, table_owner, tower_id, per_tower, slot_most):
    table_count = table_tower.shape[0]
    index = jnp.arange(table_count, dtype=jnp.int32)
    inside = table_tower == tower_id
    earlier = index[None, :] < index[:, None]
    before = inside[None, :] & earlier
    position_in = jnp.sum(before.astype(jnp.int32), axis=1)
    same_owner = table_owner[None, :] == table_owner[:, None]
    own_slot = jnp.sum((before & same_owner).astype(jnp.int32), axis=1)
    wanted = table_owner * slot_most + own_slot
    picked = inside[None, :] & (
        position_in[None, :] == jnp.arange(per_tower, dtype=jnp.int32)[:, None]
    )
    return jnp.sum(jnp.where(picked, wanted[None, :], 0), axis=1)


def on_device(
    pooled,
    cross_down,
    cross_up,
    cross_bias,
    comp_weight,
    comp_bias,
    over_weight,
    over_bias,
    table_tower,
    table_owner,
):
    tower_id = lax.axis_index("tower")
    slot_most = pooled.shape[2]
    emb_width = pooled.shape[3]
    feature_count = cross_up.shape[3] * lax.axis_size("shard")
    per_tower = feature_count // emb_width
    received = lax.all_to_all(pooled, "shard", split_axis=1, concat_axis=2, tiled=True)
    wanted = slot_order(table_tower, table_owner, tower_id, per_tower, slot_most)
    tables = jnp.take(received[0], wanted, axis=1)
    sample_count = tables.shape[0]
    base = tables.reshape(sample_count, feature_count)
    state = base
    for section_index in range(cross_down.shape[1]):
        current = state
        lowered = jnp.dot(
            current,
            lax.all_gather(cross_down[0, section_index], "shard", axis=0, tiled=True),
            preferred_element_type=jnp.float32,
        ).astype(jnp.bfloat16)
        raised = jnp.dot(
            lowered,
            lax.all_gather(cross_up[0, section_index], "shard", axis=1, tiled=True),
            preferred_element_type=jnp.float32,
        )
        state = (
            base.astype(jnp.float32) * (raised + cross_bias[0, section_index].astype(jnp.float32))
            + state.astype(jnp.float32)
        ).astype(jnp.bfloat16)
    squeezed = jnp.dot(
        state,
        lax.all_gather(comp_weight[0], "shard", axis=0, tiled=True),
        preferred_element_type=jnp.float32,
    )
    squeezed = (squeezed + comp_bias[0].astype(jnp.float32)).astype(jnp.bfloat16)
    column_block = lax.all_gather(over_weight, "tower", axis=0, tiled=True)
    joined = lax.all_to_all(squeezed, "tower", split_axis=0, concat_axis=1, tiled=True)
    block_sums = jnp.dot(
        lax.all_gather(joined, "shard", axis=0, tiled=True),
        column_block,
        preferred_element_type=jnp.float32,
    )
    summed = lax.all_to_all(
        block_sums.astype(jnp.bfloat16), "shard", split_axis=0, concat_axis=1, tiled=True
    ).astype(block_sums.dtype)
    result = jax.nn.relu(summed + over_bias.astype(jnp.float32)).astype(jnp.bfloat16)
    return result.reshape(1, result.shape[0], result.shape[1])


def solution(mesh):
    placed = (
        P("tower", None, "shard", None),
        P("tower", None, "shard", None),
        P("tower", None, None, "shard"),
        P("tower", None, None),
        P("tower", "shard", None),
        P("tower", None),
        P("tower", "shard"),
        P(),
        P(),
        P(),
    )
    return jax.shard_map(
        on_device, mesh=mesh, in_specs=placed, out_specs=P("shard", "tower", None), check_vma=False
    )
```

profile of v0, /device:TPU:96, one launch (start us, length us, event | category | flops | bytes accessed | tf_op | source)
XLA Modules:
  0.0 418.8 jit_solution(1844951940065409984)
XLA Ops:
  6.5 0.0 all-gather.14.cloned.1.call-start
  6.5 1.9 fusion.40
  8.4 0.0 all-gather.14.cloned.1.call-update
  8.4 0.0 all-gather.16.cloned.1.call-start
  8.5 1.9 fusion.39
  10.3 0.0 all-gather.16.cloned.1.call-update
  10.4 0.0 all-gather.18.cloned.1.call-start
  10.4 0.7 all-gather.18.cloned.1.call-update
  11.1 0.0 all-gather.22.cloned.1.call-start
  11.1 0.5 all-gather.22.cloned.1.call-update
  11.7 9.4 %copy.27 = bf16[1,6144,3,128]{3,2,0,1:T(4,128)(2,1)} copy(bf16[1,6144,3,128]{3,1,2,0:T(8,128)(2,1)} %param.10) | data formatting | bytes 9437184 | tf_op args[0]
  21.0 0.0 copy-start.5
  21.0 0.0 copy-start.4
  21.0 0.0 copy-start.2
  21.1 0.0 copy-start
  21.1 7.8 %all-to-all-start = ((bf16[1,6144,3,128]{3,2,0,1:T(4,128)(2,1)}), bf16[1,6144,3,128]{3,2,0,1:T(4,128)(2,1)}, u32[]{:S(2)}, u32[]{:S(2)}) async-start(bf16[1,6144,3,128]{3,2,0,1:T(4,128)(2,1)} %copy.27), calls=%async_computation | async-start | bytes 12582912 | tf_op jit(solution)/shard_map/all_to_all | solution.py:40
  28.9 0.0 all-gather.20.cloned.1.call-start
  28.9 0.5 all-gather.20.cloned.1.call-update
  29.5 0.0 all-gather.12.cloned.1.call-start
  29.5 0.0 copy-done.5
  29.5 0.0 copy-done.4
  29.6 0.0 copy-done.2
  29.6 0.3 convert_reduce_fusion.1
  29.9 0.1 select_reduce_fusion
  30.1 0.1 broadcast_bitcast_fusion
  30.1 0.0 copy-done
  30.2 165.1 %all-to-all-done = bf16[1,6144,3,128]{3,2,0,1:T(4,128)(2,1)} async-done(((bf16[1,6144,3,128]{3,2,0,1:T(4,128)(2,1)}), bf16[1,6144,3,128]{3,2,0,1:T(4,128)(2,1)}, u32[]{:S(2)}, u32[]{:S(2)}) %all-to-all-start) | async-done | bytes 4718624 | tf_op jit(solution)/shard_map/all_to_all | solution.py:40
  195.2 3.5 copy.28
  198.7 2.4 copy.29
  201.2 3.5 gather_fusion
  204.6 0.0 all-gather.14.cloned.1.call-done
  204.7 1.3 all-gather.16.cloned.1.call-done
  206.0 8.7 %fusion.2 = bf16[384,4096]{1,0:T(8,128)(2,1)} fusion(bf16[1,1,512,4096]{3,2,1,0:T(8,128)(2,1)} %all-gather.16.cloned.1.call-done, f32[4096]{0:T(1024)S(1)} %bitcast.89, pred[4096]{0:T(1024)(128)(4,1)S(1)} %broadcast_bitcast_fusion, bf16[1,1,4096,512]{3,2,1,0:T(8,128)(2,1)} %all-gather.14.cloned.1.call-done, bf16[32,384,128]{2,1,0:T(8,128)(2,1)S(1)} %gather_fusion), kind=kOutput, calls=%fused_computation.5 | convolution fusion | flops 3232432128 | bytes 14700544 | tf_op jit(solution)/shard_map/dot_general | solution.py:53
  214.6 34.1 %all-gather.18.cloned.1.call-done = bf16[1,1,4096,512]{3,2,1,0:T(8,128)(2,1)} async-done(((bf16[1,1,256,512]{3,2,1,0:T(8,128)(2,1)}), bf16[1,1,4096,512]{3,2,1,0:T(8,128)(2,1)}) %all-gather.18.cloned.1.call-update) | async-done | bytes 4194320 | tf_op jit(solution)/shard_map/all_gather | solution.py:50
  248.8 5.7 %fusion.17 = bf16[384,512]{1,0:T(8,128)(2,1)} fusion(bf16[384,4096]{1,0:T(8,128)(2,1)} %fusion.2, bf16[1,1,4096,512]{3,2,1,0:T(8,128)(2,1)} %all-gather.18.cloned.1.call-done), kind=kOutput, calls=%fused_computation.17 | convolution fusion | flops 1610809344 | bytes 7733248 | tf_op jit(solution)/shard_map/dot_general | solution.py:48
  254.5 34.3 %all-gather.22.cloned.1.call-done = bf16[1,4096,256]{2,1,0:T(8,128)(2,1)} async-done(((bf16[1,256,256]{2,1,0:T(8,128)(2,1)}), bf16[1,4096,256]{2,1,0:T(8,128)(2,1)}) %all-gather.22.cloned.1.call-update) | async-done | bytes 2097168 | tf_op jit(solution)/shard_map/all_gather | solution.py:64
  288.8 48.6 %all-gather.20.cloned.1.call-done = bf16[1,1,512,4096]{3,2,1,0:T(8,128)(2,1)} async-done(((bf16[1,1,512,256]{3,2,1,0:T(8,128)(2,1)}), bf16[1,1,512,4096]{3,2,1,0:T(8,128)(2,1)}) %all-gather.20.cloned.1.call-update) | async-done | bytes 4194320 | tf_op jit(solution)/shard_map/all_gather | solution.py:55
  337.3 0.0 copy-start.1
  337.3 6.9 %fusion.27 = bf16[384,256]{1,0:T(8,128)(2,1)S(1)} fusion(bf16[1,4096,256]{2,1,0:T(8,128)(2,1)} %all-gather.22.cloned.1.call-done, bf16[384,4096]{1,0:T(8,128)(2,1)} %fusion.2, bf16[384,512]{1,0:T(8,128)(2,1)} %fusion.17, bf16[1,1,512,4096]{3,2,1,0:T(8,128)(2,1)} %all-gather.20.cloned.1.call-done, f32[4096]{0:T(1024)S(1)} %bitcast.88, ...), kind=kOutput, calls=%fused_computation.19 | convolution fusion | flops 2427125760 | bytes 13194240 | tf_op jit(solution)/shard_map/dot_general | solution.py:62
  344.2 14.9 %all_to_all.47 = bf16[16,24,256]{2,1,0:T(8,128)(2,1)S(1)} all-to-all(bf16[16,24,256]{2,1,0:T(8,128)(2,1)S(1)} %bitcast.87), channel_id=1, replica_groups=mesh['tower'=16,'shard'=16] {'tower'}, dimensions={0} | all-to-all | bytes 393216 | tf_op jit(solution)/shard_map/all_to_all | solution.py:69
  359.1 0.0 copy-start.3
  359.1 0.7 copy.35
  359.8 0.0 all-gather.12.cloned.1.call-update
  359.8 0.0 copy-done.1
  359.8 22.6 %all_gather.27 = bf16[4096,64]{0,1:T(8,128)(2,1)S(1)} all-gather(bf16[256,64]{0,1:T(8,128)(2,1)S(1)} %copy-done.1), channel_id=1, replica_groups=mesh['tower'=16,'shard'=16] {'tower'}, dimensions={0}, use_global_device_ids=true | all-gather | bytes 557056 | tf_op jit(solution)/shard_map/all_gather | solution.py:68
  382.4 14.9 %all-gather.12.cloned.1.call-done = bf16[384,4096]{1,0:T(8,128)(2,1)} async-done(((bf16[24,4096]{1,0:T(8,128)(2,1)}), bf16[384,4096]{1,0:T(8,128)(2,1)}) %all-gather.12.cloned.1.call-update) | async-done | bytes 3145744 | tf_op jit(solution)/shard_map/all_gather | solution.py:71
  397.3 3.0 convolution_convert_fusion
  400.3 0.1 copy.32
  400.4 0.7 reshape.108
  401.2 5.1 %all-to-all-start.2 = ((bf16[16,2,768]{2,1,0:T(2,128)(2,1)}), bf16[16,2,768]{2,1,0:T(2,128)(2,1)S(1)}, u32[]{:S(2)}, u32[]{:S(2)}) async-start(bf16[16,2,768]{2,1,0:T(2,128)(2,1)} %reshape.108), calls=%async_computation.2 | async-start | bytes 98304 | tf_op jit(solution)/shard_map/all_to_all | solution.py:75
  406.3 0.0 copy-done.3
  406.3 4.7 %all-to-all-done.2 = bf16[16,2,768]{2,1,0:T(2,128)(2,1)S(1)} async-done(((bf16[16,2,768]{2,1,0:T(2,128)(2,1)}), bf16[16,2,768]{2,1,0:T(2,128)(2,1)S(1)}, u32[]{:S(2)}, u32[]{:S(2)}) %all-to-all-start.2) | async-done | bytes 49184 | tf_op jit(solution)/shard_map/all_to_all | solution.py:75
  411.0 0.1 reshape.109
  411.2 0.1 reshape.94
  411.3 0.6 maximum_convert_fusion
  (10 shorter events, 0.1 us)
Async XLA Ops:
  6.5 198.1 %all-gather.14.cloned.1.call-start = ((), (), s32[]{:S(2)}) async-start(), calls=%async_computation.4 | async-start | bytes 4456448 | tf_op jit(solution)/shard_map/all_gather | solution.py:50
  8.4 197.5 %all-gather.16.cloned.1.call-start = ((), (), s32[]{:S(2)}) async-start(), calls=%async_computation.5 | async-start | bytes 4456448 | tf_op jit(solution)/shard_map/all_gather | solution.py:55
  10.4 238.4 %all-gather.18.cloned.1.call-start = ((), (), s32[]{:S(2)}) async-start(), calls=%async_computation.6 | async-start | bytes 4456448 | tf_op jit(solution)/shard_map/all_gather | solution.py:50
  11.1 277.7 %all-gather.22.cloned.1.call-start = ((), (), s32[]{:S(2)}) async-start(), calls=%async_computation.8 | async-start | bytes 2228224 | tf_op jit(solution)/shard_map/all_gather | solution.py:64
  21.0 8.5 %copy-start.5 = (bf16[1,256]{1,0:T(2,128)(2,1)S(1)}, bf16[1,256]{1,0:T(2,128)(2,1)}, u32[]{:S(2)}) copy-start(bf16[1,256]{1,0:T(2,128)(2,1)} %param.15) | copy-start | bytes 1540
  21.0 8.5 %copy-start.4 = (s32[512]{0:T(512)S(1)}, s32[512]{0:T(512)}, u32[]{:S(2)}) copy-start(s32[512]{0:T(512)} %param.18) | copy-start | bytes 6148
  21.0 8.5 %copy-start.2 = (s32[512]{0:T(512)S(1)}, s32[512]{0:T(512)}, u32[]{:S(2)}) copy-start(s32[512]{0:T(512)} %param.19) | copy-start | bytes 6148
  21.1 9.1 %copy-start = (bf16[1,2,4096]{2,1,0:T(2,128)(2,1)S(1)}, bf16[1,2,4096]{2,1,0:T(2,128)(2,1)}, u32[]{:S(2)}) copy-start(bf16[1,2,4096]{2,1,0:T(2,128)(2,1)} %param.13) | copy-start | bytes 49156
  21.1 174.2 %all-to-all-start = ((bf16[1,6144,3,128]{3,2,0,1:T(4,128)(2,1)}), bf16[1,6144,3,128]{3,2,0,1:T(4,128)(2,1)}, u32[]{:S(2)}, u32[]{:S(2)}) async-start(bf16[1,6144,3,128]{3,2,0,1:T(4,128)(2,1)} %copy.27), calls=%async_computation | async-start | bytes 12582912 | tf_op jit(solution)/shard_map/all_to_all | solution.py:40
  28.9 308.4 %all-gather.20.cloned.1.call-start = ((), (), s32[]{:S(2)}) async-start(), calls=%async_computation.7 | async-start | bytes 4456448 | tf_op jit(solution)/shard_map/all_gather | solution.py:55
  29.5 367.8 %all-gather.12.cloned.1.call-start = ((), (), s32[]{:S(2)}) async-start(), calls=%async_computation.3 | async-start | bytes 3342336 | tf_op jit(solution)/shard_map/all_gather | solution.py:71
  337.3 22.5 %copy-start.1 = (bf16[256,64]{0,1:T(8,128)(2,1)S(1)}, bf16[256,64]{0,1:T(8,128)(2,1)}, u32[]{:S(2)}) copy-start(bf16[256,64]{0,1:T(8,128)(2,1)} %param.16) | copy-start | bytes 98308
  359.1 47.2 %copy-start.3 = (bf16[1024]{0:T(1024)(128)(2,1)S(1)}, bf16[1024]{0:T(1024)(128)(2,1)}, u32[]{:S(2)}) copy-start(bf16[1024]{0:T(1024)(128)(2,1)} %param.17) | copy-start | bytes 6148
  401.2 9.8 %all-to-all-start.2 = ((bf16[16,2,768]{2,1,0:T(2,128)(2,1)}), bf16[16,2,768]{2,1,0:T(2,128)(2,1)S(1)}, u32[]{:S(2)}, u32[]{:S(2)}) async-start(bf16[16,2,768]{2,1,0:T(2,128)(2,1)} %reshape.108), calls=%async_computation.2 | async-start | bytes 98304 | tf_op jit(solution)/shard_map/all_to_all | solution.py:75
Sparse Core Ops, SparseCore 0:
  9.2 96.2 all-gather.13
  107.2 98.6 all-gather.15
  207.8 40.9 all-gather.17
  250.5 38.2 all-gather.21
  290.4 46.9 all-gather.19
  359.9 37.3 all-gather.11
where the time goes:
time: 424 us; the launch traced here: 419 us
  waiting for transfers between devices  305 us (72%)
  blocking collectives  37.5 us (9%)
  local copies, waits for them, and re-layouts  24.4 us (6%)
  matrix products  24.2 us (6%)
  between operations  13.6 us (3%)
  starting transfers between devices  13.1 us (3%)
    all_to_all x1, waiting for transfers between devices, on_device(): lax.all_to_all(pooled, 'shard', split_axis=1, concat_axis=2, tiled=True)  165 us
    all_gather x2, waiting for transfers between devices, on_device(): lax.all_gather(cross_up[0, section_index], 'shard', axis=1, tiled=True)  49.8 us
    all_gather x1, waiting for transfers between devices, on_device(): lax.all_gather(comp_weight[0], 'shard', axis=0, tiled=True)  34.3 us
    all_gather x2, waiting for transfers between devices, on_device(): lax.all_gather(cross_down[0, section_index], 'shard', axis=0, tiled=True)  34.2 us
    all_gather x1, blocking collectives, on_device(): column_block = lax.all_gather(over_weight, 'tower', axis=0, tiled=True)  22.6 us
    all_to_all x1, blocking collectives, on_device(): lax.all_to_all(squeezed, 'tower', split_axis=0, concat_axis=1, tiled=True)  14.9 us
    all_gather x1, waiting for transfers between devices, on_device(): lax.all_gather(joined, 'shard', axis=0, tiled=True)  14.9 us
    unnamed x15, local copies, waits for them, and re-layouts  10.3 us
  transfers between devices with their start and end apart: 8, of which 7 were waited for; matrix products, arithmetic and copies ran while one was open for 9% of the time, Pallas kernels for 0%

commit v1 on v0

v1 whole, which is shorter than its diff:
```python
import jax
import jax.numpy as jnp
from jax import lax
from jax.experimental import pallas as pl
from jax.experimental.pallas import tpu as pltpu
from jax.sharding import PartitionSpec as P

F32 = jnp.float32
BF16 = jnp.bfloat16


def slot_order(table_tower, table_owner, tower_id, per_tower, slot_most):
    table_count = table_tower.shape[0]
    index = jnp.arange(table_count, dtype=jnp.int32)
    inside = table_tower == tower_id
    earlier = index[None, :] < index[:, None]
    before = inside[None, :] & earlier
    position_in = jnp.sum(before.astype(jnp.int32), axis=1)
    same_owner = table_owner[None, :] == table_owner[:, None]
    own_slot = jnp.sum((before & same_owner).astype(jnp.int32), axis=1)
    wanted = table_owner * slot_most + own_slot
    picked = inside[None, :] & (
        position_in[None, :] == jnp.arange(per_tower, dtype=jnp.int32)[:, None]
    )
    return jnp.sum(jnp.where(picked, wanted[None, :], 0), axis=1)


def tower_kernel(
    slots, received, gathered, bias, comp_bias, over_rows, out, base, state, down0, down1, up, comp, sems
):
    rows, features = base.shape
    width = comp.shape[-1]
    shards, rank = up.shape[0], down0.shape[-1]
    step = features // shards
    for p in range(features // 128):
        pltpu.make_async_copy(
            received.at[slots[p]], base.at[:, pl.ds(p * 128, 128)], sems.at[0]
        ).start()
    copies = [
        pltpu.make_async_copy(gathered.at[:, :, pl.ds(0, 32), :], down0, sems.at[1]),
        pltpu.make_async_copy(gathered.at[:, :, pl.ds(64, 64), :], up, sems.at[2]),
        pltpu.make_async_copy(gathered.at[:, :, pl.ds(32, 32), :], down1, sems.at[3]),
    ] + [
        pltpu.make_async_copy(
            gathered.at[:, :, pl.ds(128, 16), pl.ds(half * width, width)],
            comp.at[:, half],
            sems.at[4 + half],
        )
        for half in range(2)
    ]
    for copy in copies:
        copy.start()
    pltpu.make_async_copy(base, base, sems.at[0]).wait()
    copies[0].wait()
    raise_by = up.reshape(shards, up.shape[1] * up.shape[2], up.shape[3])
    lowered = jnp.dot(
        base[...], down0.reshape(features, rank)[...], preferred_element_type=F32
    ).astype(BF16)
    copies[1].wait()
    for layer in range(2):
        for s in range(shards):
            here = pl.ds(s * step, step)
            raised = jnp.dot(
                lowered, raise_by[s, :, pl.ds(layer * step, step)], preferred_element_type=F32
            )
            part = base[:, here].astype(F32)
            held = part if layer == 0 else state[:, here].astype(F32)
            state[:, here] = (part * (raised + bias[layer : layer + 1, here]) + held).astype(BF16)
        if layer == 0:
            copies[2].wait()
            lowered = jnp.dot(
                state[...], down1.reshape(features, rank)[...], preferred_element_type=F32
            ).astype(BF16)
    copies[3].wait()
    copies[4].wait()
    squeezed = jnp.dot(state[...], comp.reshape(features, width)[...], preferred_element_type=F32)
    squeezed = (squeezed + comp_bias[...]).astype(BF16)
    out[...] = jnp.dot(squeezed, over_rows[...], preferred_element_type=F32).astype(BF16)


def on_device(
    pooled,
    cross_down,
    cross_up,
    cross_bias,
    comp_weight,
    comp_bias,
    over_weight,
    over_bias,
    table_tower,
    table_owner,
):
    tower_id = lax.axis_index("tower")
    shards, towers = lax.axis_size("shard"), lax.axis_size("tower")
    _, batch, slot_most, emb = pooled.shape
    layers, rank, step = cross_up.shape[1:]
    features = step * shards
    width = comp_weight.shape[2]
    samples = batch // shards
    outputs = over_weight.shape[1] * shards

    down_part = cross_down[0].reshape(layers, 8, step // 8, rank).transpose(1, 0, 2, 3)
    up_part = cross_up[0].transpose(1, 0, 2).reshape(8, rank // 8, layers * step)
    comp_part = comp_weight[0].reshape(2, step // 2, width).transpose(1, 0, 2)
    packed = jnp.concatenate(
        [
            down_part.reshape(8, layers * step // 8, rank),
            up_part,
            comp_part.reshape(8, step // 16, 2 * width),
        ],
        axis=1,
    )
    gathered = lax.all_gather(packed, "shard", axis=0)
    by_slot = pooled[0].transpose(1, 0, 2).reshape(slot_most, shards, samples, emb)
    received = lax.all_to_all(
        by_slot.transpose(1, 0, 2, 3), "shard", split_axis=0, concat_axis=0, tiled=True
    ).reshape(shards * slot_most, samples, emb)
    over_rows = lax.all_gather(over_weight, "shard", axis=1, tiled=True)
    slots = slot_order(table_tower, table_owner, tower_id, features // emb, slot_most)

    partial = pl.pallas_call(
        tower_kernel,
        grid_spec=pltpu.PrefetchScalarGridSpec(
            num_scalar_prefetch=1,
            grid=(1,),
            in_specs=[
                pl.BlockSpec(memory_space=pl.ANY),
                pl.BlockSpec(memory_space=pl.ANY),
                pl.BlockSpec((layers, features), lambda i, *_: (0, 0)),
                pl.BlockSpec((1, width), lambda i, *_: (0, 0)),
                pl.BlockSpec((width, outputs), lambda i, *_: (0, 0)),
            ],
            out_specs=pl.BlockSpec((samples, outputs), lambda i, *_: (0, 0)),
            scratch_shapes=[
                pltpu.VMEM((samples, features), BF16),
                pltpu.VMEM((samples, features), BF16),
                pltpu.VMEM((shards, 8, step // 8, rank), BF16),
                pltpu.VMEM((shards, 8, step // 8, rank), BF16),
                pltpu.VMEM((shards, 8, rank // 8, layers * step), BF16),
                pltpu.VMEM((shards, 2, 8, step // 16, width), BF16),
                pltpu.SemaphoreType.DMA((6,)),
            ],
        ),
        out_shape=jax.ShapeDtypeStruct((samples, outputs), BF16),
        compiler_params=pltpu.CompilerParams(vmem_limit_bytes=48 * 2**20),
        cost_estimate=pl.CostEstimate(flops=8 * 10**9, bytes_accessed=24 * 10**6, transcendentals=0),
    )(
        slots,
        received,
        gathered,
        cross_bias[0].astype(F32),
        comp_bias.astype(F32),
        over_rows,
    )
    summed = lax.all_to_all(
        partial.reshape(towers, samples // towers, outputs), "tower", 0, 0, tiled=True
    )
    total = jnp.sum(summed.astype(F32), axis=0) + over_bias.astype(F32)
    return jax.nn.relu(total).astype(BF16)[None]


def solution(mesh):
    placed = (
        P("tower", None, "shard", None),
        P("tower", None, "shard", None),
        P("tower", None, None, "shard"),
        P("tower", None, None),
        P("tower", "shard", None),
        P("tower", None),
        P("tower", "shard"),
        P(),
        P(),
        P(),
    )
    return jax.shard_map(
        on_device, mesh=mesh, in_specs=placed, out_specs=P("shard", "tower", None), check_vma=False
    )
```

time: 424 us -> 266 us (0.63)
  waiting for transfers between devices: 305 us -> 43 us
  blocking collectives: 37.5 us -> 168 us
  matrix products: 24.2 us -> 0 us
  local copies, waits for them, and re-layouts: 24.4 us -> 7.59 us
  Pallas kernels: 0 us -> 15 us
    all_to_all x2, waiting for transfers between devices: 170 us -> 15 us  [the longest x1 15 us: on_device(): lax.all_to_all(partial.reshape(towers, samples // towers, outputs), 'towe...]
    all_gather x1, blocking collectives: 22.6 us -> 168 us  [on_device(): over_rows = lax.all_gather(over_weight, 'shard', axis=1, tiled=True)]
    all_gather x6 -> x1, waiting for transfers between devices: 133 us -> 28 us  [on_device(): gathered = lax.all_gather(packed, 'shard', axis=0)]
    dot_general x4 -> x0, matrix products: 24.2 us -> none  [the longest x1 8.67 us: on_device(): jnp.dot(lowered, lax.all_gather(cross_up[0, section_index], 'shard', axis...]
    pallas_call x0 -> x1, Pallas kernels: none -> 15 us  [on_device(): pl.pallas_call(tower_kernel, grid_spec=pltpu.PrefetchScalarGridSpec(num_s...]
    all_to_all x1 -> x0, blocking collectives: 14.9 us -> none  [on_device(): lax.all_to_all(squeezed, 'tower', split_axis=0, concat_axis=1, tiled=True)]
    unnamed x15 -> x16, local copies, waits for them, and re-layouts: 10.3 us -> 0.03 us
    all_to_all x3 -> x0, local copies, waits for them, and re-layouts: 6.61 us -> none  [the longest x2 5.93 us: on_device(): lax.all_to_all(pooled, 'shard', split_axis=1, concat_axis=2, tiled=True)]
  transfers between devices with their start and end apart: 8 -> 3, of which waited for: 7 -> 2; matrix products, arithmetic and copies ran while one was open for 9% -> 2% of each run, Pallas kernels for 0% -> 0%
where the time goes in v1:
time: 266 us; the launch traced here: 264 us
  blocking collectives  168 us (63%)
  waiting for transfers between devices  43 us (16%)
  Pallas kernels  15 us (6%)
  starting transfers between devices  14.6 us (5%)
  between operations  13.6 us (5%)
  local copies, waits for them, and re-layouts  7.59 us (3%)
    all_gather x1, blocking collectives, on_device(): over_rows = lax.all_gather(over_weight, 'shard', axis=1, tiled=True)  168 us
    all_gather x1, waiting for transfers between devices, on_device(): gathered = lax.all_gather(packed, 'shard', axis=0)  28 us
    all_to_all x1, waiting for transfers between devices, on_device(): lax.all_to_all(partial.reshape(towers, samples // towers, outputs), 'towe...  15 us
    pallas_call x1, Pallas kernels, on_device(): pl.pallas_call(tower_kernel, grid_spec=pltpu.PrefetchScalarGridSpec(num_s...  15 us
    all_to_all x1, starting transfers between devices, on_device(): lax.all_to_all(by_slot.transpose(1, 0, 2, 3), 'shard', split_axis=0, conc...  7.82 us
    all_to_all x1, starting transfers between devices, on_device(): lax.all_to_all(partial.reshape(towers, samples // towers, outputs), 'towe...  6.82 us
  transfers between devices with their start and end apart: 3, of which 2 were waited for; matrix products, arithmetic and copies ran while one was open for 2% of the time, Pallas kernels for 0%

profile of v1, /device:TPU:96, one launch (start us, length us, event | category | flops | bytes accessed | tf_op | source)
XLA Modules:
  0.0 264.3 jit_solution(10356823625364203405)
XLA Ops:
  6.5 0.0 copy-start
  6.5 0.0 copy-start.1
  6.5 0.0 all-gather.3.cloned.1.call-start
  6.5 1.6 copy.27
  8.2 0.3 reshape.63
  8.5 0.0 copy-done
  8.6 0.0 copy-done.1
  8.6 0.1 copy.33
  8.7 0.1 reshape.64
  8.8 1.1 pad_maximum_fusion
  10.0 0.0 all-gather.3.cloned.1.call-update
  10.0 5.1 %copy.32 = bf16[3,16,384,128]{3,2,0,1:T(8,128)(2,1)} copy(bf16[3,16,384,128]{3,2,1,0:T(8,128)(2,1)} %bitcast.32) | data formatting | bytes 9437184 | tf_op jit(solution)/shard_map/reshape | solution.py:114
  15.1 0.0 copy-start.2
  15.1 0.0 copy-start.7
  15.1 0.0 copy-start.6
  15.1 0.0 copy-start.3
  15.1 0.0 copy-start.4
  15.1 7.8 %all-to-all-start = ((bf16[16,3,384,128]{3,2,1,0:T(8,128)(2,1)}), bf16[16,3,384,128]{3,2,1,0:T(8,128)(2,1)}, u32[]{:S(2)}, u32[]{:S(2)}) async-start(bf16[16,3,384,128]{3,2,1,0:T(8,128)(2,1)} %bitcast.31), calls=%async_computation | async-start | bytes 9437184 | tf_op jit(solution)/shard_map/all_to_all | solution.py:115
  23.0 0.0 copy-done.2
  23.0 168.1 %all_gather.11 = bf16[256,1024]{0,1:T(8,128)(2,1)S(1)} all-gather(bf16[256,64]{0,1:T(8,128)(2,1)S(1)} %copy-done.2), channel_id=1, replica_groups=mesh['tower'=16,'shard'=16] {'shard'}, dimensions={1}, use_global_device_ids=true | all-gather | bytes 557056 | tf_op jit(solution)/shard_map/all_gather | solution.py:118
  191.1 0.2 copy.29.over_rows
  191.3 0.0 copy-done.7
  191.3 0.0 copy-done.6
  191.3 0.0 copy-done.3
  191.3 0.3 convert_reduce_fusion.2
  191.7 0.1 select_reduce_fusion.slots
  191.8 0.0 copy-done.4
  191.8 0.0 all-to-all-done
  191.8 28.0 %all-gather.3.cloned.1.call-done = bf16[128,144,512]{2,1,0:T(8,128)(2,1)} async-done(((bf16[8,144,512]{2,1,0:T(8,128)(2,1)}), bf16[128,144,512]{2,1,0:T(8,128)(2,1)}) %all-gather.3.cloned.1.call-update) | async-done | bytes 18874384 | tf_op jit(solution)/shard_map/all_gather | solution.py:113
  219.8 0.0 copy-start.5
  219.8 15.0 %shard_map.100 = bf16[384,1024]{1,0:T(8,128)(2,1)} custom-call(s32[32]{0:T(128)S(1)} %select_reduce_fusion.slots, bf16[48,384,128]{2,1,0:T(8,128)(2,1)} %bitcast.4.received, bf16[16,8,144,512]{3,2,1,0:T(8,128)(2,1)} %bitcast.38, f32[2,4096]{1,0:T(2,128)S(1)} %bitcast_convert_fusion.bias, f32[1,256]{1,0:T(1,128)S(1)} %convert_element_type.34.comp_bias, ...), custom_call_target="tpu_custom_call" | custom-call | flops 8000000000 | bytes 24000000 | tf_op jit(solution)/shard_map/pallas_call | solution.py:121
  234.8 6.8 %all-to-all-start.1 = ((bf16[16,24,1024]{2,1,0:T(8,128)(2,1)}), bf16[16,24,1024]{2,1,0:T(8,128)(2,1)S(1)}, u32[]{:S(2)}, u32[]{:S(2)}) async-start(bf16[16,24,1024]{2,1,0:T(8,128)(2,1)} %bitcast.14), calls=%async_computation.1 | async-start | bytes 1572864 | tf_op jit(solution)/shard_map/all_to_all | solution.py:155
  241.6 0.0 copy-done.5
  241.7 15.0 %all-to-all-done.1 = bf16[16,24,1024]{2,1,0:T(8,128)(2,1)S(1)} async-done(((bf16[16,24,1024]{2,1,0:T(8,128)(2,1)}), bf16[16,24,1024]{2,1,0:T(8,128)(2,1)S(1)}, u32[]{:S(2)}, u32[]{:S(2)}) %all-to-all-start.1) | async-done | bytes 786464 | tf_op jit(solution)/shard_map/all_to_all | solution.py:155
  256.7 0.1 convert_reduce_fusion
  256.8 0.6 fusion.3
  (6 shorter events, 0.1 us)
Async XLA Ops:
  6.5 2.0 copy-start
  6.5 2.1 copy-start.1
  6.5 213.3 %all-gather.3.cloned.1.call-start = ((), (), s32[]{:S(2)}) async-start(), calls=%async_computation.2 | async-start | bytes 20054016 | tf_op jit(solution)/shard_map/all_gather | solution.py:113
  15.1 7.8 %copy-start.2 = (bf16[256,64]{0,1:T(8,128)(2,1)S(1)}, bf16[256,64]{0,1:T(8,128)(2,1)}, u32[]{:S(2)}) copy-start(bf16[256,64]{0,1:T(8,128)(2,1)} %param.16) | copy-start | bytes 98308
  15.1 176.2 %copy-start.7 = (bf16[1,256]{1,0:T(2,128)(2,1)S(1)}, bf16[1,256]{1,0:T(2,128)(2,1)}, u32[]{:S(2)}) copy-start(bf16[1,256]{1,0:T(2,128)(2,1)} %param.15) | copy-start | bytes 1540
  15.1 176.2 %copy-start.6 = (s32[512]{0:T(512)S(1)}, s32[512]{0:T(512)}, u32[]{:S(2)}) copy-start(s32[512]{0:T(512)} %param.18) | copy-start | bytes 6148
  15.1 176.2 %copy-start.3 = (s32[512]{0:T(512)S(1)}, s32[512]{0:T(512)}, u32[]{:S(2)}) copy-start(s32[512]{0:T(512)} %param.19) | copy-start | bytes 6148
  15.1 176.7 %copy-start.4 = (bf16[1,2,4096]{2,1,0:T(2,128)(2,1)S(1)}, bf16[1,2,4096]{2,1,0:T(2,128)(2,1)}, u32[]{:S(2)}) copy-start(bf16[1,2,4096]{2,1,0:T(2,128)(2,1)} %param.13) | copy-start | bytes 49156
  15.1 176.7 %all-to-all-start = ((bf16[16,3,384,128]{3,2,1,0:T(8,128)(2,1)}), bf16[16,3,384,128]{3,2,1,0:T(8,128)(2,1)}, u32[]{:S(2)}, u32[]{:S(2)}) async-start(bf16[16,3,384,128]{3,2,1,0:T(8,128)(2,1)} %bitcast.31), calls=%async_computation | async-start | bytes 9437184 | tf_op jit(solution)/shard_map/all_to_all | solution.py:115
  219.8 21.8 %copy-start.5 = (bf16[1024]{0:T(1024)(128)(2,1)S(1)}, bf16[1024]{0:T(1024)(128)(2,1)}, u32[]{:S(2)}) copy-start(bf16[1024]{0:T(1024)(128)(2,1)} %param.17) | copy-start | bytes 6148
  234.8 21.9 %all-to-all-start.1 = ((bf16[16,24,1024]{2,1,0:T(8,128)(2,1)}), bf16[16,24,1024]{2,1,0:T(8,128)(2,1)S(1)}, u32[]{:S(2)}, u32[]{:S(2)}) async-start(bf16[16,24,1024]{2,1,0:T(8,128)(2,1)} %bitcast.14), calls=%async_computation.1 | async-start | bytes 1572864 | tf_op jit(solution)/shard_map/all_to_all | solution.py:155
Sparse Core Ops, SparseCore 0:
  10.1 209.6 all-gather.2

commit v2 on v1

v2 whole, which is shorter than its diff:
```python
import jax
import jax.numpy as jnp
from jax import lax
from jax.experimental import pallas as pl
from jax.experimental.pallas import tpu as pltpu
from jax.sharding import PartitionSpec as P

F32 = jnp.float32
BF16 = jnp.bfloat16


def slot_order(table_tower, table_owner, tower_id, per_tower, slot_most):
    table_count = table_tower.shape[0]
    index = jnp.arange(table_count, dtype=jnp.int32)
    inside = table_tower == tower_id
    earlier = index[None, :] < index[:, None]
    before = inside[None, :] & earlier
    position_in = jnp.sum(before.astype(jnp.int32), axis=1)
    same_owner = table_owner[None, :] == table_owner[:, None]
    own_slot = jnp.sum((before & same_owner).astype(jnp.int32), axis=1)
    wanted = table_owner * slot_most + own_slot
    picked = inside[None, :] & (
        position_in[None, :] == jnp.arange(per_tower, dtype=jnp.int32)[:, None]
    )
    return jnp.sum(jnp.where(picked, wanted[None, :], 0), axis=1)


def tower_kernel(places, *refs):
    n_chunks = len(refs) - 15
    received, refs = refs[:n_chunks], refs[n_chunks:]
    gathered, refs = refs[:4], refs[4:]
    bias, comp_bias, over_rows, out, base, state, down0, down1, up, comp, sems = refs
    rows, features = base.shape
    width, rank = comp.shape[-1], down0.shape[-1]
    shards = 2 * up.shape[0]
    step, tables, chunk = features // shards, features // 128, rows // n_chunks
    core, half = places[tables], places[tables + 1]

    for i in range(n_chunks):
        for p in range(tables):
            pltpu.make_async_copy(
                received[i].at[places[p]],
                base.at[pl.ds(i * chunk, chunk), pl.ds(p * 128, 128)],
                sems.at[0],
            ).start()

    def bring(target, first, count, sem):
        for n in range(4):
            c = core if n < 2 else 1 - core
            p = half if n % 2 == 0 else 1 - half
            for x in range(4):
                pltpu.make_async_copy(
                    gathered[n].at[x, :, pl.ds(first, count), :],
                    target.at[:, c, 2 * x + p],
                    sems.at[sem],
                ).start()

    bring(down0, 0, 32, 1)
    bring(up, 64, 64, 2)
    bring(down1, 32, 32, 3)
    for n in range(4):
        c = core if n < 2 else 1 - core
        p = half if n % 2 == 0 else 1 - half
        for x in range(4):
            for m in range(2):
                pltpu.make_async_copy(
                    gathered[n].at[x, :, pl.ds(128, 16), pl.ds(m * width, width)],
                    comp.at[:, c, m, 2 * x + p],
                    sems.at[4],
                ).start()

    def arrived(target, sem):
        pltpu.make_async_copy(target, target, sems.at[sem]).wait()

    arrived(base, 0)
    arrived(down0, 1)
    raise_by = up.reshape(shards, rank, 2 * step)
    lowered = jnp.dot(
        base[...], down0.reshape(features, rank)[...], preferred_element_type=F32
    ).astype(BF16)
    arrived(up, 2)
    for layer in range(2):
        for s in range(shards):
            here = pl.ds(s * step, step)
            raised = jnp.dot(
                lowered, raise_by[s, :, pl.ds(layer * step, step)], preferred_element_type=F32
            )
            part = base[:, here].astype(F32)
            held = part if layer == 0 else state[:, here].astype(F32)
            state[:, here] = (part * (raised + bias[layer : layer + 1, here]) + held).astype(BF16)
        if layer == 0:
            arrived(down1, 3)
            lowered = jnp.dot(
                state[...], down1.reshape(features, rank)[...], preferred_element_type=F32
            ).astype(BF16)
    arrived(comp, 4)
    squeezed = jnp.dot(state[...], comp.reshape(features, width)[...], preferred_element_type=F32)
    squeezed = (squeezed + comp_bias[...]).astype(BF16)
    out[...] = jnp.dot(squeezed, over_rows[...], preferred_element_type=F32).astype(BF16)


CHUNKS = 2
MEMBERS = [[4 * x + 2 * h + yb for x in range(4) for yb in range(2)] for h in range(2)]
ALONG_X = [[4 * x + y for x in range(4)] for y in range(4)]
ALONG_Z = [[2 * z + core for z in range(8)] for core in range(2)]
SWAP_Y = [(i, i ^ 1) for i in range(16)]
SWAP_HALF = [(i, i ^ 2) for i in range(16)]
SWAP_CORE = [(i, i ^ 1) for i in range(16)]


def at(array, index):
    return lax.dynamic_index_in_dim(array, index, 0, keepdims=False)


def after(array, *others):
    corner = array[(0,) * array.ndim]
    for other in others:
        seen = other[(0,) * other.ndim]
        corner = jnp.where(seen == seen, corner, 0)
    return array.at[(0,) * array.ndim].set(corner)


def half_plane(pieces, member):
    whole = jnp.zeros_like(pieces)
    whole = lax.dynamic_update_index_in_dim(whole, at(pieces, member), member, 0)
    for k in range(1, 8):
        moves = [(m[g], m[(g + k) % 8]) for m in MEMBERS for g in range(8)]
        piece = lax.ppermute(at(pieces, (member + k) % 8), "tower", moves)
        first = piece if k == 1 else first
        whole = lax.dynamic_update_index_in_dim(whole, piece, (member - k) % 8, 0)
    return whole, first


def on_device(
    pooled,
    cross_down,
    cross_up,
    cross_bias,
    comp_weight,
    comp_bias,
    over_weight,
    over_bias,
    table_tower,
    table_owner,
):
    me_t, me_s = lax.axis_index("tower"), lax.axis_index("shard")
    z, core, yb, half = me_s // 2, me_s % 2, me_t % 2, (me_t // 2) % 2
    my_tower = 4 * (z // 2) + 2 * half + z % 2
    member = 2 * (me_t // 4) + yb
    shards, towers = 16, 16
    _, batch, slot_most, emb = pooled.shape
    layers, rank, step = cross_up.shape[1:]
    features = step * shards
    width = comp_weight.shape[2]
    samples = batch // shards
    small = samples // towers
    outputs = over_weight.shape[1] * shards

    down_part = cross_down[0].reshape(layers, 8, step // 8, rank).transpose(1, 0, 2, 3)
    up_part = cross_up[0].transpose(1, 0, 2).reshape(8, rank // 8, layers * step)
    comp_part = comp_weight[0].reshape(2, step // 2, width).transpose(1, 0, 2)
    packed = jnp.concatenate(
        [
            down_part.reshape(8, layers * step // 8, rank),
            up_part,
            comp_part.reshape(8, step // 16, 2 * width),
        ],
        axis=1,
    )
    spread = lax.all_to_all(packed, "tower", 0, 0, tiled=True, axis_index_groups=MEMBERS)
    mine = lax.all_to_all(spread, "shard", 0, 0, tiled=True, axis_index_groups=ALONG_Z)
    tiny = jnp.concatenate(
        [
            over_weight.reshape(-1, 128),
            cross_bias.reshape(-1, 128),
            comp_bias.reshape(-1, 128),
        ]
    )
    over_tiles, bias_tiles = over_weight.size // 128, cross_bias.size // 128
    tiny = jnp.pad(tiny, ((0, -tiny.shape[0] % 16), (0, 0)))
    tiny = lax.all_gather(tiny, "tower", axis=0)
    blocks = pooled[0].reshape(8, 2, 4, 2, 2, small, slot_most, emb)
    blocks = blocks.transpose(2, 4, 1, 6, 0, 3, 5, 7)
    rows = samples // CHUNKS
    blocks = blocks.reshape(8, 2, slot_most, CHUNKS, rows, emb)
    spread_rows, received = [], []
    for i in range(CHUNKS):
        arrived, first_piece = half_plane(blocks[:, :, :, i], member)
        spread_rows.append(arrived)
        received.append(
            lax.all_to_all(
                spread_rows[i].reshape(shards, slot_most, rows, emb), "shard", 0, 0, tiled=True
            ).reshape(shards * slot_most, rows, emb)
        )

    other = lax.ppermute(after(mine, first_piece), "tower", SWAP_Y)
    gathered = [
        lax.all_gather(part, "tower", axis=0, axis_index_groups=ALONG_X)
        for part in (after(mine, spread_rows[0], tiny), after(other, spread_rows[1], received[0]))
    ]
    gathered = [after(part, received[-1]) for part in gathered]
    gathered = gathered + [lax.ppermute(part, "shard", SWAP_CORE) for part in gathered]

    own = at(tiny, my_tower)
    bias = own[over_tiles : over_tiles + bias_tiles].reshape(layers, features).astype(F32)
    squeeze_bias = own[over_tiles + bias_tiles :][: width // 128].reshape(1, width).astype(F32)
    over_all = tiny[:, :over_tiles].reshape(4, 2, 2, width, outputs // shards)
    over_all = lax.dynamic_index_in_dim(over_all, half, 1, keepdims=False)
    over_all = jnp.repeat(over_all.reshape(8, width, outputs // shards), 2, axis=0)
    over_rows = lax.all_to_all(after(over_all, received[-1]), "shard", 0, 0, tiled=True)
    over_rows = over_rows.transpose(1, 0, 2).reshape(width, outputs)

    slots = slot_order(table_tower, table_owner, my_tower, features // emb, slot_most)
    places = jnp.concatenate([slots, core[None], yb[None]]).astype(jnp.int32)

    whole = pl.BlockSpec(memory_space=pl.ANY)
    partial = pl.pallas_call(
        tower_kernel,
        grid_spec=pltpu.PrefetchScalarGridSpec(
            num_scalar_prefetch=1,
            grid=(1,),
            in_specs=[whole] * (CHUNKS + 4)
            + [
                pl.BlockSpec((layers, features), lambda i, *_: (0, 0)),
                pl.BlockSpec((1, width), lambda i, *_: (0, 0)),
                pl.BlockSpec((width, outputs), lambda i, *_: (0, 0)),
            ],
            out_specs=pl.BlockSpec((samples, outputs), lambda i, *_: (0, 0)),
            scratch_shapes=[
                pltpu.VMEM((samples, features), BF16),
                pltpu.VMEM((samples, features), BF16),
                pltpu.VMEM((8, 2, 8, step // 8, rank), BF16),
                pltpu.VMEM((8, 2, 8, step // 8, rank), BF16),
                pltpu.VMEM((8, 2, 8, rank // 8, layers * step), BF16),
                pltpu.VMEM((8, 2, 2, 8, step // 16, width), BF16),
                pltpu.SemaphoreType.DMA((5,)),
            ],
        ),
        out_shape=jax.ShapeDtypeStruct((samples, outputs), BF16),
        compiler_params=pltpu.CompilerParams(vmem_limit_bytes=48 * 2**20),
        cost_estimate=pl.CostEstimate(flops=8 * 10**9, bytes_accessed=24 * 10**6, transcendentals=0),
    )(places, *received, *gathered, bias, squeeze_bias, over_rows)

    summed = lax.all_to_all(
        partial.reshape(8, 2 * small, outputs), "shard", 0, 0, tiled=True, axis_index_groups=ALONG_Z
    )
    summed = jnp.sum(summed.astype(F32), axis=0).reshape(2, small, outputs)
    away = lax.ppermute(at(summed, 1 - half).astype(BF16), "tower", SWAP_HALF)
    total = at(summed, half) + away.astype(F32) + over_bias.astype(F32)
    return jax.nn.relu(total).astype(BF16)[None]


def solution(mesh):
    placed = (
        P("tower", None, "shard", None),
        P("tower", None, "shard", None),
        P("tower", None, None, "shard"),
        P("tower", None, None),
        P("tower", "shard", None),
        P("tower", None),
        P("tower", "shard"),
        P(),
        P(),
        P(),
    )
    return jax.shard_map(
        on_device, mesh=mesh, in_specs=placed, out_specs=P("shard", "tower", None), check_vma=False
    )
```

time: 266 us -> 350 us (1.32); the launches traced: 264 us -> 344 us
  blocking collectives: 168 us -> 89.5 us
  local copies, waits for them, and re-layouts: 7.59 us -> 66.3 us
  waiting for transfers between devices: 43 us -> 88.1 us
  starting transfers between devices: 14.6 us -> 55.9 us
  between operations: 13.6 us -> 25.2 us
    all_gather x1, blocking collectives: 168 us -> 27.7 us  [on_device(): tiny = lax.all_gather(tiny, 'tower', axis=0)]
    all_to_all x0 -> x1, blocking collectives: none -> 61.8 us  [on_device(): lax.all_to_all(spread_rows[i].reshape(shards, slot_most, rows, emb), 'sha...]
    ppermute x0 -> x18, waiting for transfers between devices: none -> 53.7 us  [the longest x14 49.5 us: half_plane(): piece = lax.ppermute(at(pieces, (member + k) % 8), 'tower', moves)]
    all_gather x1 -> x2, waiting for transfers between devices: 28 us -> 0.02 us  [on_device(): lax.all_gather(part, 'tower', axis=0, axis_index_groups=ALONG_X)]
    ppermute x0 -> x18, starting transfers between devices: none -> 24.6 us  [the longest x14 21.6 us: half_plane(): piece = lax.ppermute(at(pieces, (member + k) % 8), 'tower', moves)]
    all_to_all x2 -> x5, waiting for transfers between devices: 15 us -> 34.3 us  [the longest x1 21.3 us: on_device(): lax.all_to_all(partial.reshape(8, 2 * small, outputs), 'shard', 0, 0, til...]
    dynamic_update_slice x0 -> x16, local copies, waits for them, and re-layouts: none -> 17.7 us  [the longest x14 15 us: half_plane(): whole = lax.dynamic_update_index_in_dim(whole, piece, (member - k) % 8, 0)]
    all_to_all x2 -> x5, starting transfers between devices: 14.6 us -> 31.2 us  [the longest x1 7.67 us: on_device(): lax.all_to_all(spread, 'shard', 0, 0, tiled=True, axis_index_groups=ALONG_Z)]
  transfers between devices with their start and end apart: 3 -> 25, of which waited for: 2 -> 10; matrix products, arithmetic and copies ran while one was open for 2% -> 16% of each run, Pallas kernels for 0% -> 0%
where the time goes in v2:
time: 350 us; the launch traced here: 344 us
  blocking collectives  89.5 us (26%)
  waiting for transfers between devices  88.1 us (25%)
  local copies, waits for them, and re-layouts  66.3 us (19%)
  starting transfers between devices  55.9 us (16%)
  between operations  25.2 us (7%)
  Pallas kernels  14.8 us (4%)
  other arithmetic  3.86 us (1%)
    all_to_all x1, blocking collectives, on_device(): lax.all_to_all(spread_rows[i].reshape(shards, slot_most, rows, emb), 'sha...  61.8 us
    ppermute x14, waiting for transfers between devices, half_plane(): piece = lax.ppermute(at(pieces, (member + k) % 8), 'tower', moves)  49.5 us
    all_gather x1, blocking collectives, on_device(): tiny = lax.all_gather(tiny, 'tower', axis=0)  27.7 us
    ppermute x14, starting transfers between devices, half_plane(): piece = lax.ppermute(at(pieces, (member + k) % 8), 'tower', moves)  21.6 us
    all_to_all x1, waiting for transfers between devices, on_device(): lax.all_to_all(partial.reshape(8, 2 * small, outputs), 'shard', 0, 0, til...  21.3 us
    dynamic_update_slice x14, local copies, waits for them, and re-layouts, half_plane(): whole = lax.dynamic_update_index_in_dim(whole, piece, (member - k) % 8, 0)  15 us
    pallas_call x1, Pallas kernels, on_device(): pl.pallas_call(tower_kernel, grid_spec=pltpu.PrefetchScalarGridSpec(num_s...  14.8 us
    all_to_all x1, waiting for transfers between devices, on_device(): lax.all_to_all(after(over_all, received[-1]), 'shard', 0, 0, tiled=True)  13 us
  transfers between devices with their start and end apart: 25, of which 10 were waited for; matrix products, arithmetic and copies ran while one was open for 16% of the time, Pallas kernels for 0%

profile of v2, /device:TPU:96, one launch (start us, length us, event | category | flops | bytes accessed | tf_op | source)
XLA Modules:
  0.0 343.7 jit_solution(14313831693226033174)
XLA Ops:
  6.5 1.0 copy.42
  7.7 1.1 copy.35
  8.8 1.6 copy.36
  10.7 1.2 pad_maximum_fusion
  11.8 5.3 %all-to-all-start.2 = ((bf16[8,144,512]{2,1,0:T(8,128)(2,1)}), bf16[8,144,512]{2,1,0:T(8,128)(2,1)}, u32[]{:S(2)}, u32[]{:S(2)}) async-start(bf16[8,144,512]{2,1,0:T(8,128)(2,1)} %pad_maximum_fusion), calls=%async_computation.2 | async-start | bytes 2359296 | tf_op jit(solution)/shard_map/all_to_all | solution.py:170
  17.2 5.8 %copy.34 = bf16[4,2,2,3,8,2,24,128]{7,6,5,4,3,2,1,0:T(8,128)(2,1)} copy(bf16[4,2,2,3,8,2,24,128]{7,6,1,5,0,2,4,3:T(8,128)(2,1)} %bitcast.132) | data formatting | bytes 9437184 | tf_op jit(solution)/shard_map/transpose | solution.py:183
  23.0 4.2 %fusion.14 = (bf16[8,2,3,1,192,128]{5,4,3,2,1,0:T(8,128)(2,1)}, bf16[8,2,3,1,192,128]{5,4,3,2,1,0:T(8,128)(2,1)S(1)}) fusion(bf16[8,2,3,2,192,128]{5,4,3,2,1,0:T(8,128)(2,1)} %bitcast.129), kind=kLoop, calls=%fused_computation.61 | loop fusion | bytes 9437184 | tf_op jit(solution)/shard_map/slice | solution.py:188
  27.2 1.4 copy-done.4
  28.6 1.3 dynamic-slice_bitcast_fusion.7
  29.9 4.1 %collective-permute-start.6 = (bf16[2,3,192,128]{3,2,1,0:T(8,128)(2,1)}, bf16[2,3,192,128]{3,2,1,0:T(8,128)(2,1)}, u32[]{:S(2)}, u32[]{:S(2)}) collective-permute-start(bf16[2,3,192,128]{3,2,1,0:T(8,128)(2,1)} %get-tuple-element.88), channel_id=1, source_target_pairs={{0,208},{16,0},{64,16},{80,64},{128,80},{144,128},{192,144},{208,1... | collective-permute-start | bytes 884744 | tf_op jit(solution)/shard_map/ppermute | solution.py:128
  36.3 2.1 collective-permute-start
  38.7 7.7 %all-to-all-start.3 = ((bf16[8,144,512]{2,1,0:T(8,128)(2,1)}), bf16[8,144,512]{2,1,0:T(8,128)(2,1)S(1)}, u32[]{:S(2)}, u32[]{:S(2)}) async-start(bf16[8,144,512]{2,1,0:T(8,128)(2,1)} %all-to-all-done.2), calls=%async_computation.3 | async-start | bytes 2359296 | tf_op jit(solution)/shard_map/all_to_all | solution.py:171
  46.4 27.7 %all-gather = bf16[3328,128]{1,0:T(8,128)(2,1)} all-gather(bf16[208,128]{1,0:T(8,128)(2,1)S(1)} %fusion.10), channel_id=2, replica_groups=mesh['tower'=16,'shard'=16] {'tower'}, dimensions={0}, use_global_device_ids=true | all-gather | bytes 905216 | tf_op jit(solution)/shard_map/all_gather | solution.py:181
  74.7 1.0 bitcast_dynamic-update-slice_fusion.15
  75.8 1.2 slice.215
  78.2 1.1 collective-permute-start.2
  79.3 1.0 bitcast_dynamic-update-slice_fusion.14
  80.3 2.8 collective-permute-start.3
  84.1 4.4 %collective-permute-done.2 = bf16[2,3,192,128]{3,2,1,0:T(8,128)(2,1)S(1)} collective-permute-done((bf16[2,3,192,128]{3,2,1,0:T(8,128)(2,1)}, bf16[2,3,192,128]{3,2,1,0:T(8,128)(2,1)S(1)}, u32[]{:S(2)}, u32[]{:S(2)}) %collective-permute-start.2) | collective-permute-done | bytes 294944 | tf_op jit(solution)/shard_map/ppermute | solution.py:128
  88.5 2.5 collective-permute-done.3
  91.1 1.0 bitcast_dynamic-update-slice_fusion.10
  92.1 1.0 bitcast_dynamic-update-slice_fusion.9
  93.1 1.0 bitcast_dynamic-update-slice_fusion.8
  97.2 1.0 copy.61
  98.3 1.1 copy-done.2
  99.4 7.3 %all-to-all-start = ((bf16[16,3,192,128]{3,2,1,0:T(8,128)(2,1)}), bf16[16,3,192,128]{3,2,1,0:T(8,128)(2,1)S(1)}, u32[]{:S(2)}, u32[]{:S(2)}) async-start(bf16[16,3,192,128]{3,2,1,0:T(8,128)(2,1)} %bitcast.131), calls=%async_computation | async-start | bytes 4718592 | tf_op jit(solution)/shard_map/all_to_all | solution.py:191
  106.8 2.7 dynamic-slice_bitcast_fusion
  109.4 2.7 collective-permute-start.7
  112.1 1.4 collective-permute-start.13
  113.8 2.5 collective-permute-start.11
  116.3 1.9 broadcast.125.clone.1
  118.3 1.7 bitcast_dynamic-update-slice_fusion.7
  119.9 11.2 %collective-permute-done.7 = bf16[2,3,192,128]{3,2,1,0:T(8,128)(2,1)S(1)} collective-permute-done((bf16[2,3,192,128]{3,2,1,0:T(8,128)(2,1)S(1)}, bf16[2,3,192,128]{3,2,1,0:T(8,128)(2,1)S(1)}, u32[]{:S(2)}, u32[]{:S(2)}) %collective-permute-start.7) | collective-permute-done | bytes 294944 | tf_op jit(solution)/shard_map/ppermute | solution.py:128
  131.8 11.0 %collective-permute-done.8 = bf16[2,3,192,128]{3,2,1,0:T(8,128)(2,1)S(1)} collective-permute-done((bf16[2,3,192,128]{3,2,1,0:T(8,128)(2,1)S(1)}, bf16[2,3,192,128]{3,2,1,0:T(8,128)(2,1)S(1)}, u32[]{:S(2)}, u32[]{:S(2)}) %collective-permute-start.8) | collective-permute-done | bytes 294944 | tf_op jit(solution)/shard_map/ppermute | solution.py:128
  142.8 2.3 collective-permute-start.10
  148.4 7.2 %collective-permute-done.9 = bf16[2,3,192,128]{3,2,1,0:T(8,128)(2,1)} collective-permute-done((bf16[2,3,192,128]{3,2,1,0:T(8,128)(2,1)}, bf16[2,3,192,128]{3,2,1,0:T(8,128)(2,1)}, u32[]{:S(2)}, u32[]{:S(2)}) %collective-permute-start.9) | collective-permute-done | bytes 294944 | tf_op jit(solution)/shard_map/ppermute | solution.py:128
  155.6 1.7 bitcast_dynamic-update-slice_fusion.4
  157.2 13.2 %collective-permute-done.10 = bf16[2,3,192,128]{3,2,1,0:T(8,128)(2,1)} collective-permute-done((bf16[2,3,192,128]{3,2,1,0:T(8,128)(2,1)}, bf16[2,3,192,128]{3,2,1,0:T(8,128)(2,1)}, u32[]{:S(2)}, u32[]{:S(2)}) %collective-permute-start.10) | collective-permute-done | bytes 294944 | tf_op jit(solution)/shard_map/ppermute | solution.py:128
  170.5 1.7 bitcast_dynamic-update-slice_fusion.3
  172.2 1.7 bitcast_dynamic-update-slice_fusion.2
  173.9 1.7 bitcast_dynamic-update-slice_fusion.1
  175.6 1.7 bitcast_dynamic-update-slice_fusion
  177.3 1.2 slice.222
  179.9 1.1 collective-permute-done.14
  180.9 1.0 copy-done.7
  184.9 1.3 scatter.25
  186.2 61.8 %all_to_all.30 = bf16[16,3,192,128]{3,2,1,0:T(8,128)(2,1)S(1)} all-to-all(bf16[16,3,192,128]{3,2,1,0:T(8,128)(2,1)} %bitcast.37), channel_id=1, replica_groups=mesh['tower'=16,'shard'=16] {'shard'}, dimensions={0} | all-to-all | bytes 4718592 | tf_op jit(solution)/shard_map/all_to_all | solution.py:191
  248.6 1.4 copy-done
  251.3 1.2 slice.219
  253.1 1.3 scatter.21.refs_2_
  254.5 1.2 slice.224
  256.3 1.3 scatter.26.refs_3_
  258.8 1.7 reshape.321
  261.3 1.2 copy.39
  263.4 1.2 slice.226
  265.2 1.2 scatter.29
  266.5 5.7 %all-to-all-start.4 = ((bf16[16,256,64]{1,2,0:T(8,128)(2,1)}), bf16[16,256,64]{1,2,0:T(8,128)(2,1)S(1)}, u32[]{:S(2)}, u32[]{:S(2)}) async-start(bf16[16,256,64]{1,2,0:T(8,128)(2,1)} %scatter.29), calls=%async_computation.4 | async-start | bytes 1048576 | tf_op jit(solution)/shard_map/all_to_all | solution.py:210
  274.2 13.0 %all-to-all-done.4 = bf16[16,256,64]{1,2,0:T(8,128)(2,1)S(1)} async-done(((bf16[16,256,64]{1,2,0:T(8,128)(2,1)}), bf16[16,256,64]{1,2,0:T(8,128)(2,1)S(1)}, u32[]{:S(2)}, u32[]{:S(2)}) %all-to-all-start.4) | async-done | bytes 524320 | tf_op jit(solution)/shard_map/all_to_all | solution.py:210
  287.4 1.7 copy-done.1
  289.1 14.8 %shard_map.100 = bf16[384,1024]{1,0:T(8,128)(2,1)} custom-call(s32[34]{0:T(128)S(1)} %pad_add_fusion.places, bf16[48,192,128]{2,1,0:T(8,128)(2,1)S(1)} %bitcast.125, bf16[48,192,128]{2,1,0:T(8,128)(2,1)S(1)} %bitcast.127, bf16[4,8,144,512]{3,2,1,0:T(8,128)(2,1)} %scatter.21.refs_2_, bf16[4,8,144,512]{3,2,1,0:T(8,128)(2,1)} %scatter.26.refs_3_, ...), custom_call_target="tpu_custom_call" | custom-call | flops 8000000000 | bytes 24000000 | tf_op jit(solution)/shard_map/pallas_call | solution.py:217
  303.9 5.2 %all-to-all-start.5 = ((bf16[8,48,1024]{2,1,0:T(8,128)(2,1)}), bf16[8,48,1024]{2,1,0:T(8,128)(2,1)S(1)}, u32[]{:S(2)}, u32[]{:S(2)}) async-start(bf16[8,48,1024]{2,1,0:T(8,128)(2,1)} %bitcast.71), calls=%async_computation.5 | async-start | bytes 1572864 | tf_op jit(solution)/shard_map/all_to_all | solution.py:244
  309.1 21.3 %all-to-all-done.5 = bf16[8,48,1024]{2,1,0:T(8,128)(2,1)S(1)} async-done(((bf16[8,48,1024]{2,1,0:T(8,128)(2,1)}), bf16[8,48,1024]{2,1,0:T(8,128)(2,1)S(1)}, u32[]{:S(2)}, u32[]{:S(2)}) %all-to-all-start.5) | async-done | bytes 786464 | tf_op jit(solution)/shard_map/all_to_all | solution.py:244
  330.6 2.5 collective-permute-start.17
  333.1 3.2 collective-permute-done.17
  (88 shorter events, 15.8 us)
Async XLA Ops:
  11.8 26.9 %all-to-all-start.2 = ((bf16[8,144,512]{2,1,0:T(8,128)(2,1)}), bf16[8,144,512]{2,1,0:T(8,128)(2,1)}, u32[]{:S(2)}, u32[]{:S(2)}) async-start(bf16[8,144,512]{2,1,0:T(8,128)(2,1)} %pad_maximum_fusion), calls=%async_computation.2 | async-start | bytes 2359296 | tf_op jit(solution)/shard_map/all_to_all | solution.py:170
  27.2 1.4 copy-start.4
  27.2 11.2 %copy-start.10 = (bf16[1,2,4096]{2,1,0:T(2,128)(2,1)S(1)}, bf16[1,2,4096]{2,1,0:T(2,128)(2,1)}, u32[]{:S(2)}) copy-start(bf16[1,2,4096]{2,1,0:T(2,128)(2,1)} %param.25) | copy-start | bytes 49156
  27.2 11.2 %copy-start.8 = (bf16[256,64]{0,1:T(8,128)(2,1)S(1)}, bf16[256,64]{0,1:T(8,128)(2,1)}, u32[]{:S(2)}) copy-start(bf16[256,64]{0,1:T(8,128)(2,1)} %param.28) | copy-start | bytes 98308
  27.2 11.5 %copy-start.13 = (bf16[1,256]{1,0:T(2,128)(2,1)S(1)}, bf16[1,256]{1,0:T(2,128)(2,1)}, u32[]{:S(2)}) copy-start(bf16[1,256]{1,0:T(2,128)(2,1)} %param.27) | copy-start | bytes 1540
  29.9 63.2 %collective-permute-start.6 = (bf16[2,3,192,128]{3,2,1,0:T(8,128)(2,1)}, bf16[2,3,192,128]{3,2,1,0:T(8,128)(2,1)}, u32[]{:S(2)}, u32[]{:S(2)}) collective-permute-start(bf16[2,3,192,128]{3,2,1,0:T(8,128)(2,1)} %get-tuple-element.88), channel_id=1, source_target_pairs={{0,208},{16,0},{64,16},{80,64},{128,80},{144,128},{192,144},{208,1... | collective-permute-start | bytes 884744 | tf_op jit(solution)/shard_map/ppermute | solution.py:128
  34.1 58.0 %collective-permute-start.5 = (bf16[2,3,192,128]{3,2,1,0:T(8,128)(2,1)}, bf16[2,3,192,128]{3,2,1,0:T(8,128)(2,1)}, u32[]{:S(2)}, u32[]{:S(2)}) collective-permute-start(bf16[2,3,192,128]{3,2,1,0:T(8,128)(2,1)} %get-tuple-element.89), channel_id=1, source_target_pairs={{0,192},{16,208},{64,0},{80,16},{128,64},{144,80},{192,128},{208,1... | collective-permute-start | bytes 884744 | tf_op jit(solution)/shard_map/ppermute | solution.py:128
  34.9 56.2 %collective-permute-start.4 = (bf16[2,3,192,128]{3,2,1,0:T(8,128)(2,1)}, bf16[2,3,192,128]{3,2,1,0:T(8,128)(2,1)}, u32[]{:S(2)}, u32[]{:S(2)}) collective-permute-start(bf16[2,3,192,128]{3,2,1,0:T(8,128)(2,1)} %get-tuple-element.90), channel_id=1, source_target_pairs={{0,144},{16,192},{64,208},{80,0},{128,16},{144,64},{192,80},{208,1... | collective-permute-start | bytes 884744 | tf_op jit(solution)/shard_map/ppermute | solution.py:128
  35.5 44.8 %collective-permute-start.1 = (bf16[2,3,192,128]{3,2,1,0:T(8,128)(2,1)}, bf16[2,3,192,128]{3,2,1,0:T(8,128)(2,1)}, u32[]{:S(2)}, u32[]{:S(2)}) collective-permute-start(bf16[2,3,192,128]{3,2,1,0:T(8,128)(2,1)} %get-tuple-element.93), channel_id=1, source_target_pairs={{0,64},{16,80},{64,128},{80,144},{128,192},{144,208},{192,0},{208,... | collective-permute-start | bytes 884744 | tf_op jit(solution)/shard_map/ppermute | solution.py:128
  36.3 41.8 %collective-permute-start = (bf16[2,3,192,128]{3,2,1,0:T(8,128)(2,1)}, bf16[2,3,192,128]{3,2,1,0:T(8,128)(2,1)}, u32[]{:S(2)}, u32[]{:S(2)}) collective-permute-start(bf16[2,3,192,128]{3,2,1,0:T(8,128)(2,1)} %get-tuple-element.94), channel_id=1, source_target_pairs={{0,16},{16,64},{64,80},{80,128},{128,144},{144,192},{192,208},{208... | collective-permute-start | bytes 884744 | tf_op jit(solution)/shard_map/ppermute | solution.py:128
  38.7 57.3 %all-to-all-start.3 = ((bf16[8,144,512]{2,1,0:T(8,128)(2,1)}), bf16[8,144,512]{2,1,0:T(8,128)(2,1)S(1)}, u32[]{:S(2)}, u32[]{:S(2)}) async-start(bf16[8,144,512]{2,1,0:T(8,128)(2,1)} %all-to-all-done.2), calls=%async_computation.3 | async-start | bytes 2359296 | tf_op jit(solution)/shard_map/all_to_all | solution.py:171
  78.2 10.3 %collective-permute-start.2 = (bf16[2,3,192,128]{3,2,1,0:T(8,128)(2,1)}, bf16[2,3,192,128]{3,2,1,0:T(8,128)(2,1)S(1)}, u32[]{:S(2)}, u32[]{:S(2)}) collective-permute-start(bf16[2,3,192,128]{3,2,1,0:T(8,128)(2,1)} %get-tuple-element.92), channel_id=1, source_target_pairs={{0,80},{16,128},{64,144},{80,192},{128,208},{144,0},{192,16},{208,... | collective-permute-start | bytes 884744 | tf_op jit(solution)/shard_map/ppermute | solution.py:128
  80.3 10.7 %collective-permute-start.3 = (bf16[2,3,192,128]{3,2,1,0:T(8,128)(2,1)}, bf16[2,3,192,128]{3,2,1,0:T(8,128)(2,1)S(1)}, u32[]{:S(2)}, u32[]{:S(2)}) collective-permute-start(bf16[2,3,192,128]{3,2,1,0:T(8,128)(2,1)} %get-tuple-element.91), channel_id=1, source_target_pairs={{0,128},{16,144},{64,192},{80,208},{128,0},{144,16},{192,64},{208,... | collective-permute-start | bytes 884744 | tf_op jit(solution)/shard_map/ppermute | solution.py:128
  94.1 5.2 %copy-start.3 = (bf16[8,2,3,192,128]{4,3,2,1,0:T(8,128)(2,1)}, bf16[8,2,3,192,128]{4,3,2,1,0:T(8,128)(2,1)S(1)}, u32[]{:S(2)}) copy-start(bf16[8,2,3,192,128]{4,3,2,1,0:T(8,128)(2,1)S(1)} %bitcast_dynamic-update-slice_fusion.8) | copy-start | bytes 7077892
  98.2 153.1 %all-gather.4.cloned.1.call-start = ((), (), s32[]{:S(2)}) async-start(), calls=%async_computation.6 | async-start | bytes 5898240 | tf_op jit(solution)/shard_map/all_gather | solution.py:198
  98.2 1.1 copy-start.2
  99.4 83.9 %all-to-all-start = ((bf16[16,3,192,128]{3,2,1,0:T(8,128)(2,1)}), bf16[16,3,192,128]{3,2,1,0:T(8,128)(2,1)S(1)}, u32[]{:S(2)}, u32[]{:S(2)}) async-start(bf16[16,3,192,128]{3,2,1,0:T(8,128)(2,1)} %bitcast.131), calls=%async_computation | async-start | bytes 4718592 | tf_op jit(solution)/shard_map/all_to_all | solution.py:191
  106.7 147.8 %all-gather.6.cloned.1.call-start = ((), (), s32[]{:S(2)}) async-start(), calls=%async_computation.7 | async-start | bytes 5898240 | tf_op jit(solution)/shard_map/all_gather | solution.py:198
  109.4 38.9 %copy-start.6 = (bf16[8,144,512]{2,1,0:T(8,128)(2,1)S(1)}, bf16[8,144,512]{2,1,0:T(8,128)(2,1)}, u32[]{:S(2)}) copy-start(bf16[8,144,512]{2,1,0:T(8,128)(2,1)} %copy.61) | copy-start | bytes 3538948
  109.4 21.7 %collective-permute-start.7 = (bf16[2,3,192,128]{3,2,1,0:T(8,128)(2,1)S(1)}, bf16[2,3,192,128]{3,2,1,0:T(8,128)(2,1)S(1)}, u32[]{:S(2)}, u32[]{:S(2)}) collective-permute-start(bf16[2,3,192,128]{3,2,1,0:T(8,128)(2,1)S(1)} %get-tuple-element.87), channel_id=1, source_target_pairs={{0,16},{16,64},{64,80},{80,128},{128,144},{144,192},{192,208},{208... | collective-permute-start | bytes 884744 | tf_op jit(solution)/shard_map/ppermute | solution.py:128
  112.1 63.5 %collective-permute-start.13 = (bf16[2,3,192,128]{3,2,1,0:T(8,128)(2,1)}, bf16[2,3,192,128]{3,2,1,0:T(8,128)(2,1)}, u32[]{:S(2)}, u32[]{:S(2)}) collective-permute-start(bf16[2,3,192,128]{3,2,1,0:T(8,128)(2,1)} %get-tuple-element.81), channel_id=1, source_target_pairs={{0,208},{16,0},{64,16},{80,64},{128,80},{144,128},{192,144},{208,1... | collective-permute-start | bytes 884744 | tf_op jit(solution)/shard_map/ppermute | solution.py:128
  113.6 60.3 %collective-permute-start.12 = (bf16[2,3,192,128]{3,2,1,0:T(8,128)(2,1)}, bf16[2,3,192,128]{3,2,1,0:T(8,128)(2,1)}, u32[]{:S(2)}, u32[]{:S(2)}) collective-permute-start(bf16[2,3,192,128]{3,2,1,0:T(8,128)(2,1)} %get-tuple-element.82), channel_id=1, source_target_pairs={{0,192},{16,208},{64,0},{80,16},{128,64},{144,80},{192,128},{208,1... | collective-permute-start | bytes 884744 | tf_op jit(solution)/shard_map/ppermute | solution.py:128
  113.8 58.4 %collective-permute-start.11 = (bf16[2,3,192,128]{3,2,1,0:T(8,128)(2,1)}, bf16[2,3,192,128]{3,2,1,0:T(8,128)(2,1)}, u32[]{:S(2)}, u32[]{:S(2)}) collective-permute-start(bf16[2,3,192,128]{3,2,1,0:T(8,128)(2,1)} %get-tuple-element.83), channel_id=1, source_target_pairs={{0,144},{16,192},{64,208},{80,0},{128,16},{144,64},{192,80},{208,1... | collective-permute-start | bytes 884744 | tf_op jit(solution)/shard_map/ppermute | solution.py:128
  116.3 26.5 %collective-permute-start.8 = (bf16[2,3,192,128]{3,2,1,0:T(8,128)(2,1)S(1)}, bf16[2,3,192,128]{3,2,1,0:T(8,128)(2,1)S(1)}, u32[]{:S(2)}, u32[]{:S(2)}) collective-permute-start(bf16[2,3,192,128]{3,2,1,0:T(8,128)(2,1)S(1)} %get-tuple-element.86), channel_id=1, source_target_pairs={{0,64},{16,80},{64,128},{80,144},{128,192},{144,208},{192,0},{208,... | collective-permute-start | bytes 884744 | tf_op jit(solution)/shard_map/ppermute | solution.py:128
  131.1 24.4 %collective-permute-start.9 = (bf16[2,3,192,128]{3,2,1,0:T(8,128)(2,1)}, bf16[2,3,192,128]{3,2,1,0:T(8,128)(2,1)}, u32[]{:S(2)}, u32[]{:S(2)}) collective-permute-start(bf16[2,3,192,128]{3,2,1,0:T(8,128)(2,1)} %get-tuple-element.85), channel_id=1, source_target_pairs={{0,80},{16,128},{64,144},{80,192},{128,208},{144,0},{192,16},{208,... | collective-permute-start | bytes 884744 | tf_op jit(solution)/shard_map/ppermute | solution.py:128
  142.8 27.7 %collective-permute-start.10 = (bf16[2,3,192,128]{3,2,1,0:T(8,128)(2,1)}, bf16[2,3,192,128]{3,2,1,0:T(8,128)(2,1)}, u32[]{:S(2)}, u32[]{:S(2)}) collective-permute-start(bf16[2,3,192,128]{3,2,1,0:T(8,128)(2,1)} %get-tuple-element.84), channel_id=1, source_target_pairs={{0,128},{16,144},{64,192},{80,208},{128,0},{144,16},{192,64},{208,... | collective-permute-start | bytes 884744 | tf_op jit(solution)/shard_map/ppermute | solution.py:128
  155.6 25.4 %collective-permute-start.14 = (bf16[8,144,512]{2,1,0:T(8,128)(2,1)S(1)}, bf16[8,144,512]{2,1,0:T(8,128)(2,1)S(1)}, u32[]{:S(2)}, u32[]{:S(2)}) collective-permute-start(bf16[8,144,512]{2,1,0:T(8,128)(2,1)S(1)} %scatter.24), channel_id=1, source_target_pairs={{0,16},{16,0},{32,48},{48,32},{64,80},{80,64},{96,112},{112,96},{1... | collective-permute-start | bytes 3538952 | tf_op jit(solution)/shard_map/ppermute | solution.py:196
  180.9 1.0 copy-start.7
  186.2 71.7 %copy-start.5 = (bf16[3328,128]{1,0:T(8,128)(2,1)S(1)}, bf16[3328,128]{1,0:T(8,128)(2,1)}, u32[]{:S(2)}) copy-start(bf16[3328,128]{1,0:T(8,128)(2,1)} %all-gather) | copy-start | bytes 2555908
  248.6 1.4 copy-start
  254.4 33.0 %collective-permute-start.15 = (bf16[4,8,144,512]{3,2,1,0:T(8,128)(2,1)}, bf16[4,8,144,512]{3,2,1,0:T(8,128)(2,1)}, u32[]{:S(2)}, u32[]{:S(2)}) collective-permute-start(bf16[4,8,144,512]{3,2,1,0:T(8,128)(2,1)} %scatter.21.refs_2_), channel_id=1, source_target_pairs={{0,1},{1,0},{2,3},{3,2},{4,5},{5,4},{6,7},{7,6},{8,9},{9,8},{10,11... | collective-permute-start | bytes 14155784 | tf_op jit(solution)/shard_map/ppermute | solution.py:202
  257.5 29.9 %collective-permute-start.16 = (bf16[4,8,144,512]{3,2,1,0:T(8,128)(2,1)}, bf16[4,8,144,512]{3,2,1,0:T(8,128)(2,1)}, u32[]{:S(2)}, u32[]{:S(2)}) collective-permute-start(bf16[4,8,144,512]{3,2,1,0:T(8,128)(2,1)} %scatter.26.refs_3_), channel_id=1, source_target_pairs={{0,1},{1,0},{2,3},{3,2},{4,5},{5,4},{6,7},{7,6},{8,9},{9,8},{10,11... | collective-permute-start | bytes 14155784 | tf_op jit(solution)/shard_map/ppermute | solution.py:202
  258.8 14.2 %copy-start.12 = (s32[512]{0:T(512)S(1)}, s32[512]{0:T(512)}, u32[]{:S(2)}) copy-start(s32[512]{0:T(512)} %param.30) | copy-start | bytes 6148
  258.8 14.2 %copy-start.9 = (s32[512]{0:T(512)S(1)}, s32[512]{0:T(512)}, u32[]{:S(2)}) copy-start(s32[512]{0:T(512)} %param.31) | copy-start | bytes 6148
  266.5 20.7 %all-to-all-start.4 = ((bf16[16,256,64]{1,2,0:T(8,128)(2,1)}), bf16[16,256,64]{1,2,0:T(8,128)(2,1)S(1)}, u32[]{:S(2)}, u32[]{:S(2)}) async-start(bf16[16,256,64]{1,2,0:T(8,128)(2,1)} %scatter.29), calls=%async_computation.4 | async-start | bytes 1048576 | tf_op jit(solution)/shard_map/all_to_all | solution.py:210
  287.4 1.7 copy-start.1
  303.9 29.2 %copy-start.11 = (bf16[1024]{0:T(1024)(128)(2,1)S(1)}, bf16[1024]{0:T(1024)(128)(2,1)}, u32[]{:S(2)}) copy-start(bf16[1024]{0:T(1024)(128)(2,1)} %param.29) | copy-start | bytes 6148
  303.9 26.5 %all-to-all-start.5 = ((bf16[8,48,1024]{2,1,0:T(8,128)(2,1)}), bf16[8,48,1024]{2,1,0:T(8,128)(2,1)S(1)}, u32[]{:S(2)}, u32[]{:S(2)}) async-start(bf16[8,48,1024]{2,1,0:T(8,128)(2,1)} %bitcast.71), calls=%async_computation.5 | async-start | bytes 1572864 | tf_op jit(solution)/shard_map/all_to_all | solution.py:244
  330.6 5.7 %collective-permute-start.17 = (bf16[24,1024]{1,0:T(8,128)(2,1)S(1)}, bf16[24,1024]{1,0:T(8,128)(2,1)S(1)}, u32[]{:S(2)}, u32[]{:S(2)}) collective-permute-start(bf16[24,1024]{1,0:T(8,128)(2,1)S(1)} %fusion.11), channel_id=1, source_target_pairs={{0,32},{16,48},{32,0},{48,16},{64,96},{80,112},{96,64},{112,80},{1... | collective-permute-start | bytes 147464 | tf_op jit(solution)/shard_map/ppermute | solution.py:248
Sparse Core Ops, SparseCore 0:
  100.8 81.1 all-gather.3
  186.3 55.9 all-gather.5

commit v3 on v1

--- a/solution.py
+++ b/solution.py
@@ -78,6 +78,55 @@
     out[...] = jnp.dot(squeezed, over_rows[...], preferred_element_type=F32).astype(BF16)
 
 
+def tower_product(slots, received, gathered, bias, squeeze_bias, over_rows):
+    rows = received.shape[1]
+    layers, features = bias.shape
+    width, outputs = over_rows.shape
+    shards, rank = gathered.shape[0], gathered.shape[3]
+    step = features // shards
+    return pl.pallas_call(
+        tower_kernel,
+        grid_spec=pltpu.PrefetchScalarGridSpec(
+            num_scalar_prefetch=1,
+            grid=(1,),
+            in_specs=[
+                pl.BlockSpec(memory_space=pl.ANY),
+                pl.BlockSpec(memory_space=pl.ANY),
+                pl.BlockSpec((layers, features), lambda i, *_: (0, 0)),
+                pl.BlockSpec((1, width), lambda i, *_: (0, 0)),
+                pl.BlockSpec((width, outputs), lambda i, *_: (0, 0)),
+            ],
+            out_specs=pl.BlockSpec((rows, outputs), lambda i, *_: (0, 0)),
+            scratch_shapes=[
+                pltpu.VMEM((rows, features), BF16),
+                pltpu.VMEM((rows, features), BF16),
+                pltpu.VMEM((shards, 8, step // 8, rank), BF16),
+                pltpu.VMEM((shards, 8, step // 8, rank), BF16),
+                pltpu.VMEM((shards, 8, rank // 8, layers * step), BF16),
+                pltpu.VMEM((shards, 2, 8, step // 16, width), BF16),
+                pltpu.SemaphoreType.DMA((6,)),
+            ],
+        ),
+        out_shape=jax.ShapeDtypeStruct((rows, outputs), BF16),
+        compiler_params=pltpu.CompilerParams(vmem_limit_bytes=48 * 2**20),
+        cost_estimate=pl.CostEstimate(
+            flops=rows * 2 * 10**7, bytes_accessed=24 * 10**6, transcendentals=0
+        ),
+    )(slots, received, gathered, bias, squeeze_bias, over_rows)
+
+
+def at(array, index):
+    return lax.dynamic_index_in_dim(array, index, 0, keepdims=False)
+
+
+def after(array, *others):
+    corner = array[(0,) * array.ndim]
+    for other in others:
+        seen = other[(0,) * other.ndim]
+        corner = jnp.where(seen == seen, corner, 0)
+    return array.at[(0,) * array.ndim].set(corner)
+
+
 def on_device(
     pooled,
     cross_down,
@@ -111,51 +160,38 @@
         axis=1,
     )
     gathered = lax.all_gather(packed, "shard", axis=0)
-    by_slot = pooled[0].transpose(1, 0, 2).reshape(slot_most, shards, samples, emb)
-    received = lax.all_to_all(
-        by_slot.transpose(1, 0, 2, 3), "shard", split_axis=0, concat_axis=0, tiled=True
-    ).reshape(shards * slot_most, samples, emb)
     over_rows = lax.all_gather(over_weight, "shard", axis=1, tiled=True)
+    small = samples // towers
+    blocks = pooled[0].reshape(shards, towers, small, slot_most, emb).transpose(0, 3, 1, 2, 4)
+    received = []
+    for first, count in ((0, 16), (16, small - 16)):
+        block = blocks[:, :, :, first : first + count].reshape(
+            shards, slot_most, towers * count, emb
+        )
+        block = after(block, gathered if received else over_rows)
+        received.append(
+            lax.all_to_all(block, "shard", 0, 0, tiled=True).reshape(
+                shards * slot_most, towers * count, emb
+            )
+        )
     slots = slot_order(table_tower, table_owner, tower_id, features // emb, slot_most)
 
-    partial = pl.pallas_call(
-        tower_kernel,
-        grid_spec=pltpu.PrefetchScalarGridSpec(
-            num_scalar_prefetch=1,
-            grid=(1,),
-            in_specs=[
-                pl.BlockSpec(memory_space=pl.ANY),
-                pl.BlockSpec(memory_space=pl.ANY),
-                pl.BlockSpec((layers, features), lambda i, *_: (0, 0)),
-                pl.BlockSpec((1, width), lambda i, *_: (0, 0)),
-                pl.BlockSpec((width, outputs), lambda i, *_: (0, 0)),
-            ],
-            out_specs=pl.BlockSpec((samples, outputs), lambda i, *_: (0, 0)),
-            scratch_shapes=[
-                pltpu.VMEM((samples, features), BF16),
-                pltpu.VMEM((samples, features), BF16),
-                pltpu.VMEM((shards, 8, step // 8, rank), BF16),
-                pltpu.VMEM((shards, 8, step // 8, rank), BF16),
-                pltpu.VMEM((shards, 8, rank // 8, layers * step), BF16),
-                pltpu.VMEM((shards, 2, 8, step // 16, width), BF16),
-                pltpu.SemaphoreType.DMA((6,)),
-            ],
-        ),
-        out_shape=jax.ShapeDtypeStruct((samples, outputs), BF16),
-        compiler_params=pltpu.CompilerParams(vmem_limit_bytes=48 * 2**20),
-        cost_estimate=pl.CostEstimate(flops=8 * 10**9, bytes_accessed=24 * 10**6, transcendentals=0),
-    )(
-        slots,
-        received,
-        gathered,
-        cross_bias[0].astype(F32),
-        comp_bias.astype(F32),
-        over_rows,
-    )
-    summed = lax.all_to_all(
-        partial.reshape(towers, samples // towers, outputs), "tower", 0, 0, tiled=True
-    )
-    total = jnp.sum(summed.astype(F32), axis=0) + over_bias.astype(F32)
+    bias, squeeze_bias = cross_bias[0].astype(F32), comp_bias.astype(F32)
+    totals = []
+    for part in received:
+        partial = tower_product(slots, part, gathered, bias, squeeze_bias, over_rows)
+        pieces = partial.reshape(towers, part.shape[1] // towers, outputs)
+        if totals:
+            summed = lax.all_to_all(pieces, "tower", 0, 0, tiled=True).astype(F32)
+            totals.append(jnp.sum(summed, axis=0))
+        else:
+            total = at(pieces, tower_id).astype(F32)
+            for k in range(1, 16):
+                moves = [(i, (i + k) % 16) for i in range(16)]
+                piece = lax.ppermute(at(pieces, (tower_id + k) % 16), "tower", moves)
+                total = total + piece.astype(F32)
+            totals.append(total)
+    total = jnp.concatenate(totals) + over_bias.astype(F32)
     return jax.nn.relu(total).astype(BF16)[None]
 
 

time: 266 us -> 276 us (1.038)
  blocking collectives: 168 us -> 19.6 us
  waiting for transfers between devices: 43 us -> 142 us
  starting transfers between devices: 14.6 us -> 48.2 us
  local copies, waits for them, and re-layouts: 7.59 us -> 23.1 us
  Pallas kernels: 15 us -> 21.2 us
  between operations: 13.6 us -> 17.5 us
    all_gather x1, blocking collectives: 168 us -> 19.6 us  [on_device(): over_rows = lax.all_gather(over_weight, 'shard', axis=1, tiled=True)]
    all_gather x1, waiting for transfers between devices: 28 us -> 134 us  [on_device(): gathered = lax.all_gather(packed, 'shard', axis=0)]
    ppermute x0 -> x15, starting transfers between devices: none -> 28.5 us  [on_device(): piece = lax.ppermute(at(pieces, (tower_id + k) % 16), 'tower', moves)]
    all_to_all x2 -> x3, waiting for transfers between devices: 15 us -> 7.56 us  [the longest x1 7.55 us: on_device(): summed = lax.all_to_all(pieces, 'tower', 0, 0, tiled=True).astype(F32)]
    pallas_call x1 -> x2, Pallas kernels: 15 us -> 21.2 us  [tower_product(): pl.pallas_call(tower_kernel, grid_spec=pltpu.PrefetchScalarGridSpec(num_s...]
    slice x0 -> x5, local copies, waits for them, and re-layouts: none -> 6.17 us  [the longest x1 2.75 us: on_device(): blocks[:, :, :, first:first + count]]
    all_to_all x2 -> x3, starting transfers between devices: 14.6 us -> 19.6 us  [the longest x2 12.9 us: on_device(): lax.all_to_all(block, 'shard', 0, 0, tiled=True)]
    unnamed x16 -> x26, local copies, waits for them, and re-layouts: 0.03 us -> 4.46 us
  transfers between devices with their start and end apart: 3 -> 19, of which waited for: 2 -> 2; matrix products, arithmetic and copies ran while one was open for 2% -> 6% of each run, Pallas kernels for 0% -> 8%
where the time goes in v3:
time: 276 us; the launch traced here: 274 us
  waiting for transfers between devices  142 us (51%)
  starting transfers between devices  48.2 us (17%)
  local copies, waits for them, and re-layouts  23.1 us (8%)
  Pallas kernels  21.2 us (8%)
  blocking collectives  19.6 us (7%)
  between operations  17.5 us (6%)
  other arithmetic  3.11 us (1%)
    all_gather x1, waiting for transfers between devices, on_device(): gathered = lax.all_gather(packed, 'shard', axis=0)  134 us
    ppermute x15, starting transfers between devices, on_device(): piece = lax.ppermute(at(pieces, (tower_id + k) % 16), 'tower', moves)  28.5 us
    pallas_call x2, Pallas kernels, tower_product(): pl.pallas_call(tower_kernel, grid_spec=pltpu.PrefetchScalarGridSpec(num_s...  21.2 us
    all_gather x1, blocking collectives, on_device(): over_rows = lax.all_gather(over_weight, 'shard', axis=1, tiled=True)  19.6 us
    all_to_all x2, starting transfers between devices, on_device(): lax.all_to_all(block, 'shard', 0, 0, tiled=True)  12.9 us
    all_to_all x1, waiting for transfers between devices, on_device(): summed = lax.all_to_all(pieces, 'tower', 0, 0, tiled=True).astype(F32)  7.55 us
    all_to_all x1, starting transfers between devices, on_device(): summed = lax.all_to_all(pieces, 'tower', 0, 0, tiled=True).astype(F32)  6.74 us
  transfers between devices with their start and end apart: 19, of which 2 were waited for; matrix products, arithmetic and copies ran while one was open for 6% of the time, Pallas kernels for 8%

profile of v3, /device:TPU:96, one launch (start us, length us, event | category | flops | bytes accessed | tf_op | source)
XLA Modules:
  0.0 274.3 jit_solution(18207855518419407998)
XLA Ops:
  6.5 1.1 copy.35
  7.6 0.1 reshape.172
  7.7 1.6 copy.28
  9.3 0.3 reshape.171
  9.7 1.1 pad_maximum_fusion
  10.9 0.0 all-gather.3.cloned.1.call-update
  10.9 3.2 %copy.34 = bf16[16,16,24,3,128]{4,2,1,3,0:T(8,128)(2,1)S(1)} copy(bf16[16,16,24,3,128]{4,2,1,0,3:T(8,128)(2,1)} %bitcast.73) | data formatting | bytes 9437184 | tf_op jit(solution)/shard_map/reshape;squeeze | solution.py:165
  14.0 0.0 copy-start.7
  14.1 2.7 %slice.78 = bf16[16,3,16,16,128]{4,3,2,1,0:T(8,128)(2,1)} slice(bf16[16,3,16,24,128]{4,3,2,1,0:T(8,128)(2,1)S(1)} %bitcast.71), slice={[0:16], [0:3], [0:16], [0:16], [0:128]} | slice | bytes 6291456 | tf_op jit(solution)/shard_map/slice | solution.py:168
  16.8 0.4 copy-done.3
  17.2 19.6 %all_gather.9 = bf16[256,1024]{0,1:T(8,128)(2,1)S(1)} all-gather(bf16[256,64]{0,1:T(8,128)(2,1)S(1)} %copy-done.7), channel_id=1, replica_groups=mesh['tower'=16,'shard'=16] {'shard'}, dimensions={1}, use_global_device_ids=true | all-gather | bytes 557056 | tf_op jit(solution)/shard_map/all_gather | solution.py:163
  36.8 0.5 slice.79
  38.6 1.2 slice.80
  40.5 1.3 scatter.6
  41.7 6.9 %all-to-all-start = ((bf16[16,3,256,128]{3,2,1,0:T(8,128)(2,1)}), bf16[16,3,256,128]{3,2,1,0:T(8,128)(2,1)S(1)}, u32[]{:S(2)}, u32[]{:S(2)}) async-start(bf16[16,3,256,128]{3,2,1,0:T(8,128)(2,1)} %scatter.6), calls=%async_computation | async-start | bytes 6291456 | tf_op jit(solution)/shard_map/all_to_all | solution.py:173
  48.6 1.5 slice_bitcast_fusion
  50.2 1.2 copy-done.4
  51.3 0.5 slice.83
  51.9 134.1 %all-gather.3.cloned.1.call-done = bf16[128,144,512]{2,1,0:T(8,128)(2,1)} async-done(((bf16[8,144,512]{2,1,0:T(8,128)(2,1)}), bf16[128,144,512]{2,1,0:T(8,128)(2,1)}) %all-gather.3.cloned.1.call-update) | async-done | bytes 18874384 | tf_op jit(solution)/shard_map/all_gather | solution.py:162
  185.9 1.2 slice.82
  189.0 1.3 scatter.9
  190.3 0.0 all-to-all-done
  190.3 6.0 %all-to-all-start.1 = ((bf16[16,3,128,128]{3,2,1,0:T(8,128)(2,1)}), bf16[16,3,128,128]{3,2,1,0:T(8,128)(2,1)}, u32[]{:S(2)}, u32[]{:S(2)}) async-start(bf16[16,3,128,128]{3,2,1,0:T(8,128)(2,1)} %scatter.9), calls=%async_computation.1 | async-start | bytes 3145728 | tf_op jit(solution)/shard_map/all_to_all | solution.py:173
  196.3 2.1 copy.30.over_rows
  198.4 0.3 convert_reduce_fusion.1
  198.7 0.1 select_reduce_fusion.slots
  198.9 1.0 copy-done
  199.9 11.3 %shard_map.100 = bf16[256,1024]{1,0:T(8,128)(2,1)S(1)} custom-call(s32[32]{0:T(128)S(1)} %select_reduce_fusion.slots, bf16[48,256,128]{2,1,0:T(8,128)(2,1)S(1)} %bitcast.65, bf16[16,8,144,512]{3,2,1,0:T(8,128)(2,1)} %bitcast.69, f32[2,4096]{1,0:T(2,128)S(1)} %bitcast_convert_fusion.bias, f32[1,256]{1,0:T(1,128)S(1)} %convert_element_type.88.comp_bias, ...), custom_call_target="tpu_custom_call" | custom-call | flops 5120000000 | bytes 24000000 | tf_op jit(solution)/shard_map/pallas_call | solution.py:87
  211.2 0.8 copy-done.2
  212.1 5.0 %collective-permute-start.14 = (bf16[16,1024]{1,0:T(8,128)(2,1)S(1)}, bf16[16,1024]{1,0:T(8,128)(2,1)S(1)}, u32[]{:S(2)}, u32[]{:S(2)}) collective-permute-start(bf16[16,1024]{1,0:T(8,128)(2,1)S(1)} %get-tuple-element.32), channel_id=1, source_target_pairs={{0,240},{16,0},{32,16},{48,32},{64,48},{80,64},{96,80},{112,96},{1... | collective-permute-start | bytes 98312 | tf_op jit(solution)/shard_map/ppermute | solution.py:191
  217.1 0.7 collective-permute-start.13
  217.8 1.2 collective-permute-start.12
  219.0 0.6 collective-permute-start.11
  219.5 2.4 collective-permute-start.10
  221.9 0.0 collective-permute-done.14
  221.9 4.0 %collective-permute-start.9 = (bf16[16,1024]{1,0:T(8,128)(2,1)S(1)}, bf16[16,1024]{1,0:T(8,128)(2,1)S(1)}, u32[]{:S(2)}, u32[]{:S(2)}) collective-permute-start(bf16[16,1024]{1,0:T(8,128)(2,1)S(1)} %get-tuple-element.37), channel_id=1, source_target_pairs={{0,160},{16,176},{32,192},{48,208},{64,224},{80,240},{96,0},{112,1... | collective-permute-start | bytes 98312 | tf_op jit(solution)/shard_map/ppermute | solution.py:191
  225.9 0.0 collective-permute-done.13
  225.9 0.0 collective-permute-start.8
  225.9 0.0 collective-permute-done.12
  225.9 2.1 collective-permute-start.7
  228.0 0.0 collective-permute-done.11
  228.0 2.1 collective-permute-start.6
  230.1 0.0 collective-permute-done.10
  230.1 3.0 %collective-permute-start.5 = (bf16[16,1024]{1,0:T(8,128)(2,1)S(1)}, bf16[16,1024]{1,0:T(8,128)(2,1)S(1)}, u32[]{:S(2)}, u32[]{:S(2)}) collective-permute-start(bf16[16,1024]{1,0:T(8,128)(2,1)S(1)} %get-tuple-element.41), channel_id=1, source_target_pairs={{0,96},{16,112},{32,128},{48,144},{64,160},{80,176},{96,192},{112,... | collective-permute-start | bytes 98312 | tf_op jit(solution)/shard_map/ppermute | solution.py:191
  233.1 0.0 collective-permute-done.9
  233.1 0.9 collective-permute-start.4
  234.0 0.0 collective-permute-done.8
  234.0 1.6 collective-permute-start.3
  235.6 0.0 collective-permute-done.7
  235.6 3.3 %collective-permute-start.2 = (bf16[16,1024]{1,0:T(8,128)(2,1)S(1)}, bf16[16,1024]{1,0:T(8,128)(2,1)S(1)}, u32[]{:S(2)}, u32[]{:S(2)}) collective-permute-start(bf16[16,1024]{1,0:T(8,128)(2,1)S(1)} %get-tuple-element.44), channel_id=1, source_target_pairs={{0,48},{16,64},{32,80},{48,96},{64,112},{80,128},{96,144},{112,160... | collective-permute-start | bytes 98312 | tf_op jit(solution)/shard_map/ppermute | solution.py:191
  238.9 0.0 collective-permute-done.6
  238.9 1.7 collective-permute-start.1
  240.6 0.0 collective-permute-done.5
  240.6 0.0 collective-permute-start
  240.6 0.0 all-to-all-done.1
  240.6 1.0 copy-done.1
  241.7 9.9 %shard_map.101 = bf16[128,1024]{1,0:T(8,128)(2,1)} custom-call(s32[32]{0:T(128)S(1)} %select_reduce_fusion.slots, bf16[48,128,128]{2,1,0:T(8,128)(2,1)} %bitcast.35.received, bf16[16,8,144,512]{3,2,1,0:T(8,128)(2,1)} %bitcast.70, f32[2,4096]{1,0:T(2,128)S(1)} %bitcast_convert_fusion.bias, f32[1,256]{1,0:T(1,128)S(1)} %convert_element_type.88.comp_bias, ...), custom_call_target="tpu_custom_call" | custom-call | flops 2560000000 | bytes 24000000 | tf_op jit(solution)/shard_map/pallas_call | solution.py:87
  251.6 6.7 %all-to-all-start.2 = ((bf16[16,8,1024]{2,1,0:T(8,128)(2,1)}), bf16[16,8,1024]{2,1,0:T(8,128)(2,1)S(1)}, u32[]{:S(2)}, u32[]{:S(2)}) async-start(bf16[16,8,1024]{2,1,0:T(8,128)(2,1)} %bitcast.37), calls=%async_computation.2 | async-start | bytes 524288 | tf_op jit(solution)/shard_map/all_to_all | solution.py:185
  258.3 0.0 collective-permute-done.4
  258.4 0.0 collective-permute-done.2
  258.4 0.0 collective-permute-done.1
  258.4 0.8 fusion.18
  259.2 7.6 %all-to-all-done.2 = bf16[16,8,1024]{2,1,0:T(8,128)(2,1)S(1)} async-done(((bf16[16,8,1024]{2,1,0:T(8,128)(2,1)}), bf16[16,8,1024]{2,1,0:T(8,128)(2,1)S(1)}, u32[]{:S(2)}, u32[]{:S(2)}) %all-to-all-start.2) | async-done | bytes 262176 | tf_op jit(solution)/shard_map/all_to_all | solution.py:185
  266.8 0.6 fusion.3
  (31 shorter events, 0.2 us)
Async XLA Ops:
  6.5 3.1 %copy-start.6 = (bf16[1,2,256,512]{3,2,1,0:T(8,128)(2,1)S(1)}, bf16[1,2,256,512]{3,2,1,0:T(8,128)(2,1)}, u32[]{:S(2)}) copy-start(bf16[1,2,256,512]{3,2,1,0:T(8,128)(2,1)} %param.15) | copy-start | bytes 1572868
  6.5 179.4 %all-gather.3.cloned.1.call-start = ((), (), s32[]{:S(2)}) async-start(), calls=%async_computation.3 | async-start | bytes 20054016 | tf_op jit(solution)/shard_map/all_gather | solution.py:162
  14.0 3.2 %copy-start.3 = (bf16[16,16,24,3,128]{4,2,1,3,0:T(8,128)(2,1)}, bf16[16,16,24,3,128]{4,2,1,3,0:T(8,128)(2,1)S(1)}, u32[]{:S(2)}) copy-start(bf16[16,16,24,3,128]{4,2,1,3,0:T(8,128)(2,1)S(1)} %copy.34) | copy-start | bytes 14155780
  14.0 3.2 %copy-start.7 = (bf16[256,64]{0,1:T(8,128)(2,1)S(1)}, bf16[256,64]{0,1:T(8,128)(2,1)}, u32[]{:S(2)}) copy-start(bf16[256,64]{0,1:T(8,128)(2,1)} %param.20) | copy-start | bytes 98308
  36.8 5.0 %copy-start.5 = (bf16[256,1024]{0,1:T(8,128)(2,1)}, bf16[256,1024]{0,1:T(8,128)(2,1)S(1)}, u32[]{:S(2)}) copy-start(bf16[256,1024]{0,1:T(8,128)(2,1)S(1)} %all_gather.9) | copy-start | bytes 1572868
  41.7 148.6 %all-to-all-start = ((bf16[16,3,256,128]{3,2,1,0:T(8,128)(2,1)}), bf16[16,3,256,128]{3,2,1,0:T(8,128)(2,1)S(1)}, u32[]{:S(2)}, u32[]{:S(2)}) async-start(bf16[16,3,256,128]{3,2,1,0:T(8,128)(2,1)} %scatter.6), calls=%async_computation | async-start | bytes 6291456 | tf_op jit(solution)/shard_map/all_to_all | solution.py:173
  50.2 1.2 copy-start.4
  51.3 147.0 %copy-start.12 = (bf16[1,256]{1,0:T(2,128)(2,1)S(1)}, bf16[1,256]{1,0:T(2,128)(2,1)}, u32[]{:S(2)}) copy-start(bf16[1,256]{1,0:T(2,128)(2,1)} %param.19) | copy-start | bytes 1540
  51.3 147.0 %copy-start.11 = (s32[512]{0:T(512)S(1)}, s32[512]{0:T(512)}, u32[]{:S(2)}) copy-start(s32[512]{0:T(512)} %param.22) | copy-start | bytes 6148
  51.3 147.1 %copy-start.8 = (s32[512]{0:T(512)S(1)}, s32[512]{0:T(512)}, u32[]{:S(2)}) copy-start(s32[512]{0:T(512)} %param.23) | copy-start | bytes 6148
  51.3 147.5 %copy-start.9 = (bf16[1,2,4096]{2,1,0:T(2,128)(2,1)S(1)}, bf16[1,2,4096]{2,1,0:T(2,128)(2,1)}, u32[]{:S(2)}) copy-start(bf16[1,2,4096]{2,1,0:T(2,128)(2,1)} %param.17) | copy-start | bytes 49156
  190.3 50.3 %all-to-all-start.1 = ((bf16[16,3,128,128]{3,2,1,0:T(8,128)(2,1)}), bf16[16,3,128,128]{3,2,1,0:T(8,128)(2,1)}, u32[]{:S(2)}, u32[]{:S(2)}) async-start(bf16[16,3,128,128]{3,2,1,0:T(8,128)(2,1)} %scatter.9), calls=%async_computation.1 | async-start | bytes 3145728 | tf_op jit(solution)/shard_map/all_to_all | solution.py:173
  198.9 1.0 copy-start
  211.2 0.8 copy-start.2
  212.1 9.8 %collective-permute-start.14 = (bf16[16,1024]{1,0:T(8,128)(2,1)S(1)}, bf16[16,1024]{1,0:T(8,128)(2,1)S(1)}, u32[]{:S(2)}, u32[]{:S(2)}) collective-permute-start(bf16[16,1024]{1,0:T(8,128)(2,1)S(1)} %get-tuple-element.32), channel_id=1, source_target_pairs={{0,240},{16,0},{32,16},{48,32},{64,48},{80,64},{96,80},{112,96},{1... | collective-permute-start | bytes 98312 | tf_op jit(solution)/shard_map/ppermute | solution.py:191
  217.1 8.8 %collective-permute-start.13 = (bf16[16,1024]{1,0:T(8,128)(2,1)S(1)}, bf16[16,1024]{1,0:T(8,128)(2,1)S(1)}, u32[]{:S(2)}, u32[]{:S(2)}) collective-permute-start(bf16[16,1024]{1,0:T(8,128)(2,1)S(1)} %get-tuple-element.33), channel_id=1, source_target_pairs={{0,224},{16,240},{32,0},{48,16},{64,32},{80,48},{96,64},{112,80},{... | collective-permute-start | bytes 98312 | tf_op jit(solution)/shard_map/ppermute | solution.py:191
  217.8 8.1 %collective-permute-start.12 = (bf16[16,1024]{1,0:T(8,128)(2,1)S(1)}, bf16[16,1024]{1,0:T(8,128)(2,1)S(1)}, u32[]{:S(2)}, u32[]{:S(2)}) collective-permute-start(bf16[16,1024]{1,0:T(8,128)(2,1)S(1)} %get-tuple-element.34), channel_id=1, source_target_pairs={{0,208},{16,224},{32,240},{48,0},{64,16},{80,32},{96,48},{112,64},... | collective-permute-start | bytes 98312 | tf_op jit(solution)/shard_map/ppermute | solution.py:191
  219.0 9.0 %collective-permute-start.11 = (bf16[16,1024]{1,0:T(8,128)(2,1)S(1)}, bf16[16,1024]{1,0:T(8,128)(2,1)S(1)}, u32[]{:S(2)}, u32[]{:S(2)}) collective-permute-start(bf16[16,1024]{1,0:T(8,128)(2,1)S(1)} %get-tuple-element.35), channel_id=1, source_target_pairs={{0,192},{16,208},{32,224},{48,240},{64,0},{80,16},{96,32},{112,48}... | collective-permute-start | bytes 98312 | tf_op jit(solution)/shard_map/ppermute | solution.py:191
  219.5 10.6 %collective-permute-start.10 = (bf16[16,1024]{1,0:T(8,128)(2,1)S(1)}, bf16[16,1024]{1,0:T(8,128)(2,1)S(1)}, u32[]{:S(2)}, u32[]{:S(2)}) collective-permute-start(bf16[16,1024]{1,0:T(8,128)(2,1)S(1)} %get-tuple-element.36), channel_id=1, source_target_pairs={{0,176},{16,192},{32,208},{48,224},{64,240},{80,0},{96,16},{112,32... | collective-permute-start | bytes 98312 | tf_op jit(solution)/shard_map/ppermute | solution.py:191
  221.9 11.3 %collective-permute-start.9 = (bf16[16,1024]{1,0:T(8,128)(2,1)S(1)}, bf16[16,1024]{1,0:T(8,128)(2,1)S(1)}, u32[]{:S(2)}, u32[]{:S(2)}) collective-permute-start(bf16[16,1024]{1,0:T(8,128)(2,1)S(1)} %get-tuple-element.37), channel_id=1, source_target_pairs={{0,160},{16,176},{32,192},{48,208},{64,224},{80,240},{96,0},{112,1... | collective-permute-start | bytes 98312 | tf_op jit(solution)/shard_map/ppermute | solution.py:191
  225.9 8.2 %collective-permute-start.8 = (bf16[16,1024]{1,0:T(8,128)(2,1)S(1)}, bf16[16,1024]{1,0:T(8,128)(2,1)S(1)}, u32[]{:S(2)}, u32[]{:S(2)}) collective-permute-start(bf16[16,1024]{1,0:T(8,128)(2,1)S(1)} %get-tuple-element.38), channel_id=1, source_target_pairs={{0,144},{16,160},{32,176},{48,192},{64,208},{80,224},{96,240},{112... | collective-permute-start | bytes 98312 | tf_op jit(solution)/shard_map/ppermute | solution.py:191
  225.9 9.7 %collective-permute-start.7 = (bf16[16,1024]{1,0:T(8,128)(2,1)S(1)}, bf16[16,1024]{1,0:T(8,128)(2,1)S(1)}, u32[]{:S(2)}, u32[]{:S(2)}) collective-permute-start(bf16[16,1024]{1,0:T(8,128)(2,1)S(1)} %get-tuple-element.39), channel_id=1, source_target_pairs={{0,128},{16,144},{32,160},{48,176},{64,192},{80,208},{96,224},{112... | collective-permute-start | bytes 98312 | tf_op jit(solution)/shard_map/ppermute | solution.py:191
  228.0 10.9 %collective-permute-start.6 = (bf16[16,1024]{1,0:T(8,128)(2,1)S(1)}, bf16[16,1024]{1,0:T(8,128)(2,1)S(1)}, u32[]{:S(2)}, u32[]{:S(2)}) collective-permute-start(bf16[16,1024]{1,0:T(8,128)(2,1)S(1)} %get-tuple-element.40), channel_id=1, source_target_pairs={{0,112},{16,128},{32,144},{48,160},{64,176},{80,192},{96,208},{112... | collective-permute-start | bytes 98312 | tf_op jit(solution)/shard_map/ppermute | solution.py:191
  230.1 10.5 %collective-permute-start.5 = (bf16[16,1024]{1,0:T(8,128)(2,1)S(1)}, bf16[16,1024]{1,0:T(8,128)(2,1)S(1)}, u32[]{:S(2)}, u32[]{:S(2)}) collective-permute-start(bf16[16,1024]{1,0:T(8,128)(2,1)S(1)} %get-tuple-element.41), channel_id=1, source_target_pairs={{0,96},{16,112},{32,128},{48,144},{64,160},{80,176},{96,192},{112,... | collective-permute-start | bytes 98312 | tf_op jit(solution)/shard_map/ppermute | solution.py:191
  233.1 25.2 %collective-permute-start.4 = (bf16[16,1024]{1,0:T(8,128)(2,1)S(1)}, bf16[16,1024]{1,0:T(8,128)(2,1)S(1)}, u32[]{:S(2)}, u32[]{:S(2)}) collective-permute-start(bf16[16,1024]{1,0:T(8,128)(2,1)S(1)} %get-tuple-element.42), channel_id=1, source_target_pairs={{0,80},{16,96},{32,112},{48,128},{64,144},{80,160},{96,176},{112,1... | collective-permute-start | bytes 98312 | tf_op jit(solution)/shard_map/ppermute | solution.py:191
  234.0 24.3 %collective-permute-start.3 = (bf16[16,1024]{1,0:T(8,128)(2,1)S(1)}, bf16[16,1024]{1,0:T(8,128)(2,1)S(1)}, u32[]{:S(2)}, u32[]{:S(2)}) collective-permute-start(bf16[16,1024]{1,0:T(8,128)(2,1)S(1)} %get-tuple-element.43), channel_id=1, source_target_pairs={{0,64},{16,80},{32,96},{48,112},{64,128},{80,144},{96,160},{112,17... | collective-permute-start | bytes 98312 | tf_op jit(solution)/shard_map/ppermute | solution.py:191
  235.6 22.8 %collective-permute-start.2 = (bf16[16,1024]{1,0:T(8,128)(2,1)S(1)}, bf16[16,1024]{1,0:T(8,128)(2,1)S(1)}, u32[]{:S(2)}, u32[]{:S(2)}) collective-permute-start(bf16[16,1024]{1,0:T(8,128)(2,1)S(1)} %get-tuple-element.44), channel_id=1, source_target_pairs={{0,48},{16,64},{32,80},{48,96},{64,112},{80,128},{96,144},{112,160... | collective-permute-start | bytes 98312 | tf_op jit(solution)/shard_map/ppermute | solution.py:191
  238.9 19.5 %collective-permute-start.1 = (bf16[16,1024]{1,0:T(8,128)(2,1)S(1)}, bf16[16,1024]{1,0:T(8,128)(2,1)S(1)}, u32[]{:S(2)}, u32[]{:S(2)}) collective-permute-start(bf16[16,1024]{1,0:T(8,128)(2,1)S(1)} %get-tuple-element.45), channel_id=1, source_target_pairs={{0,32},{16,48},{32,64},{48,80},{64,96},{80,112},{96,128},{112,144}... | collective-permute-start | bytes 98312 | tf_op jit(solution)/shard_map/ppermute | solution.py:191
  240.6 17.8 %collective-permute-start = (bf16[16,1024]{1,0:T(8,128)(2,1)S(1)}, bf16[16,1024]{1,0:T(8,128)(2,1)S(1)}, u32[]{:S(2)}, u32[]{:S(2)}) collective-permute-start(bf16[16,1024]{1,0:T(8,128)(2,1)S(1)} %get-tuple-element.31), channel_id=1, source_target_pairs={{0,16},{16,32},{32,48},{48,64},{64,80},{80,96},{96,112},{112,128},... | collective-permute-start | bytes 98312 | tf_op jit(solution)/shard_map/ppermute | solution.py:191
  240.6 1.0 copy-start.1
  241.7 16.7 %copy-start.10 = (bf16[1024]{0:T(1024)(128)(2,1)S(1)}, bf16[1024]{0:T(1024)(128)(2,1)}, u32[]{:S(2)}) copy-start(bf16[1024]{0:T(1024)(128)(2,1)} %param.21) | copy-start | bytes 6148
  251.6 15.2 %all-to-all-start.2 = ((bf16[16,8,1024]{2,1,0:T(8,128)(2,1)}), bf16[16,8,1024]{2,1,0:T(8,128)(2,1)S(1)}, u32[]{:S(2)}, u32[]{:S(2)}) async-start(bf16[16,8,1024]{2,1,0:T(8,128)(2,1)} %bitcast.37), calls=%async_computation.2 | async-start | bytes 524288 | tf_op jit(solution)/shard_map/all_to_all | solution.py:185
Sparse Core Ops, SparseCore 0:
  11.0 174.8 all-gather.2

commit v4 on v1

v4 whole, which is shorter than its diff:
```python
import jax
import jax.numpy as jnp
from jax import lax
from jax.experimental import pallas as pl
from jax.experimental.pallas import tpu as pltpu
from jax.sharding import PartitionSpec as P

F32 = jnp.float32
BF16 = jnp.bfloat16


def slot_order(table_tower, table_owner, tower_id, per_tower, slot_most):
    table_count = table_tower.shape[0]
    index = jnp.arange(table_count, dtype=jnp.int32)
    inside = table_tower == tower_id
    earlier = index[None, :] < index[:, None]
    before = inside[None, :] & earlier
    position_in = jnp.sum(before.astype(jnp.int32), axis=1)
    same_owner = table_owner[None, :] == table_owner[:, None]
    own_slot = jnp.sum((before & same_owner).astype(jnp.int32), axis=1)
    wanted = table_owner * slot_most + own_slot
    picked = inside[None, :] & (
        position_in[None, :] == jnp.arange(per_tower, dtype=jnp.int32)[:, None]
    )
    return jnp.sum(jnp.where(picked, wanted[None, :], 0), axis=1)


QUARTERS = 4


def lower_kernel(slots, received, gathered, base, lowered, down, sems):
    features, rank = base.shape[1], lowered.shape[1]
    copy = pltpu.make_async_copy(gathered.at[:, pl.ds(0, down.shape[1]), :], down, sems.at[1])
    for p in range(features // 128):
        pltpu.make_async_copy(
            received.at[slots[p]], base.at[:, pl.ds(p * 128, 128)], sems.at[0]
        ).start()
    copy.start()
    pltpu.make_async_copy(base, base, sems.at[0]).wait()
    copy.wait()
    lowered[...] = jnp.dot(
        base[...], down.reshape(features, rank)[...], preferred_element_type=F32
    ).astype(BF16)


def raise_kernel(
    tables, lowered_first, gathered, rest, bias, comp_bias, out, base, state, up0, up1, down, comp, over, sems
):
    features = base.shape[1]
    shards, rank, step = up0.shape
    width, block = comp.shape[2], shards // QUARTERS
    first = []
    for q in range(QUARTERS):
        here, there = pl.ds(q * block * step, block * step), pl.ds(q * block, block)
        first.append(
            (
                pltpu.make_async_copy(tables.at[:, here], base.at[:, here], sems.at[2 * q]),
                pltpu.make_async_copy(
                    rest.at[there, pl.ds(0, rank), :], up0.at[there], sems.at[2 * q + 1]
                ),
            )
        )
    later = [
        pltpu.make_async_copy(source, target, sems.at[2 * QUARTERS + n])
        for n, (source, target) in enumerate(
            (
                (gathered.at[:, pl.ds(step, step), :], down),
                (rest.at[:, pl.ds(rank, rank), :], up1),
                (rest.at[:, pl.ds(2 * rank, step), :], comp),
                (rest.at[:, pl.ds(2 * rank + step, over.shape[1]), :], over),
            )
        )
    ]
    for pair in first:
        pair[0].start()
        pair[1].start()
    for copy in later:
        copy.start()

    lowered = lowered_first[...]
    for s in range(shards):
        if s % block == 0:
            first[s // block][0].wait()
            first[s // block][1].wait()
        here = pl.ds(s * step, step)
        raised = jnp.dot(lowered, up0[s], preferred_element_type=F32)
        part = base[:, here].astype(F32)
        state[:, here] = (part * (raised + bias[0:1, here]) + part).astype(BF16)
    later[0].wait()
    lowered = jnp.dot(
        state[...], down.reshape(features, rank)[...], preferred_element_type=F32
    ).astype(BF16)
    later[1].wait()
    for s in range(shards):
        here = pl.ds(s * step, step)
        raised = jnp.dot(lowered, up1[s], preferred_element_type=F32)
        part, held = base[:, here].astype(F32), state[:, here].astype(F32)
        state[:, here] = (part * (raised + bias[1:2, here]) + held).astype(BF16)
    later[2].wait()
    squeezed = jnp.dot(state[...], comp.reshape(features, width)[...], preferred_element_type=F32)
    squeezed = (squeezed + comp_bias[...]).astype(BF16)
    later[3].wait()
    over_t = over.reshape(over.shape[0] * over.shape[1], width)[...]
    out[...] = lax.dot_general(
        squeezed, over_t, (((1,), (1,)), ((), ())), preferred_element_type=F32
    ).astype(BF16)


def on_device(
    pooled,
    cross_down,
    cross_up,
    cross_bias,
    comp_weight,
    comp_bias,
    over_weight,
    over_bias,
    table_tower,
    table_owner,
):
    tower_id = lax.axis_index("tower")
    shards, towers = lax.axis_size("shard"), lax.axis_size("tower")
    _, batch, slot_most, emb = pooled.shape
    layers, rank, step = cross_up.shape[1:]
    features = step * shards
    width = comp_weight.shape[2]
    samples = batch // shards
    columns = over_weight.shape[1]
    outputs = columns * shards

    gathered = lax.all_gather(cross_down[0].reshape(layers * step, rank), "shard", axis=0)
    packed = jnp.concatenate(
        [cross_up[0].reshape(layers * rank, step), comp_weight[0], over_weight.T]
    )
    rest = lax.all_gather(packed, "shard", axis=0)
    by_slot = pooled[0].transpose(1, 0, 2).reshape(slot_most, shards, samples, emb)
    received = lax.all_to_all(
        by_slot.transpose(1, 0, 2, 3), "shard", split_axis=0, concat_axis=0, tiled=True
    ).reshape(shards * slot_most, samples, emb)
    slots = slot_order(table_tower, table_owner, tower_id, features // emb, slot_most)

    anywhere = pl.BlockSpec(memory_space=pl.ANY)

    def whole(*shape):
        return pl.BlockSpec(shape, lambda i, *_: (0,) * len(shape))

    tables, lowered = pl.pallas_call(
        lower_kernel,
        grid_spec=pltpu.PrefetchScalarGridSpec(
            num_scalar_prefetch=1,
            grid=(1,),
            in_specs=[anywhere, anywhere],
            out_specs=[whole(samples, features), whole(samples, rank)],
            scratch_shapes=[
                pltpu.VMEM((shards, step, rank), BF16),
                pltpu.SemaphoreType.DMA((2,)),
            ],
        ),
        out_shape=[
            jax.ShapeDtypeStruct((samples, features), BF16),
            jax.ShapeDtypeStruct((samples, rank), BF16),
        ],
        compiler_params=pltpu.CompilerParams(vmem_limit_bytes=32 * 2**20),
        cost_estimate=pl.CostEstimate(
            flops=2 * samples * features * rank, bytes_accessed=12 * 10**6, transcendentals=0
        ),
    )(slots, received, gathered)

    partial = pl.pallas_call(
        raise_kernel,
        grid=(1,),
        in_specs=[
            anywhere,
            whole(samples, rank),
            anywhere,
            anywhere,
            whole(layers, features),
            whole(1, width),
        ],
        out_specs=whole(samples, outputs),
        scratch_shapes=[
            pltpu.VMEM((samples, features), BF16),
            pltpu.VMEM((samples, features), BF16),
            pltpu.VMEM((shards, rank, step), BF16),
            pltpu.VMEM((shards, rank, step), BF16),
            pltpu.VMEM((shards, step, rank), BF16),
            pltpu.VMEM((shards, step, width), BF16),
            pltpu.VMEM((shards, columns, width), BF16),
            pltpu.SemaphoreType.DMA((2 * QUARTERS + 4,)),
        ],
        out_shape=jax.ShapeDtypeStruct((samples, outputs), BF16),
        compiler_params=pltpu.CompilerParams(vmem_limit_bytes=48 * 2**20),
        cost_estimate=pl.CostEstimate(flops=6 * 10**9, bytes_accessed=20 * 10**6, transcendentals=0),
    )(tables, lowered, gathered, rest, cross_bias[0].astype(F32), comp_bias.astype(F32))

    summed = lax.all_to_all(
        partial.reshape(towers, samples // towers, outputs), "tower", 0, 0, tiled=True
    )
    total = jnp.sum(summed.astype(F32), axis=0) + over_bias.astype(F32)
    return jax.nn.relu(total).astype(BF16)[None]


def solution(mesh):
    placed = (
        P("tower", None, "shard", None),
        P("tower", None, "shard", None),
        P("tower", None, None, "shard"),
        P("tower", None, None),
        P("tower", "shard", None),
        P("tower", None),
        P("tower", "shard"),
        P(),
        P(),
        P(),
    )
    return jax.shard_map(
        on_device, mesh=mesh, in_specs=placed, out_specs=P("shard", "tower", None), check_vma=False
    )
```

time: 266 us -> 279 us (1.049)
  waiting for transfers between devices: 43 us -> 221 us
  blocking collectives: 168 us -> 0 us
    all_gather x1 -> x0, blocking collectives: 168 us -> none  [on_device(): over_rows = lax.all_gather(over_weight, 'shard', axis=1, tiled=True)]
    all_to_all x1, waiting for transfers between devices: 0.01 us -> 141 us  [on_device(): lax.all_to_all(by_slot.transpose(1, 0, 2, 3), 'shard', split_axis=0, conc...]
    all_gather x1 -> x2, waiting for transfers between devices: 28 us -> 63.6 us  [the longest x1 60.8 us: on_device(): rest = lax.all_gather(packed, 'shard', axis=0)]
    unnamed x16 -> x14, local copies, waits for them, and re-layouts: 0.03 us -> 4.16 us
    pallas_call x1 -> x2, Pallas kernels: 15 us -> 15.7 us  [the longest x1 11.4 us: on_device(): pl.pallas_call(raise_kernel, grid=(1,), in_specs=[anywhere, whole(samples...]
  transfers between devices with their start and end apart: 3 -> 4, of which waited for: 2 -> 4; matrix products, arithmetic and copies ran while one was open for 2% -> 3% of each run, Pallas kernels for 0% -> 2%
where the time goes in v4:
time: 279 us; the launch traced here: 278 us
  waiting for transfers between devices  221 us (79%)
  Pallas kernels  15.7 us (6%)
  starting transfers between devices  14.7 us (5%)
  between operations  13.5 us (5%)
  local copies, waits for them, and re-layouts  9.2 us (3%)
  other arithmetic  3.86 us (1%)
    all_to_all x1, waiting for transfers between devices, on_device(): lax.all_to_all(by_slot.transpose(1, 0, 2, 3), 'shard', split_axis=0, conc...  141 us
    all_gather x1, waiting for transfers between devices, on_device(): rest = lax.all_gather(packed, 'shard', axis=0)  60.8 us
    all_to_all x1, waiting for transfers between devices, on_device(): lax.all_to_all(partial.reshape(towers, samples // towers, outputs), 'towe...  15 us
    pallas_call x1, Pallas kernels, on_device(): pl.pallas_call(raise_kernel, grid=(1,), in_specs=[anywhere, whole(samples...  11.4 us
    all_to_all x1, starting transfers between devices, on_device(): lax.all_to_all(by_slot.transpose(1, 0, 2, 3), 'shard', split_axis=0, conc...  7.82 us
    all_to_all x1, starting transfers between devices, on_device(): lax.all_to_all(partial.reshape(towers, samples // towers, outputs), 'towe...  6.82 us
  transfers between devices with their start and end apart: 4, of which 4 were waited for; matrix products, arithmetic and copies ran while one was open for 3% of the time, Pallas kernels for 2%

profile of v4, /device:TPU:96, one launch (start us, length us, event | category | flops | bytes accessed | tf_op | source)
XLA Modules:
  0.0 277.6 jit_solution(6706914207247875418)
XLA Ops:
  6.5 0.0 all-gather.4.cloned.1.call-start
  6.5 0.7 all-gather.4.cloned.1.call-update
  7.3 0.0 all-gather.6.cloned.1.call-start
  7.3 2.0 pad_maximum_fusion
  9.3 0.0 all-gather.6.cloned.1.call-update
  9.3 5.0 %copy.15 = bf16[3,16,384,128]{3,2,0,1:T(8,128)(2,1)} copy(bf16[3,16,384,128]{3,2,1,0:T(8,128)(2,1)} %bitcast.26) | data formatting | bytes 9437184 | tf_op jit(solution)/shard_map/reshape | solution.py:136
  14.4 0.0 copy-start.6
  14.4 0.0 copy-start.5
  14.4 0.0 copy-start.2
  14.4 0.0 copy-start.3
  14.4 7.8 %all-to-all-start = ((bf16[16,3,384,128]{3,2,1,0:T(8,128)(2,1)}), bf16[16,3,384,128]{3,2,1,0:T(8,128)(2,1)}, u32[]{:S(2)}, u32[]{:S(2)}) async-start(bf16[16,3,384,128]{3,2,1,0:T(8,128)(2,1)} %bitcast.24), calls=%async_computation | async-start | bytes 9437184 | tf_op jit(solution)/shard_map/all_to_all | solution.py:137
  22.2 0.0 copy-done.6
  22.2 0.0 copy-done.5
  22.3 0.0 copy-done.2
  22.3 0.3 convert_reduce_fusion.2
  22.6 0.1 select_reduce_fusion.slots
  22.7 0.0 copy-done.3
  22.7 0.6 bitcast_convert_fusion.bias
  23.4 141.4 %all-to-all-done = bf16[16,3,384,128]{3,2,1,0:T(8,128)(2,1)} async-done(((bf16[16,3,384,128]{3,2,1,0:T(8,128)(2,1)}), bf16[16,3,384,128]{3,2,1,0:T(8,128)(2,1)}, u32[]{:S(2)}, u32[]{:S(2)}) %all-to-all-start) | async-done | bytes 4718624 | tf_op jit(solution)/shard_map/all_to_all | solution.py:137
  164.8 2.8 all-gather.4.cloned.1.call-done.gathered
  167.5 0.0 copy-start
  167.5 3.4 %copy-done = bf16[16,512,512]{2,1,0:T(8,128)(2,1)S(1)} copy-done((bf16[16,512,512]{2,1,0:T(8,128)(2,1)S(1)}, bf16[16,512,512]{2,1,0:T(8,128)(2,1)}, u32[]{:S(2)}) %copy-start) | copy-done | bytes 8388632
  170.9 4.3 %shard_map.100 = (bf16[384,4096]{1,0:T(8,128)(2,1)S(1)}, bf16[384,512]{1,0:T(8,128)(2,1)S(1)}) custom-call(s32[32]{0:T(128)S(1)} %select_reduce_fusion.slots, bf16[48,384,128]{2,1,0:T(8,128)(2,1)} %bitcast.4.received, bf16[16,512,512]{2,1,0:T(8,128)(2,1)S(1)} %copy-done), custom_call_target="tpu_custom_call" | custom-call | flops 1610612736 | bytes 12000000 | tf_op jit(solution)/shard_map/pallas_call | solution.py:147
  175.2 60.8 %all-gather.6.cloned.1.call-done = bf16[21504,256]{1,0:T(8,128)(2,1)} async-done(((bf16[1344,256]{1,0:T(8,128)(2,1)}), bf16[21504,256]{1,0:T(8,128)(2,1)}) %all-gather.6.cloned.1.call-update) | async-done | bytes 11010064 | tf_op jit(solution)/shard_map/all_gather | solution.py:135
  236.1 0.0 copy-start.1
  236.1 0.8 copy-done.1
  236.8 0.0 copy-start.4
  236.8 11.4 %shard_map.101 = bf16[384,1024]{1,0:T(8,128)(2,1)} custom-call(bf16[384,4096]{1,0:T(8,128)(2,1)S(1)} %get-tuple-element.7.tables, bf16[384,512]{1,0:T(8,128)(2,1)S(1)} %get-tuple-element.8.lowered_first, bf16[16,512,512]{2,1,0:T(8,128)(2,1)} %all-gather.4.cloned.1.call-done.gathered, bf16[16,1344,256]{2,1,0:T(8,128)(2,1)} %bitcast.25, ...), custom_call_target="tpu_custom_call" | custom-call | flops 6000000000 | bytes 20000000 | tf_op jit(solution)/shard_map/pallas_call | solution.py:169
  248.2 6.8 %all-to-all-start.1 = ((bf16[16,24,1024]{2,1,0:T(8,128)(2,1)}), bf16[16,24,1024]{2,1,0:T(8,128)(2,1)S(1)}, u32[]{:S(2)}, u32[]{:S(2)}) async-start(bf16[16,24,1024]{2,1,0:T(8,128)(2,1)} %bitcast.11), calls=%async_computation.1 | async-start | bytes 1572864 | tf_op jit(solution)/shard_map/all_to_all | solution.py:196
  255.0 0.0 copy-done.4
  255.0 15.0 %all-to-all-done.1 = bf16[16,24,1024]{2,1,0:T(8,128)(2,1)S(1)} async-done(((bf16[16,24,1024]{2,1,0:T(8,128)(2,1)}), bf16[16,24,1024]{2,1,0:T(8,128)(2,1)S(1)}, u32[]{:S(2)}, u32[]{:S(2)}) %all-to-all-start.1) | async-done | bytes 786464 | tf_op jit(solution)/shard_map/all_to_all | solution.py:196
  270.0 0.1 convert_reduce_fusion
  270.2 0.6 fusion.3
  (4 shorter events, 0.0 us)
Async XLA Ops:
  6.5 161.0 %all-gather.4.cloned.1.call-start = ((), (), s32[]{:S(2)}) async-start(), calls=%async_computation.2 | async-start | bytes 8912896 | tf_op jit(solution)/shard_map/all_gather | solution.py:131
  7.3 228.8 %all-gather.6.cloned.1.call-start = ((), (), s32[]{:S(2)}) async-start(), calls=%async_computation.3 | async-start | bytes 11698176 | tf_op jit(solution)/shard_map/all_gather | solution.py:135
  14.4 7.8 %copy-start.6 = (bf16[1,256]{1,0:T(2,128)(2,1)S(1)}, bf16[1,256]{1,0:T(2,128)(2,1)}, u32[]{:S(2)}) copy-start(bf16[1,256]{1,0:T(2,128)(2,1)} %param.15) | copy-start | bytes 1540
  14.4 7.8 %copy-start.5 = (s32[512]{0:T(512)S(1)}, s32[512]{0:T(512)}, u32[]{:S(2)}) copy-start(s32[512]{0:T(512)} %param.18) | copy-start | bytes 6148
  14.4 7.9 %copy-start.2 = (s32[512]{0:T(512)S(1)}, s32[512]{0:T(512)}, u32[]{:S(2)}) copy-start(s32[512]{0:T(512)} %param.19) | copy-start | bytes 6148
  14.4 8.3 %copy-start.3 = (bf16[1,2,4096]{2,1,0:T(2,128)(2,1)S(1)}, bf16[1,2,4096]{2,1,0:T(2,128)(2,1)}, u32[]{:S(2)}) copy-start(bf16[1,2,4096]{2,1,0:T(2,128)(2,1)} %param.13) | copy-start | bytes 49156
  14.4 150.3 %all-to-all-start = ((bf16[16,3,384,128]{3,2,1,0:T(8,128)(2,1)}), bf16[16,3,384,128]{3,2,1,0:T(8,128)(2,1)}, u32[]{:S(2)}, u32[]{:S(2)}) async-start(bf16[16,3,384,128]{3,2,1,0:T(8,128)(2,1)} %bitcast.24), calls=%async_computation | async-start | bytes 9437184 | tf_op jit(solution)/shard_map/all_to_all | solution.py:137
  167.5 3.4 %copy-start = (bf16[16,512,512]{2,1,0:T(8,128)(2,1)S(1)}, bf16[16,512,512]{2,1,0:T(8,128)(2,1)}, u32[]{:S(2)}) copy-start(bf16[16,512,512]{2,1,0:T(8,128)(2,1)} %all-gather.4.cloned.1.call-done.gathered) | copy-start | bytes 25165828
  236.1 0.8 copy-start.1
  236.8 18.2 %copy-start.4 = (bf16[1024]{0:T(1024)(128)(2,1)S(1)}, bf16[1024]{0:T(1024)(128)(2,1)}, u32[]{:S(2)}) copy-start(bf16[1024]{0:T(1024)(128)(2,1)} %param.17) | copy-start | bytes 6148
  248.2 21.8 %all-to-all-start.1 = ((bf16[16,24,1024]{2,1,0:T(8,128)(2,1)}), bf16[16,24,1024]{2,1,0:T(8,128)(2,1)S(1)}, u32[]{:S(2)}, u32[]{:S(2)}) async-start(bf16[16,24,1024]{2,1,0:T(8,128)(2,1)} %bitcast.11), calls=%async_computation.1 | async-start | bytes 1572864 | tf_op jit(solution)/shard_map/all_to_all | solution.py:196
Sparse Core Ops, SparseCore 0:
  9.2 158.2 all-gather.3
  169.3 66.6 all-gather.5

commit v5 on v1

v5 whole, which is shorter than its diff:
```python
import jax
import jax.numpy as jnp
from jax import lax
from jax.experimental import pallas as pl
from jax.experimental.pallas import tpu as pltpu
from jax.sharding import PartitionSpec as P

F32 = jnp.float32
BF16 = jnp.bfloat16


def slot_order(table_tower, table_owner, tower_id, per_tower, slot_most):
    table_count = table_tower.shape[0]
    index = jnp.arange(table_count, dtype=jnp.int32)
    inside = table_tower == tower_id
    earlier = index[None, :] < index[:, None]
    before = inside[None, :] & earlier
    position_in = jnp.sum(before.astype(jnp.int32), axis=1)
    same_owner = table_owner[None, :] == table_owner[:, None]
    own_slot = jnp.sum((before & same_owner).astype(jnp.int32), axis=1)
    wanted = table_owner * slot_most + own_slot
    picked = inside[None, :] & (
        position_in[None, :] == jnp.arange(per_tower, dtype=jnp.int32)[:, None]
    )
    return jnp.sum(jnp.where(picked, wanted[None, :], 0), axis=1)


QUARTERS = 4
BACK = (0, 1, 15, 2, 14, 3, 13, 4, 12, 5, 11, 6, 10, 7, 9, 8)


def tower_kernel(places, *refs):
    pieces, refs = refs[:-13], refs[-13:]
    weights, bias, comp_bias, out, base, state, down0, down1, up0, up1, comp, over, sems = refs
    features = base.shape[1]
    shards, step, rank = down0.shape
    width, slot_most = comp.shape[2], pieces[0].shape[0]
    block, half = shards // QUARTERS, rank // 2
    me = places[shards * slot_most]
    for k in range(shards):
        owner = lax.rem(me + shards - BACK[k], shards)
        for slot in range(slot_most):
            place = places[owner * slot_most + slot]

            @pl.when(place >= 0)
            def _(k=k, slot=slot, place=place):
                pltpu.make_async_copy(
                    pieces[k].at[slot],
                    base.at[:, pl.ds(pl.multiple_of(place * 128, 128), 128)],
                    sems.at[0],
                ).start()

    def bring(first, count, target, n):
        return pltpu.make_async_copy(weights.at[:, pl.ds(first, count), :], target, sems.at[n])

    early = []
    for q in range(QUARTERS):
        there = pl.ds(q * block, block)
        for h in range(2):
            early.append(
                pltpu.make_async_copy(
                    weights.at[there, pl.ds(2 * step * h, step), :],
                    down0.at[there, :, pl.ds(h * half, half)],
                    sems.at[1 + 2 * q + h],
                )
            )
    n, at_up = 1 + 2 * QUARTERS, 4 * step
    bring_up0 = bring(at_up, rank, up0, n)
    bring_down1 = [
        bring(2 * step * h + step, step, down1.at[:, :, pl.ds(h * half, half)], n + 1 + h)
        for h in range(2)
    ]
    bring_up1 = bring(at_up + rank, rank, up1, n + 3)
    bring_comp = bring(at_up + 2 * rank, step, comp, n + 4)
    bring_over = bring(at_up + 2 * rank + step, over.shape[1], over, n + 5)
    for copy in (*early, bring_up0, *bring_down1, bring_up1, bring_comp, bring_over):
        copy.start()

    pltpu.make_async_copy(base, base, sems.at[0]).wait()
    total = None
    for q in range(QUARTERS):
        early[2 * q].wait()
        early[2 * q + 1].wait()
        deep = block * step
        part = jnp.dot(
            base[:, pl.ds(q * deep, deep)],
            down0.reshape(features, rank)[pl.ds(q * deep, deep), :],
            preferred_element_type=F32,
        )
        total = part if total is None else total + part
    lowered = total.astype(BF16)
    bring_up0.wait()
    for s in range(shards):
        here = pl.ds(s * step, step)
        raised = jnp.dot(lowered, up0[s], preferred_element_type=F32)
        part = base[:, here].astype(F32)
        state[:, here] = (part * (raised + bias[0:1, here]) + part).astype(BF16)
    bring_down1[0].wait()
    bring_down1[1].wait()
    lowered = jnp.dot(
        state[...], down1.reshape(features, rank)[...], preferred_element_type=F32
    ).astype(BF16)
    bring_up1.wait()
    for s in range(shards):
        here = pl.ds(s * step, step)
        raised = jnp.dot(lowered, up1[s], preferred_element_type=F32)
        part, held = base[:, here].astype(F32), state[:, here].astype(F32)
        state[:, here] = (part * (raised + bias[1:2, here]) + held).astype(BF16)
    bring_comp.wait()
    squeezed = jnp.dot(state[...], comp.reshape(features, width)[...], preferred_element_type=F32)
    squeezed = (squeezed + comp_bias[...]).astype(BF16)
    bring_over.wait()
    over_t = over.reshape(over.shape[0] * over.shape[1], width)[...]
    out[...] = lax.dot_general(
        squeezed, over_t, (((1,), (1,)), ((), ())), preferred_element_type=F32
    ).astype(BF16)


def on_device(
    pooled,
    cross_down,
    cross_up,
    cross_bias,
    comp_weight,
    comp_bias,
    over_weight,
    over_bias,
    table_tower,
    table_owner,
):
    tower_id, shard = lax.axis_index("tower"), lax.axis_index("shard")
    shards, towers = 16, 16
    _, batch, slot_most, emb = pooled.shape
    layers, rank, step = cross_up.shape[1:]
    features = step * shards
    width = comp_weight.shape[2]
    samples = batch // shards
    columns = over_weight.shape[1]
    outputs = columns * shards

    down = cross_down[0].reshape(layers * step, rank)
    packed = jnp.concatenate(
        [
            down[:, : rank // 2],
            down[:, rank // 2 :],
            cross_up[0].reshape(layers * rank, step),
            comp_weight[0],
            over_weight.T,
        ]
    )
    weights = lax.all_gather(packed, "shard", axis=0)

    by_slot = pooled[0].transpose(1, 0, 2).reshape(slot_most, shards, samples, emb)

    def piece_for(to):
        return lax.dynamic_index_in_dim(by_slot, to % 16, 1, keepdims=False)

    pieces = [piece_for(shard)]
    for k in BACK[1:]:
        moves = [(i, (i + k) % 16) for i in range(16)]
        pieces.append(lax.ppermute(piece_for(shard + k), "shard", moves))

    slots = slot_order(table_tower, table_owner, tower_id, features // emb, slot_most)
    index = jnp.arange(shards * slot_most, dtype=jnp.int32)[:, None]
    turn = jnp.arange(1, slots.shape[0] + 1, dtype=jnp.int32)[None, :]
    places = jnp.sum(jnp.where(slots[None, :] == index, turn, 0), axis=1) - 1
    places = jnp.concatenate([places, shard[None]]).astype(jnp.int32)

    anywhere = pl.BlockSpec(memory_space=pl.ANY)

    def whole(*shape):
        return pl.BlockSpec(shape, lambda i, *_: (0,) * len(shape))

    partial = pl.pallas_call(
        tower_kernel,
        grid_spec=pltpu.PrefetchScalarGridSpec(
            num_scalar_prefetch=1,
            grid=(1,),
            in_specs=[anywhere] * (shards + 1) + [whole(layers, features), whole(1, width)],
            out_specs=whole(samples, outputs),
            scratch_shapes=[
                pltpu.VMEM((samples, features), BF16),
                pltpu.VMEM((samples, features), BF16),
                pltpu.VMEM((shards, step, rank), BF16),
                pltpu.VMEM((shards, step, rank), BF16),
                pltpu.VMEM((shards, rank, step), BF16),
                pltpu.VMEM((shards, rank, step), BF16),
                pltpu.VMEM((shards, step, width), BF16),
                pltpu.VMEM((shards, columns, width), BF16),
                pltpu.SemaphoreType.DMA((7 + 2 * QUARTERS,)),
            ],
        ),
        out_shape=jax.ShapeDtypeStruct((samples, outputs), BF16),
        compiler_params=pltpu.CompilerParams(vmem_limit_bytes=48 * 2**20),
        cost_estimate=pl.CostEstimate(flops=8 * 10**9, bytes_accessed=24 * 10**6, transcendentals=0),
    )(
        places,
        *pieces,
        weights,
        cross_bias[0].astype(F32),
        comp_bias.astype(F32),
    )

    summed = lax.all_to_all(
        partial.reshape(towers, samples // towers, outputs), "tower", 0, 0, tiled=True
    )
    total = jnp.sum(summed.astype(F32), axis=0) + over_bias.astype(F32)
    return jax.nn.relu(total).astype(BF16)[None]


def solution(mesh):
    placed = (
        P("tower", None, "shard", None),
        P("tower", None, "shard", None),
        P("tower", None, None, "shard"),
        P("tower", None, None),
        P("tower", "shard", None),
        P("tower", None),
        P("tower", "shard"),
        P(),
        P(),
        P(),
    )
    return jax.shard_map(
        on_device, mesh=mesh, in_specs=placed, out_specs=P("shard", "tower", None), check_vma=False
    )
```

time: 266 us -> 266 us (level)
  blocking collectives: 168 us -> 0 us
  waiting for transfers between devices: 43 us -> 153 us
  starting transfers between devices: 14.6 us -> 65 us
  local copies, waits for them, and re-layouts: 7.59 us -> 16 us
    all_gather x1 -> x0, blocking collectives: 168 us -> none  [on_device(): over_rows = lax.all_gather(over_weight, 'shard', axis=1, tiled=True)]
    ppermute x0 -> x15, waiting for transfers between devices: none -> 97.5 us  [on_device(): pieces.append(lax.ppermute(piece_for(shard + k), 'shard', moves))]
    ppermute x0 -> x15, starting transfers between devices: none -> 57.9 us  [on_device(): pieces.append(lax.ppermute(piece_for(shard + k), 'shard', moves))]
    all_gather x1, waiting for transfers between devices: 28 us -> 40.2 us  [on_device(): weights = lax.all_gather(packed, 'shard', axis=0)]
    unnamed x16 -> x42, local copies, waits for them, and re-layouts: 0.03 us -> 11.5 us
    all_to_all x1 -> x0, starting transfers between devices: 7.82 us -> none  [on_device(): lax.all_to_all(by_slot.transpose(1, 0, 2, 3), 'shard', split_axis=0, conc...]
    reshape x3 -> x0, local copies, waits for them, and re-layouts: 5.53 us -> none  [the longest x1 5.1 us: on_device(): pooled[0].transpose(1, 0, 2).reshape(slot_most, shards, samples, emb)]
    squeeze x0 -> x1, local copies, waits for them, and re-layouts: none -> 4.44 us  [piece_for(): return lax.dynamic_index_in_dim(by_slot, to % 16, 1, keepdims=False)]
  transfers between devices with their start and end apart: 3 -> 17, of which waited for: 2 -> 10; matrix products, arithmetic and copies ran while one was open for 2% -> 2% of each run, Pallas kernels for 0% -> 0%
where the time goes in v5:
time: 266 us; the launch traced here: 264 us
  waiting for transfers between devices  153 us (58%)
  starting transfers between devices  65 us (24%)
  local copies, waits for them, and re-layouts  16 us (6%)
  Pallas kernels  15 us (6%)
  between operations  13.8 us (5%)
    ppermute x15, waiting for transfers between devices, on_device(): pieces.append(lax.ppermute(piece_for(shard + k), 'shard', moves))  97.5 us
    ppermute x15, starting transfers between devices, on_device(): pieces.append(lax.ppermute(piece_for(shard + k), 'shard', moves))  57.9 us
    all_gather x1, waiting for transfers between devices, on_device(): weights = lax.all_gather(packed, 'shard', axis=0)  40.2 us
    all_to_all x1, waiting for transfers between devices, on_device(): lax.all_to_all(partial.reshape(towers, samples // towers, outputs), 'towe...  15 us
    pallas_call x1, Pallas kernels, on_device(): pl.pallas_call(tower_kernel, grid_spec=pltpu.PrefetchScalarGridSpec(num_s...  15 us
    unnamed x42, local copies, waits for them, and re-layouts  11.5 us
    all_to_all x1, starting transfers between devices, on_device(): lax.all_to_all(partial.reshape(towers, samples // towers, outputs), 'towe...  7.05 us
  transfers between devices with their start and end apart: 17, of which 10 were waited for; matrix products, arithmetic and copies ran while one was open for 2% of the time, Pallas kernels for 0%

profile of v5, /device:TPU:96, one launch (start us, length us, event | category | flops | bytes accessed | tf_op | source)
XLA Modules:
  0.0 263.9 jit_solution(5566920905451113826)
XLA Ops:
  6.5 0.0 all-gather.3.cloned.1.call-start
  6.5 1.0 slice_dynamic-update-slice_fusion.1
  7.6 1.0 slice_dynamic-update-slice_fusion
  8.6 0.0 copy-done.11
  8.6 0.0 copy-done.12
  8.6 0.0 copy-done.13
  8.7 1.0 copy-done.10
  9.7 0.0 all-gather.3.cloned.1.call-update
  9.9 0.0 copy-start.17
  10.0 0.0 copy-start.15
  10.0 0.0 copy-start.14
  10.0 0.0 copy-start.18
  10.0 4.4 %dynamic-slice_bitcast_fusion = (bf16[3,384,128]{2,1,0:T(8,128)(2,1)S(1)}, bf16[3,384,128]{2,1,0:T(8,128)(2,1)S(1)}, bf16[3,384,128]{2,1,0:T(8,128)(2,1)S(1)}, b...) fusion(bf16[3,16,384,128]{3,2,1,0:T(8,128)(2,1)} %bitcast.87, ...), kind=kLoop, calls=%fused_computation.6 | loop fusion | bytes 9437248 | tf_op jit(solution)/shard_map/jit(dynamic_index_in_dim)/squeeze | solution.py:156
  14.4 4.6 %collective-permute-start.14 = (bf16[3,384,128]{2,1,0:T(8,128)(2,1)S(1)}, bf16[3,384,128]{2,1,0:T(8,128)(2,1)S(1)}, u32[]{:S(2)}, u32[]{:S(2)}) collective-permute-start(bf16[3,384,128]{2,1,0:T(8,128)(2,1)S(1)} %get-tuple-element.7), channel_id=1, source_target_pairs={{0,8},{1,9},{2,10},{3,11},{4,12},{5,13},{6,14},{7,15},{8,0},{9,1},... | collective-permute-start | bytes 884744 | tf_op jit(solution)/shard_map/ppermute | solution.py:161
  19.0 0.6 collective-permute-start.13
  19.6 4.2 %collective-permute-start.12 = (bf16[3,384,128]{2,1,0:T(8,128)(2,1)S(1)}, bf16[3,384,128]{2,1,0:T(8,128)(2,1)S(1)}, u32[]{:S(2)}, u32[]{:S(2)}) collective-permute-start(bf16[3,384,128]{2,1,0:T(8,128)(2,1)S(1)} %get-tuple-element.9), channel_id=1, source_target_pairs={{0,7},{1,8},{2,9},{3,10},{4,11},{5,12},{6,13},{7,14},{8,15},{9,0},... | collective-permute-start | bytes 884744 | tf_op jit(solution)/shard_map/ppermute | solution.py:161
  23.7 0.7 collective-permute-start.11
  24.4 4.3 %collective-permute-start.10 = (bf16[3,384,128]{2,1,0:T(8,128)(2,1)S(1)}, bf16[3,384,128]{2,1,0:T(8,128)(2,1)S(1)}, u32[]{:S(2)}, u32[]{:S(2)}) collective-permute-start(bf16[3,384,128]{2,1,0:T(8,128)(2,1)S(1)} %get-tuple-element.11), channel_id=1, source_target_pairs={{0,6},{1,7},{2,8},{3,9},{4,10},{5,11},{6,12},{7,13},{8,14},{9,15},... | collective-permute-start | bytes 884744 | tf_op jit(solution)/shard_map/ppermute | solution.py:161
  28.8 0.3 convert_reduce_fusion.2
  29.2 10.5 %collective-permute-done.14.refs_15_ = bf16[3,384,128]{2,1,0:T(8,128)(2,1)S(1)} collective-permute-done((bf16[3,384,128]{2,1,0:T(8,128)(2,1)S(1)}, bf16[3,384,128]{2,1,0:T(8,128)(2,1)S(1)}, u32[]{:S(2)}, u32[]{:S(2)}) %collective-permute-start.14) | collective-permute-done | bytes 294944 | tf_op jit(solution)/shard_map/ppermute | solution.py:161
  39.7 0.0 collective-permute-start.9
  39.7 19.7 %collective-permute-done.13.refs_14_ = bf16[3,384,128]{2,1,0:T(8,128)(2,1)S(1)} collective-permute-done((bf16[3,384,128]{2,1,0:T(8,128)(2,1)S(1)}, bf16[3,384,128]{2,1,0:T(8,128)(2,1)S(1)}, u32[]{:S(2)}, u32[]{:S(2)}) %collective-permute-start.13) | collective-permute-done | bytes 294944 | tf_op jit(solution)/shard_map/ppermute | solution.py:161
  59.4 12.0 %collective-permute-start.8 = (bf16[3,384,128]{2,1,0:T(8,128)(2,1)}, bf16[3,384,128]{2,1,0:T(8,128)(2,1)S(1)}, u32[]{:S(2)}, u32[]{:S(2)}) collective-permute-start(bf16[3,384,128]{2,1,0:T(8,128)(2,1)} %get-tuple-element.13), channel_id=1, source_target_pairs={{0,5},{1,6},{2,7},{3,8},{4,9},{5,10},{6,11},{7,12},{8,13},{9,14},{... | collective-permute-start | bytes 884744 | tf_op jit(solution)/shard_map/ppermute | solution.py:161
  71.3 7.1 %collective-permute-done.12.refs_13_ = bf16[3,384,128]{2,1,0:T(8,128)(2,1)S(1)} collective-permute-done((bf16[3,384,128]{2,1,0:T(8,128)(2,1)S(1)}, bf16[3,384,128]{2,1,0:T(8,128)(2,1)S(1)}, u32[]{:S(2)}, u32[]{:S(2)}) %collective-permute-start.12) | collective-permute-done | bytes 294944 | tf_op jit(solution)/shard_map/ppermute | solution.py:161
  78.4 0.5 collective-permute-start.7
  78.9 5.5 %collective-permute-done.11.refs_12_ = bf16[3,384,128]{2,1,0:T(8,128)(2,1)S(1)} collective-permute-done((bf16[3,384,128]{2,1,0:T(8,128)(2,1)S(1)}, bf16[3,384,128]{2,1,0:T(8,128)(2,1)S(1)}, u32[]{:S(2)}, u32[]{:S(2)}) %collective-permute-start.11) | collective-permute-done | bytes 294944 | tf_op jit(solution)/shard_map/ppermute | solution.py:161
  84.4 2.9 %collective-permute-start.6 = (bf16[3,384,128]{2,1,0:T(8,128)(2,1)}, bf16[3,384,128]{2,1,0:T(8,128)(2,1)S(1)}, u32[]{:S(2)}, u32[]{:S(2)}) collective-permute-start(bf16[3,384,128]{2,1,0:T(8,128)(2,1)} %get-tuple-element.15), channel_id=1, source_target_pairs={{0,4},{1,5},{2,6},{3,7},{4,8},{5,9},{6,10},{7,11},{8,12},{9,13},{1... | collective-permute-start | bytes 884744 | tf_op jit(solution)/shard_map/ppermute | solution.py:161
  87.3 26.5 %collective-permute-done.10.refs_11_ = bf16[3,384,128]{2,1,0:T(8,128)(2,1)S(1)} collective-permute-done((bf16[3,384,128]{2,1,0:T(8,128)(2,1)S(1)}, bf16[3,384,128]{2,1,0:T(8,128)(2,1)S(1)}, u32[]{:S(2)}, u32[]{:S(2)}) %collective-permute-start.10) | collective-permute-done | bytes 294944 | tf_op jit(solution)/shard_map/ppermute | solution.py:161
  113.8 0.0 collective-permute-start.5
  113.8 0.1 select_reduce_fusion
  113.9 0.1 select_reduce_fusion.1
  114.0 9.8 %collective-permute-done.9.refs_10_ = bf16[3,384,128]{2,1,0:T(8,128)(2,1)S(1)} collective-permute-done((bf16[3,384,128]{2,1,0:T(8,128)(2,1)}, bf16[3,384,128]{2,1,0:T(8,128)(2,1)S(1)}, u32[]{:S(2)}, u32[]{:S(2)}) %collective-permute-start.9) | collective-permute-done | bytes 294944 | tf_op jit(solution)/shard_map/ppermute | solution.py:161
  123.8 0.0 collective-permute-start.4
  123.8 0.0 collective-permute-done.8.refs_9_
  123.8 7.5 %collective-permute-start.3 = (bf16[3,384,128]{2,1,0:T(8,128)(2,1)}, bf16[3,384,128]{2,1,0:T(8,128)(2,1)S(1)}, u32[]{:S(2)}, u32[]{:S(2)}) collective-permute-start(bf16[3,384,128]{2,1,0:T(8,128)(2,1)} %get-tuple-element.18), channel_id=1, source_target_pairs={{0,14},{1,15},{2,0},{3,1},{4,2},{5,3},{6,4},{7,5},{8,6},{9,7},{10,... | collective-permute-start | bytes 884744 | tf_op jit(solution)/shard_map/ppermute | solution.py:161
  131.3 0.0 collective-permute-done.7.refs_8_
  131.3 0.0 collective-permute-start.2
  131.3 0.0 collective-permute-done.6.refs_7_
  131.3 11.1 %collective-permute-start.1 = (bf16[3,384,128]{2,1,0:T(8,128)(2,1)}, bf16[3,384,128]{2,1,0:T(8,128)(2,1)S(1)}, u32[]{:S(2)}, u32[]{:S(2)}) collective-permute-start(bf16[3,384,128]{2,1,0:T(8,128)(2,1)} %get-tuple-element.20), channel_id=1, source_target_pairs={{0,15},{1,0},{2,1},{3,2},{4,3},{5,4},{6,5},{7,6},{8,7},{9,8},{10,9... | collective-permute-start | bytes 884744 | tf_op jit(solution)/shard_map/ppermute | solution.py:161
  142.4 1.6 collective-permute-done.5.refs_6_
  144.1 9.6 %collective-permute-start = (bf16[3,384,128]{2,1,0:T(8,128)(2,1)}, bf16[3,384,128]{2,1,0:T(8,128)(2,1)S(1)}, u32[]{:S(2)}, u32[]{:S(2)}) collective-permute-start(bf16[3,384,128]{2,1,0:T(8,128)(2,1)} %get-tuple-element.21), channel_id=1, source_target_pairs={{0,1},{1,2},{2,3},{3,4},{4,5},{5,6},{6,7},{7,8},{8,9},{9,10},{10,1... | collective-permute-start | bytes 884744 | tf_op jit(solution)/shard_map/ppermute | solution.py:161
  153.7 0.1 pad_add_fusion.places
  153.8 0.0 collective-permute-done.4.refs_5_
  153.8 0.7 copy-done
  154.5 0.0 collective-permute-done.3.refs_4_
  154.5 0.7 copy-done.2
  155.2 16.7 %collective-permute-done.2.refs_3_ = bf16[3,384,128]{2,1,0:T(8,128)(2,1)S(1)} collective-permute-done((bf16[3,384,128]{2,1,0:T(8,128)(2,1)}, bf16[3,384,128]{2,1,0:T(8,128)(2,1)S(1)}, u32[]{:S(2)}, u32[]{:S(2)}) %collective-permute-start.2) | collective-permute-done | bytes 294944 | tf_op jit(solution)/shard_map/ppermute | solution.py:161
  172.0 0.7 copy-done.4
  172.7 0.0 collective-permute-done.1.refs_2_
  172.7 0.7 copy-done.6
  173.5 0.0 collective-permute-done.refs_1_
  173.5 0.7 copy-done.8
  174.2 40.2 %all-gather.3.cloned.1.call-done = bf16[37888,256]{1,0:T(8,128)(2,1)} async-done(((bf16[2368,256]{1,0:T(8,128)(2,1)}), bf16[37888,256]{1,0:T(8,128)(2,1)}) %all-gather.3.cloned.1.call-update) | async-done | bytes 19398672 | tf_op jit(solution)/shard_map/all_gather | solution.py:151
  214.4 1.0 copy-done.1
  215.4 1.0 copy-done.3
  216.3 1.0 copy-done.5
  217.3 1.0 copy-done.7
  218.3 1.0 copy-done.9
  219.2 15.0 %shard_map.100 = bf16[384,1024]{1,0:T(8,128)(2,1)} custom-call(s32[49]{0:T(128)S(1)} %pad_add_fusion.places, bf16[3,384,128]{2,1,0:T(8,128)(2,1)S(1)} %get-tuple-element.22.refs_0_, bf16[3,384,128]{2,1,0:T(8,128)(2,1)S(1)} %copy-done.9, bf16[3,384,128]{2,1,0:T(8,128)(2,1)S(1)} %copy-done.7, bf16[3,384,128]{2,1,0:T(8,128)(2,1)S(1)} %copy-done.5, ...), custom_call_target="tpu_custom_call" | custom-call | flops 8000000000 | bytes 24000000 | tf_op jit(solution)/shard_map/pallas_call | solution.py:174
  234.2 0.0 copy-start.16
  234.2 7.1 %all-to-all-start = ((bf16[16,24,1024]{2,1,0:T(8,128)(2,1)}), bf16[16,24,1024]{2,1,0:T(8,128)(2,1)S(1)}, u32[]{:S(2)}, u32[]{:S(2)}) async-start(bf16[16,24,1024]{2,1,0:T(8,128)(2,1)} %bitcast.26), calls=%async_computation | async-start | bytes 1572864 | tf_op jit(solution)/shard_map/all_to_all | solution.py:204
  241.3 15.0 %all-to-all-done = bf16[16,24,1024]{2,1,0:T(8,128)(2,1)S(1)} async-done(((bf16[16,24,1024]{2,1,0:T(8,128)(2,1)}), bf16[16,24,1024]{2,1,0:T(8,128)(2,1)S(1)}, u32[]{:S(2)}, u32[]{:S(2)}) %all-to-all-start) | async-done | bytes 786464 | tf_op jit(solution)/shard_map/all_to_all | solution.py:204
  256.3 0.1 convert_reduce_fusion
  256.4 0.6 fusion.3
  (29 shorter events, 0.1 us)
Async XLA Ops:
  6.5 2.0 copy-start.11
  6.5 2.1 copy-start.12
  6.5 2.1 copy-start.13
  6.5 207.9 %all-gather.3.cloned.1.call-start = ((), (), s32[]{:S(2)}) async-start(), calls=%async_computation.1 | async-start | bytes 20611072 | tf_op jit(solution)/shard_map/all_gather | solution.py:151
  8.7 1.0 copy-start.10
  9.9 18.8 %copy-start.17 = (s32[512]{0:T(512)S(1)}, s32[512]{0:T(512)}, u32[]{:S(2)}) copy-start(s32[512]{0:T(512)} %param.18) | copy-start | bytes 6148
  10.0 18.8 %copy-start.15 = (bf16[1,2,4096]{2,1,0:T(2,128)(2,1)S(1)}, bf16[1,2,4096]{2,1,0:T(2,128)(2,1)}, u32[]{:S(2)}) copy-start(bf16[1,2,4096]{2,1,0:T(2,128)(2,1)} %param.13) | copy-start | bytes 49156
  10.0 18.8 %copy-start.14 = (s32[512]{0:T(512)S(1)}, s32[512]{0:T(512)}, u32[]{:S(2)}) copy-start(s32[512]{0:T(512)} %param.19) | copy-start | bytes 6148
  10.0 19.1 %copy-start.18 = (bf16[1,256]{1,0:T(2,128)(2,1)S(1)}, bf16[1,256]{1,0:T(2,128)(2,1)}, u32[]{:S(2)}) copy-start(bf16[1,256]{1,0:T(2,128)(2,1)} %param.15) | copy-start | bytes 1540
  14.4 25.3 %collective-permute-start.14 = (bf16[3,384,128]{2,1,0:T(8,128)(2,1)S(1)}, bf16[3,384,128]{2,1,0:T(8,128)(2,1)S(1)}, u32[]{:S(2)}, u32[]{:S(2)}) collective-permute-start(bf16[3,384,128]{2,1,0:T(8,128)(2,1)S(1)} %get-tuple-element.7), channel_id=1, source_target_pairs={{0,8},{1,9},{2,10},{3,11},{4,12},{5,13},{6,14},{7,15},{8,0},{9,1},... | collective-permute-start | bytes 884744 | tf_op jit(solution)/shard_map/ppermute | solution.py:161
  19.0 40.4 %collective-permute-start.13 = (bf16[3,384,128]{2,1,0:T(8,128)(2,1)S(1)}, bf16[3,384,128]{2,1,0:T(8,128)(2,1)S(1)}, u32[]{:S(2)}, u32[]{:S(2)}) collective-permute-start(bf16[3,384,128]{2,1,0:T(8,128)(2,1)S(1)} %get-tuple-element.8), channel_id=1, source_target_pairs={{0,9},{1,10},{2,11},{3,12},{4,13},{5,14},{6,15},{7,0},{8,1},{9,2},... | collective-permute-start | bytes 884744 | tf_op jit(solution)/shard_map/ppermute | solution.py:161
  19.6 58.9 %collective-permute-start.12 = (bf16[3,384,128]{2,1,0:T(8,128)(2,1)S(1)}, bf16[3,384,128]{2,1,0:T(8,128)(2,1)S(1)}, u32[]{:S(2)}, u32[]{:S(2)}) collective-permute-start(bf16[3,384,128]{2,1,0:T(8,128)(2,1)S(1)} %get-tuple-element.9), channel_id=1, source_target_pairs={{0,7},{1,8},{2,9},{3,10},{4,11},{5,12},{6,13},{7,14},{8,15},{9,0},... | collective-permute-start | bytes 884744 | tf_op jit(solution)/shard_map/ppermute | solution.py:161
  23.7 60.6 %collective-permute-start.11 = (bf16[3,384,128]{2,1,0:T(8,128)(2,1)S(1)}, bf16[3,384,128]{2,1,0:T(8,128)(2,1)S(1)}, u32[]{:S(2)}, u32[]{:S(2)}) collective-permute-start(bf16[3,384,128]{2,1,0:T(8,128)(2,1)S(1)} %get-tuple-element.10), channel_id=1, source_target_pairs={{0,10},{1,11},{2,12},{3,13},{4,14},{5,15},{6,0},{7,1},{8,2},{9,3},... | collective-permute-start | bytes 884744 | tf_op jit(solution)/shard_map/ppermute | solution.py:161
  24.4 89.3 %collective-permute-start.10 = (bf16[3,384,128]{2,1,0:T(8,128)(2,1)S(1)}, bf16[3,384,128]{2,1,0:T(8,128)(2,1)S(1)}, u32[]{:S(2)}, u32[]{:S(2)}) collective-permute-start(bf16[3,384,128]{2,1,0:T(8,128)(2,1)S(1)} %get-tuple-element.11), channel_id=1, source_target_pairs={{0,6},{1,7},{2,8},{3,9},{4,10},{5,11},{6,12},{7,13},{8,14},{9,15},... | collective-permute-start | bytes 884744 | tf_op jit(solution)/shard_map/ppermute | solution.py:161
  39.7 84.1 %collective-permute-start.9 = (bf16[3,384,128]{2,1,0:T(8,128)(2,1)}, bf16[3,384,128]{2,1,0:T(8,128)(2,1)S(1)}, u32[]{:S(2)}, u32[]{:S(2)}) collective-permute-start(bf16[3,384,128]{2,1,0:T(8,128)(2,1)} %get-tuple-element.12), channel_id=1, source_target_pairs={{0,11},{1,12},{2,13},{3,14},{4,15},{5,0},{6,1},{7,2},{8,3},{9,4},{... | collective-permute-start | bytes 884744 | tf_op jit(solution)/shard_map/ppermute | solution.py:161
  59.4 64.4 %collective-permute-start.8 = (bf16[3,384,128]{2,1,0:T(8,128)(2,1)}, bf16[3,384,128]{2,1,0:T(8,128)(2,1)S(1)}, u32[]{:S(2)}, u32[]{:S(2)}) collective-permute-start(bf16[3,384,128]{2,1,0:T(8,128)(2,1)} %get-tuple-element.13), channel_id=1, source_target_pairs={{0,5},{1,6},{2,7},{3,8},{4,9},{5,10},{6,11},{7,12},{8,13},{9,14},{... | collective-permute-start | bytes 884744 | tf_op jit(solution)/shard_map/ppermute | solution.py:161
  78.4 52.9 %collective-permute-start.7 = (bf16[3,384,128]{2,1,0:T(8,128)(2,1)}, bf16[3,384,128]{2,1,0:T(8,128)(2,1)S(1)}, u32[]{:S(2)}, u32[]{:S(2)}) collective-permute-start(bf16[3,384,128]{2,1,0:T(8,128)(2,1)} %get-tuple-element.14), channel_id=1, source_target_pairs={{0,12},{1,13},{2,14},{3,15},{4,0},{5,1},{6,2},{7,3},{8,4},{9,5},{1... | collective-permute-start | bytes 884744 | tf_op jit(solution)/shard_map/ppermute | solution.py:161
  84.4 47.0 %collective-permute-start.6 = (bf16[3,384,128]{2,1,0:T(8,128)(2,1)}, bf16[3,384,128]{2,1,0:T(8,128)(2,1)S(1)}, u32[]{:S(2)}, u32[]{:S(2)}) collective-permute-start(bf16[3,384,128]{2,1,0:T(8,128)(2,1)} %get-tuple-element.15), channel_id=1, source_target_pairs={{0,4},{1,5},{2,6},{3,7},{4,8},{5,9},{6,10},{7,11},{8,12},{9,13},{1... | collective-permute-start | bytes 884744 | tf_op jit(solution)/shard_map/ppermute | solution.py:161
  113.8 30.3 %collective-permute-start.5 = (bf16[3,384,128]{2,1,0:T(8,128)(2,1)}, bf16[3,384,128]{2,1,0:T(8,128)(2,1)S(1)}, u32[]{:S(2)}, u32[]{:S(2)}) collective-permute-start(bf16[3,384,128]{2,1,0:T(8,128)(2,1)} %get-tuple-element.16), channel_id=1, source_target_pairs={{0,13},{1,14},{2,15},{3,0},{4,1},{5,2},{6,3},{7,4},{8,5},{9,6},{10... | collective-permute-start | bytes 884744 | tf_op jit(solution)/shard_map/ppermute | solution.py:161
  123.8 30.0 %collective-permute-start.4 = (bf16[3,384,128]{2,1,0:T(8,128)(2,1)}, bf16[3,384,128]{2,1,0:T(8,128)(2,1)S(1)}, u32[]{:S(2)}, u32[]{:S(2)}) collective-permute-start(bf16[3,384,128]{2,1,0:T(8,128)(2,1)} %get-tuple-element.17), channel_id=1, source_target_pairs={{0,3},{1,4},{2,5},{3,6},{4,7},{5,8},{6,9},{7,10},{8,11},{9,12},{10... | collective-permute-start | bytes 884744 | tf_op jit(solution)/shard_map/ppermute | solution.py:161
  123.8 30.7 %collective-permute-start.3 = (bf16[3,384,128]{2,1,0:T(8,128)(2,1)}, bf16[3,384,128]{2,1,0:T(8,128)(2,1)S(1)}, u32[]{:S(2)}, u32[]{:S(2)}) collective-permute-start(bf16[3,384,128]{2,1,0:T(8,128)(2,1)} %get-tuple-element.18), channel_id=1, source_target_pairs={{0,14},{1,15},{2,0},{3,1},{4,2},{5,3},{6,4},{7,5},{8,6},{9,7},{10,... | collective-permute-start | bytes 884744 | tf_op jit(solution)/shard_map/ppermute | solution.py:161
  131.3 40.7 %collective-permute-start.2 = (bf16[3,384,128]{2,1,0:T(8,128)(2,1)}, bf16[3,384,128]{2,1,0:T(8,128)(2,1)S(1)}, u32[]{:S(2)}, u32[]{:S(2)}) collective-permute-start(bf16[3,384,128]{2,1,0:T(8,128)(2,1)} %get-tuple-element.19), channel_id=1, source_target_pairs={{0,2},{1,3},{2,4},{3,5},{4,6},{5,7},{6,8},{7,9},{8,10},{9,11},{10,... | collective-permute-start | bytes 884744 | tf_op jit(solution)/shard_map/ppermute | solution.py:161
  131.3 41.4 %collective-permute-start.1 = (bf16[3,384,128]{2,1,0:T(8,128)(2,1)}, bf16[3,384,128]{2,1,0:T(8,128)(2,1)S(1)}, u32[]{:S(2)}, u32[]{:S(2)}) collective-permute-start(bf16[3,384,128]{2,1,0:T(8,128)(2,1)} %get-tuple-element.20), channel_id=1, source_target_pairs={{0,15},{1,0},{2,1},{3,2},{4,3},{5,4},{6,5},{7,6},{8,7},{9,8},{10,9... | collective-permute-start | bytes 884744 | tf_op jit(solution)/shard_map/ppermute | solution.py:161
  144.1 29.4 %collective-permute-start = (bf16[3,384,128]{2,1,0:T(8,128)(2,1)}, bf16[3,384,128]{2,1,0:T(8,128)(2,1)S(1)}, u32[]{:S(2)}, u32[]{:S(2)}) collective-permute-start(bf16[3,384,128]{2,1,0:T(8,128)(2,1)} %get-tuple-element.21), channel_id=1, source_target_pairs={{0,1},{1,2},{2,3},{3,4},{4,5},{5,6},{6,7},{7,8},{8,9},{9,10},{10,1... | collective-permute-start | bytes 884744 | tf_op jit(solution)/shard_map/ppermute | solution.py:161
  153.8 0.7 copy-start
  154.5 0.7 copy-start.2
  172.0 0.7 copy-start.4
  172.7 0.7 copy-start.6
  173.5 0.7 copy-start.8
  214.4 1.0 copy-start.1
  215.4 1.0 copy-start.3
  216.3 1.0 copy-start.5
  217.3 1.0 copy-start.7
  218.3 1.0 copy-start.9
  234.2 7.1 %copy-start.16 = (bf16[1024]{0:T(1024)(128)(2,1)S(1)}, bf16[1024]{0:T(1024)(128)(2,1)}, u32[]{:S(2)}) copy-start(bf16[1024]{0:T(1024)(128)(2,1)} %param.17) | copy-start | bytes 6148
  234.2 22.1 %all-to-all-start = ((bf16[16,24,1024]{2,1,0:T(8,128)(2,1)}), bf16[16,24,1024]{2,1,0:T(8,128)(2,1)S(1)}, u32[]{:S(2)}, u32[]{:S(2)}) async-start(bf16[16,24,1024]{2,1,0:T(8,128)(2,1)} %bitcast.26), calls=%async_computation | async-start | bytes 1572864 | tf_op jit(solution)/shard_map/all_to_all | solution.py:204
Sparse Core Ops, SparseCore 0:
  9.8 204.5 all-gather.2

commit v6 on v5

--- a/solution.py
+++ b/solution.py
@@ -29,13 +29,9 @@
 BACK = (0, 1, 15, 2, 14, 3, 13, 4, 12, 5, 11, 6, 10, 7, 9, 8)
 
 
-def tower_kernel(places, *refs):
-    pieces, refs = refs[:-13], refs[-13:]
-    weights, bias, comp_bias, out, base, state, down0, down1, up0, up1, comp, over, sems = refs
-    features = base.shape[1]
-    shards, step, rank = down0.shape
-    width, slot_most = comp.shape[2], pieces[0].shape[0]
-    block, half = shards // QUARTERS, rank // 2
+def table_kernel(places, *refs):
+    pieces, (base, sem) = refs[:-2], refs[-2:]
+    shards, slot_most = len(pieces), pieces[0].shape[0]
     me = places[shards * slot_most]
     for k in range(shards):
         owner = lax.rem(me + shards - BACK[k], shards)
@@ -47,24 +43,38 @@
                 pltpu.make_async_copy(
                     pieces[k].at[slot],
                     base.at[:, pl.ds(pl.multiple_of(place * 128, 128), 128)],
-                    sems.at[0],
+                    sem,
                 ).start()
+
+    pltpu.make_async_copy(base, base, sem).wait()
+
+
+def tower_kernel(
+    tables, weights, bias, comp_bias, out, base, state, down0, down1, up0, up1, comp, over, sems
+):
+    features = base.shape[1]
+    shards, step, rank = down0.shape
+    width = comp.shape[2]
+    block, half = shards // QUARTERS, rank // 2
 
     def bring(first, count, target, n):
         return pltpu.make_async_copy(weights.at[:, pl.ds(first, count), :], target, sems.at[n])
 
     early = []
     for q in range(QUARTERS):
-        there = pl.ds(q * block, block)
+        there, columns = pl.ds(q * block, block), pl.ds(q * block * step, block * step)
+        early.append(
+            pltpu.make_async_copy(tables.at[:, columns], base.at[:, columns], sems.at[3 * q])
+        )
         for h in range(2):
             early.append(
                 pltpu.make_async_copy(
                     weights.at[there, pl.ds(2 * step * h, step), :],
                     down0.at[there, :, pl.ds(h * half, half)],
-                    sems.at[1 + 2 * q + h],
+                    sems.at[3 * q + 1 + h],
                 )
             )
-    n, at_up = 1 + 2 * QUARTERS, 4 * step
+    n, at_up = 3 * QUARTERS, 4 * step
     bring_up0 = bring(at_up, rank, up0, n)
     bring_down1 = [
         bring(2 * step * h + step, step, down1.at[:, :, pl.ds(h * half, half)], n + 1 + h)
@@ -76,11 +86,10 @@
     for copy in (*early, bring_up0, *bring_down1, bring_up1, bring_comp, bring_over):
         copy.start()
 
-    pltpu.make_async_copy(base, base, sems.at[0]).wait()
     total = None
     for q in range(QUARTERS):
-        early[2 * q].wait()
-        early[2 * q + 1].wait()
+        for copy in early[3 * q : 3 * q + 3]:
+            copy.wait()
         deep = block * step
         part = jnp.dot(
             base[:, pl.ds(q * deep, deep)],
@@ -171,12 +180,25 @@
     def whole(*shape):
         return pl.BlockSpec(shape, lambda i, *_: (0,) * len(shape))
 
-    partial = pl.pallas_call(
-        tower_kernel,
+    tables = pl.pallas_call(
+        table_kernel,
         grid_spec=pltpu.PrefetchScalarGridSpec(
             num_scalar_prefetch=1,
             grid=(1,),
-            in_specs=[anywhere] * (shards + 1) + [whole(layers, features), whole(1, width)],
+            in_specs=[anywhere] * shards,
+            out_specs=whole(samples, features),
+            scratch_shapes=[pltpu.SemaphoreType.DMA],
+        ),
+        out_shape=jax.ShapeDtypeStruct((samples, features), BF16),
+        compiler_params=pltpu.CompilerParams(vmem_limit_bytes=12 * 2**20),
+        cost_estimate=pl.CostEstimate(flops=0, bytes_accessed=10 * 10**6, transcendentals=0),
+    )(places, *pieces)
+
+    partial = pl.pallas_call(
+        tower_kernel,
+        grid_spec=pl.GridSpec(
+            grid=(1,),
+            in_specs=[anywhere, anywhere, whole(layers, features), whole(1, width)],
             out_specs=whole(samples, outputs),
             scratch_shapes=[
                 pltpu.VMEM((samples, features), BF16),
@@ -187,19 +209,13 @@
                 pltpu.VMEM((shards, rank, step), BF16),
                 pltpu.VMEM((shards, step, width), BF16),
                 pltpu.VMEM((shards, columns, width), BF16),
-                pltpu.SemaphoreType.DMA((7 + 2 * QUARTERS,)),
+                pltpu.SemaphoreType.DMA((6 + 3 * QUARTERS,)),
             ],
         ),
         out_shape=jax.ShapeDtypeStruct((samples, outputs), BF16),
-        compiler_params=pltpu.CompilerParams(vmem_limit_bytes=48 * 2**20),
+        compiler_params=pltpu.CompilerParams(vmem_limit_bytes=36 * 2**20),
         cost_estimate=pl.CostEstimate(flops=8 * 10**9, bytes_accessed=24 * 10**6, transcendentals=0),
-    )(
-        places,
-        *pieces,
-        weights,
-        cross_bias[0].astype(F32),
-        comp_bias.astype(F32),
-    )
+    )(tables, weights, cross_bias[0].astype(F32), comp_bias.astype(F32))
 
     summed = lax.all_to_all(
         partial.reshape(towers, samples // towers, outputs), "tower", 0, 0, tiled=True

time: 266 us -> 260 us (0.977)
  starting transfers between devices: 65 us -> 40.7 us
  waiting for transfers between devices: 153 us -> 172 us
    ppermute x15, starting transfers between devices: 57.9 us -> 33.5 us  [on_device(): pieces.append(lax.ppermute(piece_for(shard + k), 'shard', moves))]
    ppermute x15, waiting for transfers between devices: 97.5 us -> 120 us  [on_device(): pieces.append(lax.ppermute(piece_for(shard + k), 'shard', moves))]
    all_gather x1, waiting for transfers between devices: 40.2 us -> 37.3 us  [on_device(): weights = lax.all_gather(packed, 'shard', axis=0)]
    unnamed x42 -> x44, local copies, waits for them, and re-layouts: 11.5 us -> 12.4 us
    pallas_call x1 -> x2, Pallas kernels: 15 us -> 14.2 us  [the longest x1 12.4 us: on_device(): pl.pallas_call(tower_kernel, grid_spec=pl.GridSpec(grid=(1,), in_specs=[a...]
  transfers between devices with their start and end apart: 17 -> 17, of which waited for: 10 -> 10; matrix products, arithmetic and copies ran while one was open for 2% -> 2% of each run, Pallas kernels for 0% -> 1%
where the time goes in v6:
time: 260 us; the launch traced here: 259 us
  waiting for transfers between devices  172 us (66%)
  starting transfers between devices  40.7 us (16%)
  local copies, waits for them, and re-layouts  17 us (7%)
  Pallas kernels  14.2 us (5%)
  between operations  13.9 us (5%)
    ppermute x15, waiting for transfers between devices, on_device(): pieces.append(lax.ppermute(piece_for(shard + k), 'shard', moves))  120 us
    all_gather x1, waiting for transfers between devices, on_device(): weights = lax.all_gather(packed, 'shard', axis=0)  37.3 us
    ppermute x15, starting transfers between devices, on_device(): pieces.append(lax.ppermute(piece_for(shard + k), 'shard', moves))  33.5 us
    all_to_all x1, waiting for transfers between devices, on_device(): lax.all_to_all(partial.reshape(towers, samples // towers, outputs), 'towe...  15 us
    unnamed x44, local copies, waits for them, and re-layouts  12.4 us
    pallas_call x1, Pallas kernels, on_device(): pl.pallas_call(tower_kernel, grid_spec=pl.GridSpec(grid=(1,), in_specs=[a...  12.4 us
    all_to_all x1, starting transfers between devices, on_device(): lax.all_to_all(partial.reshape(towers, samples // towers, outputs), 'towe...  7.16 us
  transfers between devices with their start and end apart: 17, of which 10 were waited for; matrix products, arithmetic and copies ran while one was open for 2% of the time, Pallas kernels for 1%

profile of v6, /device:TPU:96, one launch (start us, length us, event | category | flops | bytes accessed | tf_op | source)
XLA Modules:
  0.0 259.2 jit_solution(14542339297328890967)
XLA Ops:
  6.5 1.0 slice_dynamic-update-slice_fusion.1
  7.6 1.0 slice_dynamic-update-slice_fusion
  8.6 0.0 copy-done.14
  8.7 1.0 copy-done.11
  9.7 0.0 all-gather.3.cloned.1.call-update
  9.9 0.0 copy-start.18
  9.9 0.0 copy-start.16
  10.0 0.0 copy-start.15
  10.0 0.0 copy-start.19
  10.0 4.6 %dynamic-slice_bitcast_fusion = (bf16[3,384,128]{2,1,0:T(8,128)(2,1)}, bf16[3,384,128]{2,1,0:T(8,128)(2,1)}, bf16[3,384,128]{2,1,0:T(8,128)(2,1)}, bf16[3,384,12...) fusion(bf16[3,16,384,128]{3,2,1,0:T(8,128)(2,1)} %bitcast.88, ...), kind=kLoop, calls=%fused_computation.6 | loop fusion | bytes 9437248 | tf_op jit(solution)/shard_map/jit(dynamic_index_in_dim)/squeeze | solution.py:165
  14.5 0.0 collective-permute-start
  14.5 1.7 collective-permute-start.1
  16.3 4.0 %collective-permute-start.10 = (bf16[3,384,128]{2,1,0:T(8,128)(2,1)}, bf16[3,384,128]{2,1,0:T(8,128)(2,1)S(1)}, u32[]{:S(2)}, u32[]{:S(2)}) collective-permute-start(bf16[3,384,128]{2,1,0:T(8,128)(2,1)} %get-tuple-element.11), channel_id=1, source_target_pairs={{0,6},{1,7},{2,8},{3,9},{4,10},{5,11},{6,12},{7,13},{8,14},{9,15},... | collective-permute-start | bytes 884744 | tf_op jit(solution)/shard_map/ppermute | solution.py:170
  20.3 0.0 collective-permute-start.11
  20.3 3.5 %collective-permute-start.12 = (bf16[3,384,128]{2,1,0:T(8,128)(2,1)}, bf16[3,384,128]{2,1,0:T(8,128)(2,1)S(1)}, u32[]{:S(2)}, u32[]{:S(2)}) collective-permute-start(bf16[3,384,128]{2,1,0:T(8,128)(2,1)} %get-tuple-element.9), channel_id=1, source_target_pairs={{0,7},{1,8},{2,9},{3,10},{4,11},{5,12},{6,13},{7,14},{8,15},{9,0},... | collective-permute-start | bytes 884744 | tf_op jit(solution)/shard_map/ppermute | solution.py:170
  23.8 0.0 copy-done.15
  23.8 0.3 convert_reduce_fusion.2
  24.2 0.0 collective-permute-done.refs_1_
  24.2 0.0 copy-start.1
  24.2 0.7 copy-done.1
  24.9 2.2 collective-permute-start.13
  27.1 0.0 collective-permute-done.1.refs_2_
  27.1 0.7 copy-done.3
  27.8 7.3 %collective-permute-start.14 = (bf16[3,384,128]{2,1,0:T(8,128)(2,1)}, bf16[3,384,128]{2,1,0:T(8,128)(2,1)S(1)}, u32[]{:S(2)}, u32[]{:S(2)}) collective-permute-start(bf16[3,384,128]{2,1,0:T(8,128)(2,1)} %get-tuple-element.7), channel_id=1, source_target_pairs={{0,8},{1,9},{2,10},{3,11},{4,12},{5,13},{6,14},{7,15},{8,0},{9,1},... | collective-permute-start | bytes 884744 | tf_op jit(solution)/shard_map/ppermute | solution.py:170
  35.1 9.5 %collective-permute-done.10.refs_11_ = bf16[3,384,128]{2,1,0:T(8,128)(2,1)S(1)} collective-permute-done((bf16[3,384,128]{2,1,0:T(8,128)(2,1)}, bf16[3,384,128]{2,1,0:T(8,128)(2,1)S(1)}, u32[]{:S(2)}, u32[]{:S(2)}) %collective-permute-start.10) | collective-permute-done | bytes 294944 | tf_op jit(solution)/shard_map/ppermute | solution.py:170
  44.6 0.7 copy-done.5
  45.4 7.7 %collective-permute-start.2 = (bf16[3,384,128]{2,1,0:T(8,128)(2,1)}, bf16[3,384,128]{2,1,0:T(8,128)(2,1)S(1)}, u32[]{:S(2)}, u32[]{:S(2)}) collective-permute-start(bf16[3,384,128]{2,1,0:T(8,128)(2,1)} %get-tuple-element.19), channel_id=1, source_target_pairs={{0,2},{1,3},{2,4},{3,5},{4,6},{5,7},{6,8},{7,9},{8,10},{9,11},{10,... | collective-permute-start | bytes 884744 | tf_op jit(solution)/shard_map/ppermute | solution.py:170
  53.0 0.0 collective-permute-done.11.refs_12_
  53.0 0.7 copy-done.7
  53.8 0.8 collective-permute-start.3
  54.6 23.6 %collective-permute-done.12.refs_13_ = bf16[3,384,128]{2,1,0:T(8,128)(2,1)S(1)} collective-permute-done((bf16[3,384,128]{2,1,0:T(8,128)(2,1)}, bf16[3,384,128]{2,1,0:T(8,128)(2,1)S(1)}, u32[]{:S(2)}, u32[]{:S(2)}) %collective-permute-start.12) | collective-permute-done | bytes 294944 | tf_op jit(solution)/shard_map/ppermute | solution.py:170
  78.2 0.7 copy-done.9
  78.9 0.0 collective-permute-start.4
  78.9 0.1 select_reduce_fusion
  79.1 0.1 select_reduce_fusion.1
  79.2 0.0 collective-permute-done.13.refs_14_
  79.2 2.7 %collective-permute-start.5 = (bf16[3,384,128]{2,1,0:T(8,128)(2,1)S(1)}, bf16[3,384,128]{2,1,0:T(8,128)(2,1)S(1)}, u32[]{:S(2)}, u32[]{:S(2)}) collective-permute-start(bf16[3,384,128]{2,1,0:T(8,128)(2,1)S(1)} %get-tuple-element.16), channel_id=1, source_target_pairs={{0,13},{1,14},{2,15},{3,0},{4,1},{5,2},{6,3},{7,4},{8,5},{9,6},{10... | collective-permute-start | bytes 884744 | tf_op jit(solution)/shard_map/ppermute | solution.py:170
  81.9 16.9 %collective-permute-done.14.refs_15_ = bf16[3,384,128]{2,1,0:T(8,128)(2,1)S(1)} collective-permute-done((bf16[3,384,128]{2,1,0:T(8,128)(2,1)}, bf16[3,384,128]{2,1,0:T(8,128)(2,1)S(1)}, u32[]{:S(2)}, u32[]{:S(2)}) %collective-permute-start.14) | collective-permute-done | bytes 294944 | tf_op jit(solution)/shard_map/ppermute | solution.py:170
  98.8 0.0 collective-permute-start.6
  98.8 25.7 %collective-permute-done.2.refs_3_ = bf16[3,384,128]{2,1,0:T(8,128)(2,1)S(1)} collective-permute-done((bf16[3,384,128]{2,1,0:T(8,128)(2,1)}, bf16[3,384,128]{2,1,0:T(8,128)(2,1)S(1)}, u32[]{:S(2)}, u32[]{:S(2)}) %collective-permute-start.2) | collective-permute-done | bytes 294944 | tf_op jit(solution)/shard_map/ppermute | solution.py:170
  124.5 0.0 collective-permute-start.7
  124.5 0.0 collective-permute-done.3.refs_4_
  124.5 0.0 collective-permute-start.8
  124.5 0.0 collective-permute-done.4.refs_5_
  124.6 3.5 %collective-permute-start.9 = (bf16[3,384,128]{2,1,0:T(8,128)(2,1)S(1)}, bf16[3,384,128]{2,1,0:T(8,128)(2,1)S(1)}, u32[]{:S(2)}, u32[]{:S(2)}) collective-permute-start(bf16[3,384,128]{2,1,0:T(8,128)(2,1)S(1)} %get-tuple-element.12), channel_id=1, source_target_pairs={{0,11},{1,12},{2,13},{3,14},{4,15},{5,0},{6,1},{7,2},{8,3},{9,4},{... | collective-permute-start | bytes 884744 | tf_op jit(solution)/shard_map/ppermute | solution.py:170
  128.1 0.1 pad_add_fusion.places
  128.2 0.0 collective-permute-done.5.refs_6_
  128.2 4.6 %collective-permute-done.6.refs_7_ = bf16[3,384,128]{2,1,0:T(8,128)(2,1)S(1)} collective-permute-done((bf16[3,384,128]{2,1,0:T(8,128)(2,1)S(1)}, bf16[3,384,128]{2,1,0:T(8,128)(2,1)S(1)}, u32[]{:S(2)}, u32[]{:S(2)}) %collective-permute-start.6) | collective-permute-done | bytes 294944 | tf_op jit(solution)/shard_map/ppermute | solution.py:170
  132.8 12.1 %collective-permute-done.7.refs_8_ = bf16[3,384,128]{2,1,0:T(8,128)(2,1)S(1)} collective-permute-done((bf16[3,384,128]{2,1,0:T(8,128)(2,1)S(1)}, bf16[3,384,128]{2,1,0:T(8,128)(2,1)S(1)}, u32[]{:S(2)}, u32[]{:S(2)}) %collective-permute-start.7) | collective-permute-done | bytes 294944 | tf_op jit(solution)/shard_map/ppermute | solution.py:170
  144.9 14.0 %collective-permute-done.8.refs_9_ = bf16[3,384,128]{2,1,0:T(8,128)(2,1)S(1)} collective-permute-done((bf16[3,384,128]{2,1,0:T(8,128)(2,1)S(1)}, bf16[3,384,128]{2,1,0:T(8,128)(2,1)S(1)}, u32[]{:S(2)}, u32[]{:S(2)}) %collective-permute-start.8) | collective-permute-done | bytes 294944 | tf_op jit(solution)/shard_map/ppermute | solution.py:170
  158.9 13.3 %collective-permute-done.9.refs_10_ = bf16[3,384,128]{2,1,0:T(8,128)(2,1)S(1)} collective-permute-done((bf16[3,384,128]{2,1,0:T(8,128)(2,1)S(1)}, bf16[3,384,128]{2,1,0:T(8,128)(2,1)S(1)}, u32[]{:S(2)}, u32[]{:S(2)}) %collective-permute-start.9) | collective-permute-done | bytes 294944 | tf_op jit(solution)/shard_map/ppermute | solution.py:170
  172.2 1.0 copy-done.2
  173.2 1.0 copy-done.4
  174.1 1.0 copy-done.6
  175.1 1.0 copy-done.8
  176.1 1.0 copy-done.10
  177.1 1.8 shard_map.100.tables
  178.9 37.3 %all-gather.3.cloned.1.call-done = bf16[37888,256]{1,0:T(8,128)(2,1)} async-done(((bf16[2368,256]{1,0:T(8,128)(2,1)}), bf16[37888,256]{1,0:T(8,128)(2,1)}) %all-gather.3.cloned.1.call-update) | async-done | bytes 19398672 | tf_op jit(solution)/shard_map/all_gather | solution.py:160
  216.2 12.4 %shard_map.101 = bf16[384,1024]{1,0:T(8,128)(2,1)S(1)} custom-call(bf16[384,4096]{1,0:T(8,128)(2,1)S(1)} %shard_map.100.tables, bf16[16,2368,256]{2,1,0:T(8,128)(2,1)} %bitcast.92, f32[2,4096]{1,0:T(2,128)S(1)} %bitcast_convert_fusion.bias, f32[1,256]{1,0:T(1,128)S(1)} %convert_element_type.34.comp_bias), custom_call_target="tpu_custom_call" | custom-call | flops 8000000000 | bytes 24000000 | tf_op jit(solution)/shard_map/pallas_call | solution.py:197
  228.5 0.9 copy-done
  229.4 7.2 %all-to-all-start = ((bf16[16,24,1024]{2,1,0:T(8,128)(2,1)}), bf16[16,24,1024]{2,1,0:T(8,128)(2,1)S(1)}, u32[]{:S(2)}, u32[]{:S(2)}) async-start(bf16[16,24,1024]{2,1,0:T(8,128)(2,1)} %bitcast.87), calls=%async_computation | async-start | bytes 1572864 | tf_op jit(solution)/shard_map/all_to_all | solution.py:220
  236.6 15.0 %all-to-all-done = bf16[16,24,1024]{2,1,0:T(8,128)(2,1)S(1)} async-done(((bf16[16,24,1024]{2,1,0:T(8,128)(2,1)}), bf16[16,24,1024]{2,1,0:T(8,128)(2,1)S(1)}, u32[]{:S(2)}, u32[]{:S(2)}) %all-to-all-start) | async-done | bytes 786464 | tf_op jit(solution)/shard_map/all_to_all | solution.py:220
  251.6 0.1 convert_reduce_fusion
  251.8 0.6 fusion.3
  (32 shorter events, 0.1 us)
Async XLA Ops:
  6.5 2.0 copy-start.12
  6.5 2.1 copy-start.13
  6.5 2.1 copy-start.14
  6.5 209.6 %all-gather.3.cloned.1.call-start = ((), (), s32[]{:S(2)}) async-start(), calls=%async_computation.1 | async-start | bytes 20611072 | tf_op jit(solution)/shard_map/all_gather | solution.py:160
  8.7 1.0 copy-start.11
  9.9 13.9 %copy-start.18 = (s32[512]{0:T(512)S(1)}, s32[512]{0:T(512)}, u32[]{:S(2)}) copy-start(s32[512]{0:T(512)} %param.18) | copy-start | bytes 6148
  9.9 13.9 %copy-start.16 = (bf16[1,2,4096]{2,1,0:T(2,128)(2,1)S(1)}, bf16[1,2,4096]{2,1,0:T(2,128)(2,1)}, u32[]{:S(2)}) copy-start(bf16[1,2,4096]{2,1,0:T(2,128)(2,1)} %param.13) | copy-start | bytes 49156
  10.0 13.9 %copy-start.15 = (s32[512]{0:T(512)S(1)}, s32[512]{0:T(512)}, u32[]{:S(2)}) copy-start(s32[512]{0:T(512)} %param.19) | copy-start | bytes 6148
  10.0 14.2 %copy-start.19 = (bf16[1,256]{1,0:T(2,128)(2,1)S(1)}, bf16[1,256]{1,0:T(2,128)(2,1)}, u32[]{:S(2)}) copy-start(bf16[1,256]{1,0:T(2,128)(2,1)} %param.15) | copy-start | bytes 1540
  14.5 9.6 %collective-permute-start = (bf16[3,384,128]{2,1,0:T(8,128)(2,1)}, bf16[3,384,128]{2,1,0:T(8,128)(2,1)S(1)}, u32[]{:S(2)}, u32[]{:S(2)}) collective-permute-start(bf16[3,384,128]{2,1,0:T(8,128)(2,1)} %get-tuple-element.21), channel_id=1, source_target_pairs={{0,1},{1,2},{2,3},{3,4},{4,5},{5,6},{6,7},{7,8},{8,9},{9,10},{10,1... | collective-permute-start | bytes 884744 | tf_op jit(solution)/shard_map/ppermute | solution.py:170
  14.5 12.5 %collective-permute-start.1 = (bf16[3,384,128]{2,1,0:T(8,128)(2,1)}, bf16[3,384,128]{2,1,0:T(8,128)(2,1)S(1)}, u32[]{:S(2)}, u32[]{:S(2)}) collective-permute-start(bf16[3,384,128]{2,1,0:T(8,128)(2,1)} %get-tuple-element.20), channel_id=1, source_target_pairs={{0,15},{1,0},{2,1},{3,2},{4,3},{5,4},{6,5},{7,6},{8,7},{9,8},{10,9... | collective-permute-start | bytes 884744 | tf_op jit(solution)/shard_map/ppermute | solution.py:170
  16.3 28.4 %collective-permute-start.10 = (bf16[3,384,128]{2,1,0:T(8,128)(2,1)}, bf16[3,384,128]{2,1,0:T(8,128)(2,1)S(1)}, u32[]{:S(2)}, u32[]{:S(2)}) collective-permute-start(bf16[3,384,128]{2,1,0:T(8,128)(2,1)} %get-tuple-element.11), channel_id=1, source_target_pairs={{0,6},{1,7},{2,8},{3,9},{4,10},{5,11},{6,12},{7,13},{8,14},{9,15},... | collective-permute-start | bytes 884744 | tf_op jit(solution)/shard_map/ppermute | solution.py:170
  20.3 32.7 %collective-permute-start.11 = (bf16[3,384,128]{2,1,0:T(8,128)(2,1)}, bf16[3,384,128]{2,1,0:T(8,128)(2,1)S(1)}, u32[]{:S(2)}, u32[]{:S(2)}) collective-permute-start(bf16[3,384,128]{2,1,0:T(8,128)(2,1)} %get-tuple-element.10), channel_id=1, source_target_pairs={{0,10},{1,11},{2,12},{3,13},{4,14},{5,15},{6,0},{7,1},{8,2},{9,3},... | collective-permute-start | bytes 884744 | tf_op jit(solution)/shard_map/ppermute | solution.py:170
  20.3 57.9 %collective-permute-start.12 = (bf16[3,384,128]{2,1,0:T(8,128)(2,1)}, bf16[3,384,128]{2,1,0:T(8,128)(2,1)S(1)}, u32[]{:S(2)}, u32[]{:S(2)}) collective-permute-start(bf16[3,384,128]{2,1,0:T(8,128)(2,1)} %get-tuple-element.9), channel_id=1, source_target_pairs={{0,7},{1,8},{2,9},{3,10},{4,11},{5,12},{6,13},{7,14},{8,15},{9,0},... | collective-permute-start | bytes 884744 | tf_op jit(solution)/shard_map/ppermute | solution.py:170
  24.2 0.7 copy-start.1
  24.9 54.3 %collective-permute-start.13 = (bf16[3,384,128]{2,1,0:T(8,128)(2,1)}, bf16[3,384,128]{2,1,0:T(8,128)(2,1)S(1)}, u32[]{:S(2)}, u32[]{:S(2)}) collective-permute-start(bf16[3,384,128]{2,1,0:T(8,128)(2,1)} %get-tuple-element.8), channel_id=1, source_target_pairs={{0,9},{1,10},{2,11},{3,12},{4,13},{5,14},{6,15},{7,0},{8,1},{9,2},... | collective-permute-start | bytes 884744 | tf_op jit(solution)/shard_map/ppermute | solution.py:170
  27.1 0.7 copy-start.3
  27.8 71.0 %collective-permute-start.14 = (bf16[3,384,128]{2,1,0:T(8,128)(2,1)}, bf16[3,384,128]{2,1,0:T(8,128)(2,1)S(1)}, u32[]{:S(2)}, u32[]{:S(2)}) collective-permute-start(bf16[3,384,128]{2,1,0:T(8,128)(2,1)} %get-tuple-element.7), channel_id=1, source_target_pairs={{0,8},{1,9},{2,10},{3,11},{4,12},{5,13},{6,14},{7,15},{8,0},{9,1},... | collective-permute-start | bytes 884744 | tf_op jit(solution)/shard_map/ppermute | solution.py:170
  44.6 0.7 copy-start.5
  45.4 79.2 %collective-permute-start.2 = (bf16[3,384,128]{2,1,0:T(8,128)(2,1)}, bf16[3,384,128]{2,1,0:T(8,128)(2,1)S(1)}, u32[]{:S(2)}, u32[]{:S(2)}) collective-permute-start(bf16[3,384,128]{2,1,0:T(8,128)(2,1)} %get-tuple-element.19), channel_id=1, source_target_pairs={{0,2},{1,3},{2,4},{3,5},{4,6},{5,7},{6,8},{7,9},{8,10},{9,11},{10,... | collective-permute-start | bytes 884744 | tf_op jit(solution)/shard_map/ppermute | solution.py:170
  53.0 0.7 copy-start.7
  53.8 70.8 %collective-permute-start.3 = (bf16[3,384,128]{2,1,0:T(8,128)(2,1)}, bf16[3,384,128]{2,1,0:T(8,128)(2,1)S(1)}, u32[]{:S(2)}, u32[]{:S(2)}) collective-permute-start(bf16[3,384,128]{2,1,0:T(8,128)(2,1)} %get-tuple-element.18), channel_id=1, source_target_pairs={{0,14},{1,15},{2,0},{3,1},{4,2},{5,3},{6,4},{7,5},{8,6},{9,7},{10,... | collective-permute-start | bytes 884744 | tf_op jit(solution)/shard_map/ppermute | solution.py:170
  78.2 0.7 copy-start.9
  78.9 45.6 %collective-permute-start.4 = (bf16[3,384,128]{2,1,0:T(8,128)(2,1)}, bf16[3,384,128]{2,1,0:T(8,128)(2,1)S(1)}, u32[]{:S(2)}, u32[]{:S(2)}) collective-permute-start(bf16[3,384,128]{2,1,0:T(8,128)(2,1)} %get-tuple-element.17), channel_id=1, source_target_pairs={{0,3},{1,4},{2,5},{3,6},{4,7},{5,8},{6,9},{7,10},{8,11},{9,12},{10... | collective-permute-start | bytes 884744 | tf_op jit(solution)/shard_map/ppermute | solution.py:170
  79.2 49.0 %collective-permute-start.5 = (bf16[3,384,128]{2,1,0:T(8,128)(2,1)S(1)}, bf16[3,384,128]{2,1,0:T(8,128)(2,1)S(1)}, u32[]{:S(2)}, u32[]{:S(2)}) collective-permute-start(bf16[3,384,128]{2,1,0:T(8,128)(2,1)S(1)} %get-tuple-element.16), channel_id=1, source_target_pairs={{0,13},{1,14},{2,15},{3,0},{4,1},{5,2},{6,3},{7,4},{8,5},{9,6},{10... | collective-permute-start | bytes 884744 | tf_op jit(solution)/shard_map/ppermute | solution.py:170
  98.8 34.0 %collective-permute-start.6 = (bf16[3,384,128]{2,1,0:T(8,128)(2,1)S(1)}, bf16[3,384,128]{2,1,0:T(8,128)(2,1)S(1)}, u32[]{:S(2)}, u32[]{:S(2)}) collective-permute-start(bf16[3,384,128]{2,1,0:T(8,128)(2,1)S(1)} %get-tuple-element.15), channel_id=1, source_target_pairs={{0,4},{1,5},{2,6},{3,7},{4,8},{5,9},{6,10},{7,11},{8,12},{9,13},{1... | collective-permute-start | bytes 884744 | tf_op jit(solution)/shard_map/ppermute | solution.py:170
  124.5 20.4 %collective-permute-start.7 = (bf16[3,384,128]{2,1,0:T(8,128)(2,1)S(1)}, bf16[3,384,128]{2,1,0:T(8,128)(2,1)S(1)}, u32[]{:S(2)}, u32[]{:S(2)}) collective-permute-start(bf16[3,384,128]{2,1,0:T(8,128)(2,1)S(1)} %get-tuple-element.14), channel_id=1, source_target_pairs={{0,12},{1,13},{2,14},{3,15},{4,0},{5,1},{6,2},{7,3},{8,4},{9,5},{1... | collective-permute-start | bytes 884744 | tf_op jit(solution)/shard_map/ppermute | solution.py:170
  124.5 34.4 %collective-permute-start.8 = (bf16[3,384,128]{2,1,0:T(8,128)(2,1)S(1)}, bf16[3,384,128]{2,1,0:T(8,128)(2,1)S(1)}, u32[]{:S(2)}, u32[]{:S(2)}) collective-permute-start(bf16[3,384,128]{2,1,0:T(8,128)(2,1)S(1)} %get-tuple-element.13), channel_id=1, source_target_pairs={{0,5},{1,6},{2,7},{3,8},{4,9},{5,10},{6,11},{7,12},{8,13},{9,14},{... | collective-permute-start | bytes 884744 | tf_op jit(solution)/shard_map/ppermute | solution.py:170
  124.6 47.7 %collective-permute-start.9 = (bf16[3,384,128]{2,1,0:T(8,128)(2,1)S(1)}, bf16[3,384,128]{2,1,0:T(8,128)(2,1)S(1)}, u32[]{:S(2)}, u32[]{:S(2)}) collective-permute-start(bf16[3,384,128]{2,1,0:T(8,128)(2,1)S(1)} %get-tuple-element.12), channel_id=1, source_target_pairs={{0,11},{1,12},{2,13},{3,14},{4,15},{5,0},{6,1},{7,2},{8,3},{9,4},{... | collective-permute-start | bytes 884744 | tf_op jit(solution)/shard_map/ppermute | solution.py:170
  172.2 1.0 copy-start.2
  173.2 1.0 copy-start.4
  174.1 1.0 copy-start.6
  175.1 1.0 copy-start.8
  176.1 1.0 copy-start.10
  228.5 0.9 copy-start
  229.4 7.2 %copy-start.17 = (bf16[1024]{0:T(1024)(128)(2,1)S(1)}, bf16[1024]{0:T(1024)(128)(2,1)}, u32[]{:S(2)}) copy-start(bf16[1024]{0:T(1024)(128)(2,1)} %param.17) | copy-start | bytes 6148
  229.4 22.2 %all-to-all-start = ((bf16[16,24,1024]{2,1,0:T(8,128)(2,1)}), bf16[16,24,1024]{2,1,0:T(8,128)(2,1)S(1)}, u32[]{:S(2)}, u32[]{:S(2)}) async-start(bf16[16,24,1024]{2,1,0:T(8,128)(2,1)} %bitcast.87), calls=%async_computation | async-start | bytes 1572864 | tf_op jit(solution)/shard_map/all_to_all | solution.py:220
Sparse Core Ops, SparseCore 0:
  9.8 206.2 all-gather.2

commit v7 on v6

--- a/solution.py
+++ b/solution.py
@@ -27,6 +27,20 @@
 
 QUARTERS = 4
 BACK = (0, 1, 15, 2, 14, 3, 13, 4, 12, 5, 11, 6, 10, 7, 9, 8)
+
+
+def pack_kernel(down, up, comp, over, out, sems):
+    half = out.shape[1]
+    sources = [down.at[:, pl.ds(0, half)], down.at[:, pl.ds(half, half)], up, comp, over]
+    copies, first = [], 0
+    for n, source in enumerate(sources):
+        count = source.shape[0]
+        copies.append(pltpu.make_async_copy(source, out.at[pl.ds(first, count), :], sems.at[n]))
+        first += count
+    for copy in copies:
+        copy.start()
+    for copy in copies:
+        copy.wait()
 
 
 def table_kernel(places, *refs):
@@ -147,16 +161,20 @@
     columns = over_weight.shape[1]
     outputs = columns * shards
 
-    down = cross_down[0].reshape(layers * step, rank)
-    packed = jnp.concatenate(
-        [
-            down[:, : rank // 2],
-            down[:, rank // 2 :],
-            cross_up[0].reshape(layers * rank, step),
-            comp_weight[0],
-            over_weight.T,
-        ]
-    )
+    parts = (
+        cross_down[0].reshape(layers * step, rank),
+        cross_up[0].reshape(layers * rank, step),
+        comp_weight[0],
+        over_weight.T,
+    )
+    packed = pl.pallas_call(
+        pack_kernel,
+        in_specs=[pl.BlockSpec(memory_space=pl.ANY)] * len(parts),
+        out_specs=pl.BlockSpec(memory_space=pl.ANY),
+        scratch_shapes=[pltpu.SemaphoreType.DMA((len(parts) + 1,))],
+        out_shape=jax.ShapeDtypeStruct((sum(p.size for p in parts) // step, step), BF16),
+        compiler_params=pltpu.CompilerParams(vmem_limit_bytes=58 * 2**20),
+    )(*parts)
     weights = lax.all_gather(packed, "shard", axis=0)
 
     by_slot = pooled[0].transpose(1, 0, 2).reshape(slot_most, shards, samples, emb)
@@ -213,7 +231,7 @@
             ],
         ),
         out_shape=jax.ShapeDtypeStruct((samples, outputs), BF16),
-        compiler_params=pltpu.CompilerParams(vmem_limit_bytes=36 * 2**20),
+        compiler_params=pltpu.CompilerParams(vmem_limit_bytes=58 * 2**20),
         cost_estimate=pl.CostEstimate(flops=8 * 10**9, bytes_accessed=24 * 10**6, transcendentals=0),
     )(tables, weights, cross_bias[0].astype(F32), comp_bias.astype(F32))
 

time: 260 us -> 295 us (1.13)
  Pallas kernels: 14.2 us -> 54.2 us
  local copies, waits for them, and re-layouts: 17 us -> 6.11 us
  waiting for transfers between devices: 172 us -> 178 us
    pallas_call x0 -> x1, Pallas kernels: none -> 37.9 us  [on_device(): pl.pallas_call(pack_kernel, in_specs=[pl.BlockSpec(memory_space=pl.ANY)]...]
    unnamed x44 -> x10, local copies, waits for them, and re-layouts: 12.4 us -> 1.7 us
    all_gather x1, waiting for transfers between devices: 37.3 us -> 40.6 us  [on_device(): weights = lax.all_gather(packed, 'shard', axis=0)]
where the time goes in v7:
time: 295 us
  waiting for transfers between devices  178 us (60%)
  Pallas kernels  54.2 us (18%)
  starting transfers between devices  40 us (14%)
  between operations  13.7 us (5%)
  local copies, waits for them, and re-layouts  6.11 us (2%)
  other arithmetic  3.3 us (1%)
    ppermute x15, waiting for transfers between devices, on_device(): pieces.append(lax.ppermute(piece_for(shard + k), 'shard', moves))  122 us
    all_gather x1, waiting for transfers between devices, on_device(): weights = lax.all_gather(packed, 'shard', axis=0)  40.6 us
    pallas_call x1, Pallas kernels, on_device(): pl.pallas_call(pack_kernel, in_specs=[pl.BlockSpec(memory_space=pl.ANY)]...  37.9 us
    ppermute x15, starting transfers between devices, on_device(): pieces.append(lax.ppermute(piece_for(shard + k), 'shard', moves))  32.9 us
    all_to_all x1, waiting for transfers between devices, on_device(): lax.all_to_all(partial.reshape(towers, samples // towers, outputs), 'towe...  15 us
    pallas_call x1, Pallas kernels, on_device(): pl.pallas_call(tower_kernel, grid_spec=pl.GridSpec(grid=(1,), in_specs=[a...  14.5 us
    all_to_all x1, starting transfers between devices, on_device(): lax.all_to_all(partial.reshape(towers, samples // towers, outputs), 'towe...  7.03 us
  transfers between devices with their start and end apart: 17, of which 10 were waited for; matrix products, arithmetic and copies ran while one was open for 2% of the time, Pallas kernels for 1%

profile of v7, /device:TPU:96, one launch (start us, length us, event | category | flops | bytes accessed | tf_op | source)
XLA Modules:
  0.0 294.9 jit_solution(17647834659137494808)
XLA Ops:
  6.5 0.0 all-gather.3.cloned.1.call-start
  6.5 37.9 %shard_map.101 = bf16[2368,256]{1,0:T(8,128)(2,1)} custom-call(bf16[512,512]{1,0:T(8,128)(2,1)} %bitcast.87, bf16[1024,256]{1,0:T(8,128)(2,1)} %bitcast.88, bf16[256,256]{1,0:T(8,128)(2,1)} %bitcast.89, bf16[64,256]{1,0:T(8,128)(2,1)} %bitcast.90), custom_call_target="tpu_custom_call" | custom-call | tf_op jit(solution)/shard_map/pallas_call | solution.py:170
  44.4 0.0 all-gather.3.cloned.1.call-update
  44.7 0.0 copy-start.3
  44.7 0.0 copy-start.1
  44.7 0.0 copy-start.4
  44.7 4.4 %dynamic-slice_bitcast_fusion = (bf16[3,384,128]{2,1,0:T(8,128)(2,1)}, bf16[3,384,128]{2,1,0:T(8,128)(2,1)}, bf16[3,384,128]{2,1,0:T(8,128)(2,1)}, bf16[3,384,12...) fusion(bf16[3,16,384,128]{3,2,1,0:T(8,128)(2,1)} %bitcast.85, ...), kind=kLoop, calls=%fused_computation.6 | loop fusion | bytes 9437248 | tf_op jit(solution)/shard_map/jit(dynamic_index_in_dim)/squeeze | solution.py:183
  49.1 0.0 collective-permute-start
  49.1 1.7 collective-permute-start.1
  50.9 4.0 %collective-permute-start.10 = (bf16[3,384,128]{2,1,0:T(8,128)(2,1)}, bf16[3,384,128]{2,1,0:T(8,128)(2,1)S(1)}, u32[]{:S(2)}, u32[]{:S(2)}) collective-permute-start(bf16[3,384,128]{2,1,0:T(8,128)(2,1)} %get-tuple-element.11), channel_id=1, source_target_pairs={{0,6},{1,7},{2,8},{3,9},{4,10},{5,11},{6,12},{7,13},{8,14},{9,15},... | collective-permute-start | bytes 884744 | tf_op jit(solution)/shard_map/ppermute | solution.py:188
  54.9 0.0 collective-permute-start.11
  54.9 3.5 %collective-permute-start.12 = (bf16[3,384,128]{2,1,0:T(8,128)(2,1)}, bf16[3,384,128]{2,1,0:T(8,128)(2,1)S(1)}, u32[]{:S(2)}, u32[]{:S(2)}) collective-permute-start(bf16[3,384,128]{2,1,0:T(8,128)(2,1)} %get-tuple-element.9), channel_id=1, source_target_pairs={{0,7},{1,8},{2,9},{3,10},{4,11},{5,12},{6,13},{7,14},{8,15},{9,0},... | collective-permute-start | bytes 884744 | tf_op jit(solution)/shard_map/ppermute | solution.py:188
  58.4 0.0 copy-done.3
  58.4 1.3 bitcast_convert_fusion.bias
  59.7 0.0 copy-done.1
  59.7 0.3 convert_reduce_fusion.2
  60.0 0.0 copy-done.4
  60.0 0.6 convert_element_type.34.comp_bias
  60.6 0.0 collective-permute-done.refs_1_
  60.6 2.2 collective-permute-start.13
  62.8 0.0 collective-permute-done.1.refs_2_
  62.8 5.6 %collective-permute-start.14 = (bf16[3,384,128]{2,1,0:T(8,128)(2,1)}, bf16[3,384,128]{2,1,0:T(8,128)(2,1)S(1)}, u32[]{:S(2)}, u32[]{:S(2)}) collective-permute-start(bf16[3,384,128]{2,1,0:T(8,128)(2,1)} %get-tuple-element.7), channel_id=1, source_target_pairs={{0,8},{1,9},{2,10},{3,11},{4,12},{5,13},{6,14},{7,15},{8,0},{9,1},... | collective-permute-start | bytes 884744 | tf_op jit(solution)/shard_map/ppermute | solution.py:188
  68.4 10.8 %collective-permute-done.10.refs_11_ = bf16[3,384,128]{2,1,0:T(8,128)(2,1)S(1)} collective-permute-done((bf16[3,384,128]{2,1,0:T(8,128)(2,1)}, bf16[3,384,128]{2,1,0:T(8,128)(2,1)S(1)}, u32[]{:S(2)}, u32[]{:S(2)}) %collective-permute-start.10) | collective-permute-done | bytes 294944 | tf_op jit(solution)/shard_map/ppermute | solution.py:188
  79.2 7.7 %collective-permute-start.2 = (bf16[3,384,128]{2,1,0:T(8,128)(2,1)}, bf16[3,384,128]{2,1,0:T(8,128)(2,1)S(1)}, u32[]{:S(2)}, u32[]{:S(2)}) collective-permute-start(bf16[3,384,128]{2,1,0:T(8,128)(2,1)} %get-tuple-element.19), channel_id=1, source_target_pairs={{0,2},{1,3},{2,4},{3,5},{4,6},{5,7},{6,8},{7,9},{8,10},{9,11},{10,... | collective-permute-start | bytes 884744 | tf_op jit(solution)/shard_map/ppermute | solution.py:188
  86.9 0.0 collective-permute-done.11.refs_12_
  86.9 1.9 collective-permute-start.3
  88.9 24.3 %collective-permute-done.12.refs_13_ = bf16[3,384,128]{2,1,0:T(8,128)(2,1)S(1)} collective-permute-done((bf16[3,384,128]{2,1,0:T(8,128)(2,1)}, bf16[3,384,128]{2,1,0:T(8,128)(2,1)S(1)}, u32[]{:S(2)}, u32[]{:S(2)}) %collective-permute-start.12) | collective-permute-done | bytes 294944 | tf_op jit(solution)/shard_map/ppermute | solution.py:188
  113.2 0.0 collective-permute-start.4
  113.2 0.1 select_reduce_fusion
  113.3 0.1 select_reduce_fusion.1
  113.4 0.0 collective-permute-done.13.refs_14_
  113.4 2.7 collective-permute-start.5
  116.1 17.1 %collective-permute-done.14.refs_15_ = bf16[3,384,128]{2,1,0:T(8,128)(2,1)S(1)} collective-permute-done((bf16[3,384,128]{2,1,0:T(8,128)(2,1)}, bf16[3,384,128]{2,1,0:T(8,128)(2,1)S(1)}, u32[]{:S(2)}, u32[]{:S(2)}) %collective-permute-start.14) | collective-permute-done | bytes 294944 | tf_op jit(solution)/shard_map/ppermute | solution.py:188
  133.2 0.0 collective-permute-start.6
  133.2 26.0 %collective-permute-done.2.refs_3_ = bf16[3,384,128]{2,1,0:T(8,128)(2,1)S(1)} collective-permute-done((bf16[3,384,128]{2,1,0:T(8,128)(2,1)}, bf16[3,384,128]{2,1,0:T(8,128)(2,1)S(1)}, u32[]{:S(2)}, u32[]{:S(2)}) %collective-permute-start.2) | collective-permute-done | bytes 294944 | tf_op jit(solution)/shard_map/ppermute | solution.py:188
  159.1 0.0 collective-permute-start.7
  159.2 0.0 collective-permute-done.3.refs_4_
  159.2 0.0 collective-permute-start.8
  159.2 0.0 collective-permute-done.4.refs_5_
  159.2 3.5 %collective-permute-start.9 = (bf16[3,384,128]{2,1,0:T(8,128)(2,1)S(1)}, bf16[3,384,128]{2,1,0:T(8,128)(2,1)S(1)}, u32[]{:S(2)}, u32[]{:S(2)}) collective-permute-start(bf16[3,384,128]{2,1,0:T(8,128)(2,1)S(1)} %get-tuple-element.12), channel_id=1, source_target_pairs={{0,11},{1,12},{2,13},{3,14},{4,15},{5,0},{6,1},{7,2},{8,3},{9,4},{... | collective-permute-start | bytes 884744 | tf_op jit(solution)/shard_map/ppermute | solution.py:188
  162.7 0.1 pad_add_fusion.places
  162.8 0.0 collective-permute-done.5.refs_6_
  162.8 4.5 %collective-permute-done.6.refs_7_ = bf16[3,384,128]{2,1,0:T(8,128)(2,1)S(1)} collective-permute-done((bf16[3,384,128]{2,1,0:T(8,128)(2,1)S(1)}, bf16[3,384,128]{2,1,0:T(8,128)(2,1)S(1)}, u32[]{:S(2)}, u32[]{:S(2)}) %collective-permute-start.6) | collective-permute-done | bytes 294944 | tf_op jit(solution)/shard_map/ppermute | solution.py:188
  167.3 12.2 %collective-permute-done.7.refs_8_ = bf16[3,384,128]{2,1,0:T(8,128)(2,1)S(1)} collective-permute-done((bf16[3,384,128]{2,1,0:T(8,128)(2,1)S(1)}, bf16[3,384,128]{2,1,0:T(8,128)(2,1)S(1)}, u32[]{:S(2)}, u32[]{:S(2)}) %collective-permute-start.7) | collective-permute-done | bytes 294944 | tf_op jit(solution)/shard_map/ppermute | solution.py:188
  179.5 13.9 %collective-permute-done.8.refs_9_ = bf16[3,384,128]{2,1,0:T(8,128)(2,1)S(1)} collective-permute-done((bf16[3,384,128]{2,1,0:T(8,128)(2,1)S(1)}, bf16[3,384,128]{2,1,0:T(8,128)(2,1)S(1)}, u32[]{:S(2)}, u32[]{:S(2)}) %collective-permute-start.8) | collective-permute-done | bytes 294944 | tf_op jit(solution)/shard_map/ppermute | solution.py:188
  193.4 13.2 %collective-permute-done.9.refs_10_ = bf16[3,384,128]{2,1,0:T(8,128)(2,1)S(1)} collective-permute-done((bf16[3,384,128]{2,1,0:T(8,128)(2,1)S(1)}, bf16[3,384,128]{2,1,0:T(8,128)(2,1)S(1)}, u32[]{:S(2)}, u32[]{:S(2)}) %collective-permute-start.9) | collective-permute-done | bytes 294944 | tf_op jit(solution)/shard_map/ppermute | solution.py:188
  206.6 1.8 shard_map.100.tables
  208.4 0.0 copy-start
  208.4 1.7 copy-done
  210.1 40.6 %all-gather.3.cloned.1.call-done = bf16[37888,256]{1,0:T(8,128)(2,1)} async-done(((bf16[2368,256]{1,0:T(8,128)(2,1)}), bf16[37888,256]{1,0:T(8,128)(2,1)}) %all-gather.3.cloned.1.call-update) | async-done | bytes 19398672 | tf_op jit(solution)/shard_map/all_gather | solution.py:178
  250.7 0.0 copy-start.2
  250.7 14.5 %shard_map.102 = bf16[384,1024]{1,0:T(8,128)(2,1)} custom-call(bf16[384,4096]{1,0:T(8,128)(2,1)} %copy-done, bf16[16,2368,256]{2,1,0:T(8,128)(2,1)} %bitcast.91, f32[2,4096]{1,0:T(2,128)} %bitcast_convert_fusion.bias, f32[1,256]{1,0:T(1,128)} %convert_element_type.34.comp_bias), custom_call_target="tpu_custom_call" | custom-call | flops 8000000000 | bytes 24000000 | tf_op jit(solution)/shard_map/pallas_call | solution.py:215
  265.2 7.0 %all-to-all-start = ((bf16[16,24,1024]{2,1,0:T(8,128)(2,1)}), bf16[16,24,1024]{2,1,0:T(8,128)(2,1)S(1)}, u32[]{:S(2)}, u32[]{:S(2)}) async-start(bf16[16,24,1024]{2,1,0:T(8,128)(2,1)} %bitcast.86), calls=%async_computation | async-start | bytes 1572864 | tf_op jit(solution)/shard_map/all_to_all | solution.py:238
  272.3 0.0 copy-done.2
  272.3 15.0 %all-to-all-done = bf16[16,24,1024]{2,1,0:T(8,128)(2,1)S(1)} async-done(((bf16[16,24,1024]{2,1,0:T(8,128)(2,1)}), bf16[16,24,1024]{2,1,0:T(8,128)(2,1)S(1)}, u32[]{:S(2)}, u32[]{:S(2)}) %all-to-all-start) | async-done | bytes 786464 | tf_op jit(solution)/shard_map/all_to_all | solution.py:238
  287.3 0.1 convert_reduce_fusion
  287.4 0.6 fusion.3
  (5 shorter events, 0.0 us)
Async XLA Ops:
  6.5 244.2 %all-gather.3.cloned.1.call-start = ((), (), s32[]{:S(2)}) async-start(), calls=%async_computation.1 | async-start | bytes 20611072 | tf_op jit(solution)/shard_map/all_gather | solution.py:178
  44.7 13.7 %copy-start.3 = (s32[512]{0:T(512)S(1)}, s32[512]{0:T(512)}, u32[]{:S(2)}) copy-start(s32[512]{0:T(512)} %param.18) | copy-start | bytes 6148
  44.7 15.1 %copy-start.1 = (s32[512]{0:T(512)S(1)}, s32[512]{0:T(512)}, u32[]{:S(2)}) copy-start(s32[512]{0:T(512)} %param.19) | copy-start | bytes 6148
  44.7 15.3 %copy-start.4 = (bf16[1,256]{1,0:T(2,128)(2,1)S(1)}, bf16[1,256]{1,0:T(2,128)(2,1)}, u32[]{:S(2)}) copy-start(bf16[1,256]{1,0:T(2,128)(2,1)} %param.15) | copy-start | bytes 1540
  49.1 11.5 %collective-permute-start = (bf16[3,384,128]{2,1,0:T(8,128)(2,1)}, bf16[3,384,128]{2,1,0:T(8,128)(2,1)S(1)}, u32[]{:S(2)}, u32[]{:S(2)}) collective-permute-start(bf16[3,384,128]{2,1,0:T(8,128)(2,1)} %get-tuple-element.21), channel_id=1, source_target_pairs={{0,1},{1,2},{2,3},{3,4},{4,5},{5,6},{6,7},{7,8},{8,9},{9,10},{10,1... | collective-permute-start | bytes 884744 | tf_op jit(solution)/shard_map/ppermute | solution.py:188
  49.1 13.7 %collective-permute-start.1 = (bf16[3,384,128]{2,1,0:T(8,128)(2,1)}, bf16[3,384,128]{2,1,0:T(8,128)(2,1)S(1)}, u32[]{:S(2)}, u32[]{:S(2)}) collective-permute-start(bf16[3,384,128]{2,1,0:T(8,128)(2,1)} %get-tuple-element.20), channel_id=1, source_target_pairs={{0,15},{1,0},{2,1},{3,2},{4,3},{5,4},{6,5},{7,6},{8,7},{9,8},{10,9... | collective-permute-start | bytes 884744 | tf_op jit(solution)/shard_map/ppermute | solution.py:188
  50.9 28.3 %collective-permute-start.10 = (bf16[3,384,128]{2,1,0:T(8,128)(2,1)}, bf16[3,384,128]{2,1,0:T(8,128)(2,1)S(1)}, u32[]{:S(2)}, u32[]{:S(2)}) collective-permute-start(bf16[3,384,128]{2,1,0:T(8,128)(2,1)} %get-tuple-element.11), channel_id=1, source_target_pairs={{0,6},{1,7},{2,8},{3,9},{4,10},{5,11},{6,12},{7,13},{8,14},{9,15},... | collective-permute-start | bytes 884744 | tf_op jit(solution)/shard_map/ppermute | solution.py:188
  54.9 32.0 %collective-permute-start.11 = (bf16[3,384,128]{2,1,0:T(8,128)(2,1)}, bf16[3,384,128]{2,1,0:T(8,128)(2,1)S(1)}, u32[]{:S(2)}, u32[]{:S(2)}) collective-permute-start(bf16[3,384,128]{2,1,0:T(8,128)(2,1)} %get-tuple-element.10), channel_id=1, source_target_pairs={{0,10},{1,11},{2,12},{3,13},{4,14},{5,15},{6,0},{7,1},{8,2},{9,3},... | collective-permute-start | bytes 884744 | tf_op jit(solution)/shard_map/ppermute | solution.py:188
  54.9 58.3 %collective-permute-start.12 = (bf16[3,384,128]{2,1,0:T(8,128)(2,1)}, bf16[3,384,128]{2,1,0:T(8,128)(2,1)S(1)}, u32[]{:S(2)}, u32[]{:S(2)}) collective-permute-start(bf16[3,384,128]{2,1,0:T(8,128)(2,1)} %get-tuple-element.9), channel_id=1, source_target_pairs={{0,7},{1,8},{2,9},{3,10},{4,11},{5,12},{6,13},{7,14},{8,15},{9,0},... | collective-permute-start | bytes 884744 | tf_op jit(solution)/shard_map/ppermute | solution.py:188
  60.6 52.8 %collective-permute-start.13 = (bf16[3,384,128]{2,1,0:T(8,128)(2,1)}, bf16[3,384,128]{2,1,0:T(8,128)(2,1)S(1)}, u32[]{:S(2)}, u32[]{:S(2)}) collective-permute-start(bf16[3,384,128]{2,1,0:T(8,128)(2,1)} %get-tuple-element.8), channel_id=1, source_target_pairs={{0,9},{1,10},{2,11},{3,12},{4,13},{5,14},{6,15},{7,0},{8,1},{9,2},... | collective-permute-start | bytes 884744 | tf_op jit(solution)/shard_map/ppermute | solution.py:188
  62.8 70.4 %collective-permute-start.14 = (bf16[3,384,128]{2,1,0:T(8,128)(2,1)}, bf16[3,384,128]{2,1,0:T(8,128)(2,1)S(1)}, u32[]{:S(2)}, u32[]{:S(2)}) collective-permute-start(bf16[3,384,128]{2,1,0:T(8,128)(2,1)} %get-tuple-element.7), channel_id=1, source_target_pairs={{0,8},{1,9},{2,10},{3,11},{4,12},{5,13},{6,14},{7,15},{8,0},{9,1},... | collective-permute-start | bytes 884744 | tf_op jit(solution)/shard_map/ppermute | solution.py:188
  79.2 80.0 %collective-permute-start.2 = (bf16[3,384,128]{2,1,0:T(8,128)(2,1)}, bf16[3,384,128]{2,1,0:T(8,128)(2,1)S(1)}, u32[]{:S(2)}, u32[]{:S(2)}) collective-permute-start(bf16[3,384,128]{2,1,0:T(8,128)(2,1)} %get-tuple-element.19), channel_id=1, source_target_pairs={{0,2},{1,3},{2,4},{3,5},{4,6},{5,7},{6,8},{7,9},{8,10},{9,11},{10,... | collective-permute-start | bytes 884744 | tf_op jit(solution)/shard_map/ppermute | solution.py:188
  86.9 72.2 %collective-permute-start.3 = (bf16[3,384,128]{2,1,0:T(8,128)(2,1)}, bf16[3,384,128]{2,1,0:T(8,128)(2,1)S(1)}, u32[]{:S(2)}, u32[]{:S(2)}) collective-permute-start(bf16[3,384,128]{2,1,0:T(8,128)(2,1)} %get-tuple-element.18), channel_id=1, source_target_pairs={{0,14},{1,15},{2,0},{3,1},{4,2},{5,3},{6,4},{7,5},{8,6},{9,7},{10,... | collective-permute-start | bytes 884744 | tf_op jit(solution)/shard_map/ppermute | solution.py:188
  113.2 46.0 %collective-permute-start.4 = (bf16[3,384,128]{2,1,0:T(8,128)(2,1)S(1)}, bf16[3,384,128]{2,1,0:T(8,128)(2,1)S(1)}, u32[]{:S(2)}, u32[]{:S(2)}) collective-permute-start(bf16[3,384,128]{2,1,0:T(8,128)(2,1)S(1)} %get-tuple-element.17), channel_id=1, source_target_pairs={{0,3},{1,4},{2,5},{3,6},{4,7},{5,8},{6,9},{7,10},{8,11},{9,12},{10... | collective-permute-start | bytes 884744 | tf_op jit(solution)/shard_map/ppermute | solution.py:188
  113.4 49.4 %collective-permute-start.5 = (bf16[3,384,128]{2,1,0:T(8,128)(2,1)S(1)}, bf16[3,384,128]{2,1,0:T(8,128)(2,1)S(1)}, u32[]{:S(2)}, u32[]{:S(2)}) collective-permute-start(bf16[3,384,128]{2,1,0:T(8,128)(2,1)S(1)} %get-tuple-element.16), channel_id=1, source_target_pairs={{0,13},{1,14},{2,15},{3,0},{4,1},{5,2},{6,3},{7,4},{8,5},{9,6},{10... | collective-permute-start | bytes 884744 | tf_op jit(solution)/shard_map/ppermute | solution.py:188
  133.2 34.2 %collective-permute-start.6 = (bf16[3,384,128]{2,1,0:T(8,128)(2,1)S(1)}, bf16[3,384,128]{2,1,0:T(8,128)(2,1)S(1)}, u32[]{:S(2)}, u32[]{:S(2)}) collective-permute-start(bf16[3,384,128]{2,1,0:T(8,128)(2,1)S(1)} %get-tuple-element.15), channel_id=1, source_target_pairs={{0,4},{1,5},{2,6},{3,7},{4,8},{5,9},{6,10},{7,11},{8,12},{9,13},{1... | collective-permute-start | bytes 884744 | tf_op jit(solution)/shard_map/ppermute | solution.py:188
  159.1 20.4 %collective-permute-start.7 = (bf16[3,384,128]{2,1,0:T(8,128)(2,1)S(1)}, bf16[3,384,128]{2,1,0:T(8,128)(2,1)S(1)}, u32[]{:S(2)}, u32[]{:S(2)}) collective-permute-start(bf16[3,384,128]{2,1,0:T(8,128)(2,1)S(1)} %get-tuple-element.14), channel_id=1, source_target_pairs={{0,12},{1,13},{2,14},{3,15},{4,0},{5,1},{6,2},{7,3},{8,4},{9,5},{1... | collective-permute-start | bytes 884744 | tf_op jit(solution)/shard_map/ppermute | solution.py:188
  159.2 34.3 %collective-permute-start.8 = (bf16[3,384,128]{2,1,0:T(8,128)(2,1)S(1)}, bf16[3,384,128]{2,1,0:T(8,128)(2,1)S(1)}, u32[]{:S(2)}, u32[]{:S(2)}) collective-permute-start(bf16[3,384,128]{2,1,0:T(8,128)(2,1)S(1)} %get-tuple-element.13), channel_id=1, source_target_pairs={{0,5},{1,6},{2,7},{3,8},{4,9},{5,10},{6,11},{7,12},{8,13},{9,14},{... | collective-permute-start | bytes 884744 | tf_op jit(solution)/shard_map/ppermute | solution.py:188
  159.2 47.4 %collective-permute-start.9 = (bf16[3,384,128]{2,1,0:T(8,128)(2,1)S(1)}, bf16[3,384,128]{2,1,0:T(8,128)(2,1)S(1)}, u32[]{:S(2)}, u32[]{:S(2)}) collective-permute-start(bf16[3,384,128]{2,1,0:T(8,128)(2,1)S(1)} %get-tuple-element.12), channel_id=1, source_target_pairs={{0,11},{1,12},{2,13},{3,14},{4,15},{5,0},{6,1},{7,2},{8,3},{9,4},{... | collective-permute-start | bytes 884744 | tf_op jit(solution)/shard_map/ppermute | solution.py:188
  208.4 1.7 copy-start
  250.7 21.5 %copy-start.2 = (bf16[1024]{0:T(1024)(128)(2,1)S(1)}, bf16[1024]{0:T(1024)(128)(2,1)}, u32[]{:S(2)}) copy-start(bf16[1024]{0:T(1024)(128)(2,1)} %param.17) | copy-start | bytes 6148
  265.2 22.1 %all-to-all-start = ((bf16[16,24,1024]{2,1,0:T(8,128)(2,1)}), bf16[16,24,1024]{2,1,0:T(8,128)(2,1)S(1)}, u32[]{:S(2)}, u32[]{:S(2)}) async-start(bf16[16,24,1024]{2,1,0:T(8,128)(2,1)} %bitcast.86), calls=%async_computation | async-start | bytes 1572864 | tf_op jit(solution)/shard_map/all_to_all | solution.py:238
Sparse Core Ops, SparseCore 0:
  44.6 206.1 all-gather.2

commit v8 on v7

--- a/solution.py
+++ b/solution.py
@@ -26,12 +26,12 @@
 
 
 QUARTERS = 4
-BACK = (0, 1, 15, 2, 14, 3, 13, 4, 12, 5, 11, 6, 10, 7, 9, 8)
-
-
-def pack_kernel(down, up, comp, over, out, sems):
+BACK = (0, 8, 1, 15, 7, 2, 14, 9, 3, 13, 6, 4, 12, 10, 5, 11)
+
+
+def pack_kernel(down, up, comp, out, sems):
     half = out.shape[1]
-    sources = [down.at[:, pl.ds(0, half)], down.at[:, pl.ds(half, half)], up, comp, over]
+    sources = [down.at[:, pl.ds(0, half)], down.at[:, pl.ds(half, half)], up, comp]
     copies, first = [], 0
     for n, source in enumerate(sources):
         count = source.shape[0]
@@ -64,7 +64,7 @@
 
 
 def tower_kernel(
-    tables, weights, bias, comp_bias, out, base, state, down0, down1, up0, up1, comp, over, sems
+    tables, weights, bias, comp_bias, out, base, state, down0, down1, up0, up1, comp, sems
 ):
     features = base.shape[1]
     shards, step, rank = down0.shape
@@ -96,8 +96,7 @@
     ]
     bring_up1 = bring(at_up + rank, rank, up1, n + 3)
     bring_comp = bring(at_up + 2 * rank, step, comp, n + 4)
-    bring_over = bring(at_up + 2 * rank + step, over.shape[1], over, n + 5)
-    for copy in (*early, bring_up0, *bring_down1, bring_up1, bring_comp, bring_over):
+    for copy in (*early, bring_up0, *bring_down1, bring_up1, bring_comp):
         copy.start()
 
     total = None
@@ -131,12 +130,34 @@
         state[:, here] = (part * (raised + bias[1:2, here]) + held).astype(BF16)
     bring_comp.wait()
     squeezed = jnp.dot(state[...], comp.reshape(features, width)[...], preferred_element_type=F32)
-    squeezed = (squeezed + comp_bias[...]).astype(BF16)
-    bring_over.wait()
-    over_t = over.reshape(over.shape[0] * over.shape[1], width)[...]
-    out[...] = lax.dot_general(
-        squeezed, over_t, (((1,), (1,)), ((), ())), preferred_element_type=F32
-    ).astype(BF16)
+    out[...] = (squeezed + comp_bias[...]).astype(BF16)
+
+
+def over_kernel(place, joined, *refs):
+    pieces, (bias, out, held, sems) = refs[:-4], refs[-4:]
+    copies = [
+        pltpu.make_async_copy(piece, held.at[n], sems.at[n]) for n, piece in enumerate(pieces)
+    ]
+    for copy in copies:
+        copy.start()
+    x, y = place[0], place[1]
+    total = None
+    for n, copy in enumerate(copies):
+        copy.wait()
+        tower = 4 * lax.rem(x + 4 - n // 4, 4) + lax.rem(y + 4 - n % 4, 4)
+        part = lax.dot_general(
+            joined[tower], held[n], (((1,), (1,)), ((), ())), preferred_element_type=F32
+        )
+        total = part if total is None else total + part
+    out[...] = jnp.maximum(total + bias[...], 0.0).astype(BF16)
+
+
+def once(*others):
+    zero = jnp.int32(0)
+    for other in others:
+        seen = other[(0,) * other.ndim]
+        zero = zero + jnp.where(seen == seen, 0, 1)
+    return zero
 
 
 def on_device(
@@ -158,45 +179,64 @@
     features = step * shards
     width = comp_weight.shape[2]
     samples = batch // shards
-    columns = over_weight.shape[1]
-    outputs = columns * shards
+    outputs = over_weight.shape[1] * shards
+
+    anywhere = pl.BlockSpec(memory_space=pl.ANY)
+
+    def whole(*shape):
+        return pl.BlockSpec(shape, lambda i, *_: (0,) * len(shape))
 
     parts = (
         cross_down[0].reshape(layers * step, rank),
         cross_up[0].reshape(layers * rank, step),
         comp_weight[0],
-        over_weight.T,
     )
+    packed_rows = sum(part.size for part in parts) // step
     packed = pl.pallas_call(
         pack_kernel,
-        in_specs=[pl.BlockSpec(memory_space=pl.ANY)] * len(parts),
-        out_specs=pl.BlockSpec(memory_space=pl.ANY),
+        grid=(1,),
+        in_specs=[anywhere] * len(parts),
+        out_specs=whole(packed_rows, step),
         scratch_shapes=[pltpu.SemaphoreType.DMA((len(parts) + 1,))],
-        out_shape=jax.ShapeDtypeStruct((sum(p.size for p in parts) // step, step), BF16),
+        out_shape=jax.ShapeDtypeStruct((packed_rows, step), BF16),
         compiler_params=pltpu.CompilerParams(vmem_limit_bytes=58 * 2**20),
     )(*parts)
     weights = lax.all_gather(packed, "shard", axis=0)
 
+    over_rows = lax.all_gather(over_weight.T, "shard", axis=0, tiled=True)
     by_slot = pooled[0].transpose(1, 0, 2).reshape(slot_most, shards, samples, emb)
 
     def piece_for(to):
         return lax.dynamic_index_in_dim(by_slot, to % 16, 1, keepdims=False)
 
-    pieces = [piece_for(shard)]
-    for k in BACK[1:]:
-        moves = [(i, (i + k) % 16) for i in range(16)]
-        pieces.append(lax.ppermute(piece_for(shard + k), "shard", moves))
+    pieces, zero, over_x, over_all = {0: piece_for(shard)}, once(over_rows), [over_rows], []
+    for n in range(5):
+        sent = []
+        if n == 0:
+            for d in range(1, 4):
+                moves = [(i, (i + 4 * d) % 16) for i in range(16)]
+                over_x.append(lax.ppermute(over_rows, "tower", moves))
+            sent = over_x[1:]
+        else:
+            if n == 1:
+                over_x = jnp.stack(over_x)
+            part = lax.dynamic_index_in_dim(over_x, n - 1 + zero, 0, keepdims=False)
+            over_all.append(part)
+            for e in range(1, 4):
+                moves = [(i, i // 4 * 4 + (i + e) % 4) for i in range(16)]
+                sent.append(lax.ppermute(part, "tower", moves))
+            over_all += sent
+        for k in BACK[1 + 3 * n : 4 + 3 * n]:
+            moves = [(i, (i + k) % 16) for i in range(16)]
+            pieces[k] = lax.ppermute(piece_for(shard + k + zero), "shard", moves)
+        zero = once(*sent, *[pieces[k] for k in BACK[1 + 3 * n : 4 + 3 * n]])
+    pieces = [pieces[k] for k in BACK]
 
     slots = slot_order(table_tower, table_owner, tower_id, features // emb, slot_most)
     index = jnp.arange(shards * slot_most, dtype=jnp.int32)[:, None]
     turn = jnp.arange(1, slots.shape[0] + 1, dtype=jnp.int32)[None, :]
     places = jnp.sum(jnp.where(slots[None, :] == index, turn, 0), axis=1) - 1
-    places = jnp.concatenate([places, shard[None]]).astype(jnp.int32)
-
-    anywhere = pl.BlockSpec(memory_space=pl.ANY)
-
-    def whole(*shape):
-        return pl.BlockSpec(shape, lambda i, *_: (0,) * len(shape))
+    places = jnp.concatenate([places, (shard + zero)[None]]).astype(jnp.int32)
 
     tables = pl.pallas_call(
         table_kernel,
@@ -208,16 +248,16 @@
             scratch_shapes=[pltpu.SemaphoreType.DMA],
         ),
         out_shape=jax.ShapeDtypeStruct((samples, features), BF16),
-        compiler_params=pltpu.CompilerParams(vmem_limit_bytes=12 * 2**20),
+        compiler_params=pltpu.CompilerParams(vmem_limit_bytes=40 * 2**20),
         cost_estimate=pl.CostEstimate(flops=0, bytes_accessed=10 * 10**6, transcendentals=0),
     )(places, *pieces)
 
-    partial = pl.pallas_call(
+    squeezed = pl.pallas_call(
         tower_kernel,
         grid_spec=pl.GridSpec(
             grid=(1,),
             in_specs=[anywhere, anywhere, whole(layers, features), whole(1, width)],
-            out_specs=whole(samples, outputs),
+            out_specs=whole(samples, width),
             scratch_shapes=[
                 pltpu.VMEM((samples, features), BF16),
                 pltpu.VMEM((samples, features), BF16),
@@ -226,20 +266,36 @@
                 pltpu.VMEM((shards, rank, step), BF16),
                 pltpu.VMEM((shards, rank, step), BF16),
                 pltpu.VMEM((shards, step, width), BF16),
-                pltpu.VMEM((shards, columns, width), BF16),
-                pltpu.SemaphoreType.DMA((6 + 3 * QUARTERS,)),
+                pltpu.SemaphoreType.DMA((5 + 3 * QUARTERS,)),
             ],
         ),
-        out_shape=jax.ShapeDtypeStruct((samples, outputs), BF16),
-        compiler_params=pltpu.CompilerParams(vmem_limit_bytes=58 * 2**20),
+        out_shape=jax.ShapeDtypeStruct((samples, width), BF16),
+        compiler_params=pltpu.CompilerParams(vmem_limit_bytes=36 * 2**20),
         cost_estimate=pl.CostEstimate(flops=8 * 10**9, bytes_accessed=24 * 10**6, transcendentals=0),
     )(tables, weights, cross_bias[0].astype(F32), comp_bias.astype(F32))
 
-    summed = lax.all_to_all(
-        partial.reshape(towers, samples // towers, outputs), "tower", 0, 0, tiled=True
-    )
-    total = jnp.sum(summed.astype(F32), axis=0) + over_bias.astype(F32)
-    return jax.nn.relu(total).astype(BF16)[None]
+    small = samples // towers
+    joined = lax.all_to_all(squeezed.reshape(towers, small, width), "tower", 0, 0, tiled=True)
+    place = jnp.stack([tower_id // 4, tower_id % 4]).astype(jnp.int32)
+    scores = pl.pallas_call(
+        over_kernel,
+        grid_spec=pltpu.PrefetchScalarGridSpec(
+            num_scalar_prefetch=1,
+            grid=(1,),
+            in_specs=[whole(towers, small, width)]
+            + [anywhere] * towers
+            + [whole(1, outputs)],
+            out_specs=whole(small, outputs),
+            scratch_shapes=[
+                pltpu.VMEM((towers, outputs, width), BF16),
+                pltpu.SemaphoreType.DMA((towers,)),
+            ],
+        ),
+        out_shape=jax.ShapeDtypeStruct((small, outputs), BF16),
+        compiler_params=pltpu.CompilerParams(vmem_limit_bytes=58 * 2**20),
+        cost_estimate=pl.CostEstimate(flops=2 * 10**8, bytes_accessed=9 * 10**6, transcendentals=0),
+    )(place, joined, *over_all, over_bias.astype(F32)[None])
+    return scores[None]
 
 
 def solution(mesh):

time: 295 us -> 349 us (1.18); the launches traced: 295 us -> 343 us
  waiting for transfers between devices: 178 us -> 122 us
  local copies, waits for them, and re-layouts: 6.11 us -> 53 us
  between operations: 13.7 us -> 54.7 us
  Pallas kernels: 54.2 us -> 24.5 us
  starting transfers between devices: 40 us -> 67.3 us
  blocking collectives: 0 us -> 18.1 us
    all_gather x1, waiting for transfers between devices: 40.6 us -> 0.02 us  [on_device(): weights = lax.all_gather(packed, 'shard', axis=0)]
    ppermute x15 -> x30, starting transfers between devices: 32.9 us -> 61.3 us  [the longest x15 32.5 us: on_device(): pieces[k] = lax.ppermute(piece_for(shard + k + zero), 'shard', moves)]
    pallas_call x1 -> x2, Pallas kernels: 37.9 us -> 10 us  [the longest x1 7.69 us: on_device(): pl.pallas_call(over_kernel, grid_spec=pltpu.PrefetchScalarGridSpec(num_sc...]
    slice x0 -> x31, local copies, waits for them, and re-layouts: none -> 21.1 us  [once(): seen = other[(0,) * other.ndim]]
    all_gather x0 -> x1, blocking collectives: none -> 18.1 us  [on_device(): over_rows = lax.all_gather(over_weight.T, 'shard', axis=0, tiled=True)]
    unnamed x10 -> x98, local copies, waits for them, and re-layouts: 1.7 us -> 17.4 us
    all_to_all x1, waiting for transfers between devices: 15 us -> 6.96 us  [on_device(): lax.all_to_all(squeezed.reshape(towers, small, width), 'tower', 0, 0, til...]
    ppermute x15 -> x30, waiting for transfers between devices: 122 us -> 115 us  [the longest x15 115 us: on_device(): pieces[k] = lax.ppermute(piece_for(shard + k + zero), 'shard', moves)]
  transfers between devices with their start and end apart: 17 -> 32, of which waited for: 10 -> 14; matrix products, arithmetic and copies ran while one was open for 2% -> 11% of each run, Pallas kernels for 1% -> 1%
where the time goes in v8:
time: 349 us; the launch traced here: 343 us
  waiting for transfers between devices  122 us (35%)
  starting transfers between devices  67.3 us (19%)
  between operations  54.7 us (16%)
  local copies, waits for them, and re-layouts  53 us (15%)
  Pallas kernels  24.5 us (7%)
  blocking collectives  18.1 us (5%)
  other arithmetic  3.72 us (1%)
    ppermute x15, waiting for transfers between devices, on_device(): pieces[k] = lax.ppermute(piece_for(shard + k + zero), 'shard', moves)  115 us
    ppermute x15, starting transfers between devices, on_device(): pieces[k] = lax.ppermute(piece_for(shard + k + zero), 'shard', moves)  32.5 us
    ppermute x12, starting transfers between devices, on_device(): sent.append(lax.ppermute(part, 'tower', moves))  23.2 us
    slice x31, local copies, waits for them, and re-layouts, once(): seen = other[(0,) * other.ndim]  21.1 us
    all_gather x1, blocking collectives, on_device(): over_rows = lax.all_gather(over_weight.T, 'shard', axis=0, tiled=True)  18.1 us
    unnamed x98, local copies, waits for them, and re-layouts  17.4 us
    pallas_call x1, Pallas kernels, on_device(): pl.pallas_call(tower_kernel, grid_spec=pl.GridSpec(grid=(1,), in_specs=[a...  12.6 us
    squeeze x5, local copies, waits for them, and re-layouts, piece_for(): return lax.dynamic_index_in_dim(by_slot, to % 16, 1, keepdims=False)  10.6 us
  transfers between devices with their start and end apart: 32, of which 14 were waited for; matrix products, arithmetic and copies ran while one was open for 11% of the time, Pallas kernels for 1%

profile of v8, /device:TPU:96, one launch (start us, length us, event | category | flops | bytes accessed | tf_op | source)
XLA Modules:
  0.0 343.0 jit_solution(17652222592773653572)
XLA Ops:
  6.5 2.3 shard_map.101
  8.9 18.1 %all_gather.9 = bf16[1024,256]{1,0:T(8,128)(2,1)S(1)} all-gather(bf16[64,256]{1,0:T(8,128)(2,1)S(1)} %bitcast.128), channel_id=1, replica_groups=mesh['tower'=16,'shard'=16] {'shard'}, dimensions={0}, use_global_device_ids=true | all-gather | bytes 557056 | tf_op jit(solution)/shard_map/all_gather | solution.py:206
  28.9 1.9 dynamic-slice_bitcast_fusion.17
  30.9 2.3 collective-permute-start.3
  33.1 1.5 collective-permute-start
  34.6 2.7 collective-permute-start.1
  37.3 1.5 collective-permute-start.2
  38.7 17.3 %collective-permute-done.3.refs_1_ = bf16[3,384,128]{2,1,0:T(8,128)(2,1)S(1)} collective-permute-done((bf16[3,384,128]{2,1,0:T(8,128)(2,1)S(1)}, bf16[3,384,128]{2,1,0:T(8,128)(2,1)S(1)}, u32[]{:S(2)}, u32[]{:S(2)}) %collective-permute-start.3) | collective-permute-done | bytes 294944 | tf_op jit(solution)/shard_map/ppermute | solution.py:231
  58.2 5.3 %collective-permute-done.4.refs_2_ = bf16[3,384,128]{2,1,0:T(8,128)(2,1)S(1)} collective-permute-done((bf16[3,384,128]{2,1,0:T(8,128)(2,1)}, bf16[3,384,128]{2,1,0:T(8,128)(2,1)S(1)}, u32[]{:S(2)}, u32[]{:S(2)}) %collective-permute-start.4) | collective-permute-done | bytes 294944 | tf_op jit(solution)/shard_map/ppermute | solution.py:231
  65.4 1.6 collective-permute-done.5.refs_3_
  74.5 2.2 dynamic-slice_bitcast_fusion.14
  76.7 2.7 collective-permute-start.9
  79.4 1.8 pad_maximum_fusion
  82.2 1.5 collective-permute-start.6
  83.8 2.8 collective-permute-start.7
  86.6 1.4 collective-permute-start.8
  88.0 4.6 %collective-permute-start.10 = (bf16[3,384,128]{2,1,0:T(8,128)(2,1)}, bf16[3,384,128]{2,1,0:T(8,128)(2,1)S(1)}, u32[]{:S(2)}, u32[]{:S(2)}) collective-permute-start(bf16[3,384,128]{2,1,0:T(8,128)(2,1)} %get-tuple-element.18), channel_id=1, source_target_pairs={{0,2},{1,3},{2,4},{3,5},{4,6},{5,7},{6,8},{7,9},{8,10},{9,11},{10,... | collective-permute-start | bytes 884744 | tf_op jit(solution)/shard_map/ppermute | solution.py:231
  92.6 9.5 %collective-permute-done.9.refs_4_ = bf16[3,384,128]{2,1,0:T(8,128)(2,1)S(1)} collective-permute-done((bf16[3,384,128]{2,1,0:T(8,128)(2,1)}, bf16[3,384,128]{2,1,0:T(8,128)(2,1)S(1)}, u32[]{:S(2)}, u32[]{:S(2)}) %collective-permute-start.9) | collective-permute-done | bytes 294944 | tf_op jit(solution)/shard_map/ppermute | solution.py:231
  102.2 1.9 collective-permute-start.11
  105.8 12.6 %collective-permute-done.10.refs_5_ = bf16[3,384,128]{2,1,0:T(8,128)(2,1)S(1)} collective-permute-done((bf16[3,384,128]{2,1,0:T(8,128)(2,1)}, bf16[3,384,128]{2,1,0:T(8,128)(2,1)S(1)}, u32[]{:S(2)}, u32[]{:S(2)}) %collective-permute-start.10) | collective-permute-done | bytes 294944 | tf_op jit(solution)/shard_map/ppermute | solution.py:231
  122.2 1.2 slice.131
  124.7 1.2 slice.132
  127.2 1.2 slice.133
  129.8 2.1 dynamic-slice_bitcast_fusion.11
  131.9 5.1 %collective-permute-start.15 = (bf16[3,384,128]{2,1,0:T(8,128)(2,1)}, bf16[3,384,128]{2,1,0:T(8,128)(2,1)S(1)}, u32[]{:S(2)}, u32[]{:S(2)}) collective-permute-start(bf16[3,384,128]{2,1,0:T(8,128)(2,1)} %get-tuple-element.16), channel_id=1, source_target_pairs={{0,9},{1,10},{2,11},{3,12},{4,13},{5,14},{6,15},{7,0},{8,1},{9,2},... | collective-permute-start | bytes 884744 | tf_op jit(solution)/shard_map/ppermute | solution.py:231
  137.9 2.0 collective-permute-start.12
  139.9 3.1 collective-permute-start.13
  143.0 1.3 collective-permute-start.14
  144.3 14.9 %collective-permute-done.15.refs_7_ = bf16[3,384,128]{2,1,0:T(8,128)(2,1)S(1)} collective-permute-done((bf16[3,384,128]{2,1,0:T(8,128)(2,1)}, bf16[3,384,128]{2,1,0:T(8,128)(2,1)S(1)}, u32[]{:S(2)}, u32[]{:S(2)}) %collective-permute-start.15) | collective-permute-done | bytes 294944 | tf_op jit(solution)/shard_map/ppermute | solution.py:231
  159.2 2.8 collective-permute-start.17
  163.8 1.1 collective-permute-done.16.refs_8_
  166.8 2.5 collective-permute-done.17.refs_9_
  171.2 1.2 slice.137
  173.7 1.1 slice.138
  176.1 1.1 slice.139
  178.6 2.1 dynamic-slice_bitcast_fusion.8
  180.8 4.1 %collective-permute-start.21 = (bf16[3,384,128]{2,1,0:T(8,128)(2,1)}, bf16[3,384,128]{2,1,0:T(8,128)(2,1)S(1)}, u32[]{:S(2)}, u32[]{:S(2)}) collective-permute-start(bf16[3,384,128]{2,1,0:T(8,128)(2,1)} %get-tuple-element.13), channel_id=1, source_target_pairs={{0,6},{1,7},{2,8},{3,9},{4,10},{5,11},{6,12},{7,13},{8,14},{9,15},... | collective-permute-start | bytes 884744 | tf_op jit(solution)/shard_map/ppermute | solution.py:231
  184.8 1.1 dynamic-slice_bitcast_fusion.1.refs_8_
  185.9 1.6 collective-permute-start.18
  187.5 2.7 collective-permute-start.19
  190.2 1.5 collective-permute-start.20
  191.7 3.5 %collective-permute-start.22 = (bf16[3,384,128]{2,1,0:T(8,128)(2,1)}, bf16[3,384,128]{2,1,0:T(8,128)(2,1)S(1)}, u32[]{:S(2)}, u32[]{:S(2)}) collective-permute-start(bf16[3,384,128]{2,1,0:T(8,128)(2,1)} %get-tuple-element.12), channel_id=1, source_target_pairs={{0,4},{1,5},{2,6},{3,7},{4,8},{5,9},{6,10},{7,11},{8,12},{9,13},{1... | collective-permute-start | bytes 884744 | tf_op jit(solution)/shard_map/ppermute | solution.py:231
  195.2 7.2 %collective-permute-done.21.refs_10_ = bf16[3,384,128]{2,1,0:T(8,128)(2,1)S(1)} collective-permute-done((bf16[3,384,128]{2,1,0:T(8,128)(2,1)}, bf16[3,384,128]{2,1,0:T(8,128)(2,1)S(1)}, u32[]{:S(2)}, u32[]{:S(2)}) %collective-permute-start.21) | collective-permute-done | bytes 294944 | tf_op jit(solution)/shard_map/ppermute | solution.py:231
  202.3 3.8 %collective-permute-start.23 = (bf16[3,384,128]{2,1,0:T(8,128)(2,1)}, bf16[3,384,128]{2,1,0:T(8,128)(2,1)S(1)}, u32[]{:S(2)}, u32[]{:S(2)}) collective-permute-start(bf16[3,384,128]{2,1,0:T(8,128)(2,1)} %get-tuple-element.11), channel_id=1, source_target_pairs={{0,12},{1,13},{2,14},{3,15},{4,0},{5,1},{6,2},{7,3},{8,4},{9,5},{1... | collective-permute-start | bytes 884744 | tf_op jit(solution)/shard_map/ppermute | solution.py:231
  208.4 6.6 %collective-permute-done.22.refs_11_ = bf16[3,384,128]{2,1,0:T(8,128)(2,1)S(1)} collective-permute-done((bf16[3,384,128]{2,1,0:T(8,128)(2,1)}, bf16[3,384,128]{2,1,0:T(8,128)(2,1)S(1)}, u32[]{:S(2)}, u32[]{:S(2)}) %collective-permute-start.22) | collective-permute-done | bytes 294944 | tf_op jit(solution)/shard_map/ppermute | solution.py:231
  216.8 7.7 %collective-permute-done.23.refs_12_ = bf16[3,384,128]{2,1,0:T(8,128)(2,1)S(1)} collective-permute-done((bf16[3,384,128]{2,1,0:T(8,128)(2,1)}, bf16[3,384,128]{2,1,0:T(8,128)(2,1)S(1)}, u32[]{:S(2)}, u32[]{:S(2)}) %collective-permute-start.23) | collective-permute-done | bytes 294944 | tf_op jit(solution)/shard_map/ppermute | solution.py:231
  230.1 1.2 slice.145
  232.6 2.2 dynamic-slice_bitcast_fusion.4
  234.9 1.1 dynamic-slice_bitcast_fusion.refs_12_
  236.0 2.1 collective-permute-start.24
  238.1 2.1 collective-permute-start.25
  240.2 1.2 collective-permute-start.26
  241.5 1.1 collective-permute-start.28
  242.6 17.0 %collective-permute-done.27.refs_13_ = bf16[3,384,128]{2,1,0:T(8,128)(2,1)S(1)} collective-permute-done((bf16[3,384,128]{2,1,0:T(8,128)(2,1)}, bf16[3,384,128]{2,1,0:T(8,128)(2,1)S(1)}, u32[]{:S(2)}, u32[]{:S(2)}) %collective-permute-start.27) | collective-permute-done | bytes 294944 | tf_op jit(solution)/shard_map/ppermute | solution.py:231
  264.9 11.3 %collective-permute-done.29.refs_15_ = bf16[3,384,128]{2,1,0:T(8,128)(2,1)S(1)} collective-permute-done((bf16[3,384,128]{2,1,0:T(8,128)(2,1)S(1)}, bf16[3,384,128]{2,1,0:T(8,128)(2,1)S(1)}, u32[]{:S(2)}, u32[]{:S(2)}) %collective-permute-start.29) | collective-permute-done | bytes 294944 | tf_op jit(solution)/shard_map/ppermute | solution.py:231
  286.4 1.0 copy-done.5
  287.4 1.0 copy-done.7
  288.4 1.0 copy-done.9
  290.3 1.0 copy-done.13
  298.9 1.9 shard_map.100.tables
  300.8 12.6 %shard_map.102 = bf16[384,256]{1,0:T(8,128)(2,1)} custom-call(bf16[384,4096]{1,0:T(8,128)(2,1)S(1)} %shard_map.100.tables, bf16[16,2304,256]{2,1,0:T(8,128)(2,1)} %bitcast.130, f32[2,4096]{1,0:T(2,128)S(1)} %bitcast_convert_fusion.bias, f32[1,256]{1,0:T(1,128)S(1)} %convert_element_type.19.comp_bias), custom_call_target="tpu_custom_call" | custom-call | flops 8000000000 | bytes 24000000 | tf_op jit(solution)/shard_map/pallas_call | solution.py:255
  313.5 6.0 %all-to-all-start = ((bf16[16,24,256]{2,1,0:T(8,128)(2,1)}), bf16[16,24,256]{2,1,0:T(8,128)(2,1)S(1)}, u32[]{:S(2)}, u32[]{:S(2)}) async-start(bf16[16,24,256]{2,1,0:T(8,128)(2,1)} %bitcast.57), calls=%async_computation | async-start | bytes 393216 | tf_op jit(solution)/shard_map/all_to_all | solution.py:278
  320.8 7.0 %all-to-all-done.joined = bf16[16,24,256]{2,1,0:T(8,128)(2,1)S(1)} async-done(((bf16[16,24,256]{2,1,0:T(8,128)(2,1)}), bf16[16,24,256]{2,1,0:T(8,128)(2,1)S(1)}, u32[]{:S(2)}, u32[]{:S(2)}) %all-to-all-start) | async-done | bytes 196640 | tf_op jit(solution)/shard_map/all_to_all | solution.py:278
  328.4 7.7 %shard_map.103 = bf16[24,1024]{1,0:T(8,128)(2,1)} custom-call(s32[2]{0:T(128)} %pad_add_fusion.place, bf16[16,24,256]{2,1,0:T(8,128)(2,1)} %copy-done.34, bf16[1024,256]{1,0:T(8,128)(2,1)} %dynamic-slice_bitcast_fusion.3.refs_0_, bf16[1024,256]{1,0:T(8,128)(2,1)} %collective-permute-done.6.refs_1_, bf16[1024,256]{1,0:T(8,128)(2,1)} %collective-permute-done.7.refs_2_, ...), custom_call_target="tpu_custom_call" | custom-call | flops 200000000 | bytes 9000000 | tf_op jit(solution)/shard_map/pallas_call | solution.py:280
  (157 shorter events, 30.6 us)
Async XLA Ops:
  6.5 2.4 copy-start.43
  6.5 294.3 %all-gather.3.cloned.1.call-start = ((), (), s32[]{:S(2)}) async-start(), calls=%async_computation.1 | async-start | bytes 20054016 | tf_op jit(solution)/shard_map/all_gather | solution.py:204
  27.1 52.4 %copy-start.33 = (bf16[1024,256]{1,0:T(8,128)(2,1)}, bf16[1024,256]{1,0:T(8,128)(2,1)S(1)}, u32[]{:S(2)}) copy-start(bf16[1024,256]{1,0:T(8,128)(2,1)S(1)} %all_gather.9) | copy-start | bytes 1572868
  30.9 25.2 %collective-permute-start.3 = (bf16[3,384,128]{2,1,0:T(8,128)(2,1)S(1)}, bf16[3,384,128]{2,1,0:T(8,128)(2,1)S(1)}, u32[]{:S(2)}, u32[]{:S(2)}) collective-permute-start(bf16[3,384,128]{2,1,0:T(8,128)(2,1)S(1)} %get-tuple-element.22), channel_id=1, source_target_pairs={{0,8},{1,9},{2,10},{3,11},{4,12},{5,13},{6,14},{7,15},{8,0},{9,1},... | collective-permute-start | bytes 884744 | tf_op jit(solution)/shard_map/ppermute | solution.py:231
  33.1 35.7 %collective-permute-start = (bf16[1024,256]{1,0:T(8,128)(2,1)S(1)}, bf16[1024,256]{1,0:T(8,128)(2,1)S(1)}, u32[]{:S(2)}, u32[]{:S(2)}) collective-permute-start(bf16[1024,256]{1,0:T(8,128)(2,1)S(1)} %all_gather.9), channel_id=1, source_target_pairs={{0,64},{16,80},{32,96},{48,112},{64,128},{80,144},{96,160},{112,17... | collective-permute-start | bytes 1572872 | tf_op jit(solution)/shard_map/ppermute | solution.py:218
  34.6 36.1 %collective-permute-start.1 = (bf16[1024,256]{1,0:T(8,128)(2,1)S(1)}, bf16[1024,256]{1,0:T(8,128)(2,1)S(1)}, u32[]{:S(2)}, u32[]{:S(2)}) collective-permute-start(bf16[1024,256]{1,0:T(8,128)(2,1)S(1)} %all_gather.9), channel_id=1, source_target_pairs={{0,128},{16,144},{32,160},{48,176},{64,192},{80,208},{96,224},{112... | collective-permute-start | bytes 1572872 | tf_op jit(solution)/shard_map/ppermute | solution.py:218
  37.3 35.3 %collective-permute-start.2 = (bf16[1024,256]{1,0:T(8,128)(2,1)S(1)}, bf16[1024,256]{1,0:T(8,128)(2,1)S(1)}, u32[]{:S(2)}, u32[]{:S(2)}) collective-permute-start(bf16[1024,256]{1,0:T(8,128)(2,1)S(1)} %all_gather.9), channel_id=1, source_target_pairs={{0,192},{16,208},{32,224},{48,240},{64,0},{80,16},{96,32},{112,48}... | collective-permute-start | bytes 1572872 | tf_op jit(solution)/shard_map/ppermute | solution.py:218
  38.7 24.8 %collective-permute-start.4 = (bf16[3,384,128]{2,1,0:T(8,128)(2,1)}, bf16[3,384,128]{2,1,0:T(8,128)(2,1)S(1)}, u32[]{:S(2)}, u32[]{:S(2)}) collective-permute-start(bf16[3,384,128]{2,1,0:T(8,128)(2,1)} %get-tuple-element.21), channel_id=1, source_target_pairs={{0,1},{1,2},{2,3},{3,4},{4,5},{5,6},{6,7},{7,8},{8,9},{9,10},{10,1... | collective-permute-start | bytes 884744 | tf_op jit(solution)/shard_map/ppermute | solution.py:231
  56.0 25.3 %copy-start = (bf16[3,384,128]{2,1,0:T(8,128)(2,1)}, bf16[3,384,128]{2,1,0:T(8,128)(2,1)S(1)}, u32[]{:S(2)}) copy-start(bf16[3,384,128]{2,1,0:T(8,128)(2,1)S(1)} %collective-permute-done.3.refs_1_) | copy-start | bytes 884740
  56.0 10.9 %collective-permute-start.5 = (bf16[3,384,128]{2,1,0:T(8,128)(2,1)S(1)}, bf16[3,384,128]{2,1,0:T(8,128)(2,1)S(1)}, u32[]{:S(2)}, u32[]{:S(2)}) collective-permute-start(bf16[3,384,128]{2,1,0:T(8,128)(2,1)S(1)} %get-tuple-element.20), channel_id=1, source_target_pairs={{0,15},{1,0},{2,1},{3,2},{4,3},{5,4},{6,5},{7,6},{8,7},{9,8},{10,9... | collective-permute-start | bytes 884744 | tf_op jit(solution)/shard_map/ppermute | solution.py:231
  63.5 17.8 %copy-start.2 = (bf16[3,384,128]{2,1,0:T(8,128)(2,1)}, bf16[3,384,128]{2,1,0:T(8,128)(2,1)S(1)}, u32[]{:S(2)}) copy-start(bf16[3,384,128]{2,1,0:T(8,128)(2,1)S(1)} %collective-permute-done.4.refs_2_) | copy-start | bytes 884740
  67.0 14.4 %copy-start.4 = (bf16[3,384,128]{2,1,0:T(8,128)(2,1)}, bf16[3,384,128]{2,1,0:T(8,128)(2,1)S(1)}, u32[]{:S(2)}) copy-start(bf16[3,384,128]{2,1,0:T(8,128)(2,1)S(1)} %collective-permute-done.5.refs_3_) | copy-start | bytes 884740
  68.8 10.6 %copy-start.40 = (bf16[1024,256]{1,0:T(8,128)(2,1)}, bf16[1024,256]{1,0:T(8,128)(2,1)S(1)}, u32[]{:S(2)}) copy-start(bf16[1024,256]{1,0:T(8,128)(2,1)S(1)} %collective-permute-done) | copy-start | bytes 1572868
  70.7 8.8 %copy-start.41 = (bf16[1024,256]{1,0:T(8,128)(2,1)}, bf16[1024,256]{1,0:T(8,128)(2,1)S(1)}, u32[]{:S(2)}) copy-start(bf16[1024,256]{1,0:T(8,128)(2,1)S(1)} %collective-permute-done.1) | copy-start | bytes 1572868
  72.6 6.9 %copy-start.42 = (bf16[1024,256]{1,0:T(8,128)(2,1)}, bf16[1024,256]{1,0:T(8,128)(2,1)S(1)}, u32[]{:S(2)}) copy-start(bf16[1024,256]{1,0:T(8,128)(2,1)S(1)} %collective-permute-done.2) | copy-start | bytes 1572868
  76.7 25.4 %collective-permute-start.9 = (bf16[3,384,128]{2,1,0:T(8,128)(2,1)}, bf16[3,384,128]{2,1,0:T(8,128)(2,1)S(1)}, u32[]{:S(2)}, u32[]{:S(2)}) collective-permute-start(bf16[3,384,128]{2,1,0:T(8,128)(2,1)} %get-tuple-element.19), channel_id=1, source_target_pairs={{0,7},{1,8},{2,9},{3,10},{4,11},{5,12},{6,13},{7,14},{8,15},{9,0},... | collective-permute-start | bytes 884744 | tf_op jit(solution)/shard_map/ppermute | solution.py:231
  81.3 62.9 %copy-start.30 = (bf16[4,1024,256]{2,1,0:T(8,128)(2,1)}, bf16[4,1024,256]{2,1,0:T(8,128)(2,1)S(1)}, u32[]{:S(2)}) copy-start(bf16[4,1024,256]{2,1,0:T(8,128)(2,1)S(1)} %pad_maximum_fusion) | copy-start | bytes 6291460
  81.3 80.7 %copy-start.45 = (bf16[1,2,4096]{2,1,0:T(2,128)(2,1)S(1)}, bf16[1,2,4096]{2,1,0:T(2,128)(2,1)}, u32[]{:S(2)}) copy-start(bf16[1,2,4096]{2,1,0:T(2,128)(2,1)} %param.13) | copy-start | bytes 49156
  82.2 40.0 %collective-permute-start.6 = (bf16[1024,256]{1,0:T(8,128)(2,1)}, bf16[1024,256]{1,0:T(8,128)(2,1)}, u32[]{:S(2)}, u32[]{:S(2)}) collective-permute-start(bf16[1024,256]{1,0:T(8,128)(2,1)} %dynamic-slice_bitcast_fusion.3.refs_0_), channel_id=1, source_target_pairs={{0,16},{16,32},{32,48},{48,0},{64,80},{80,96},{96,112},{112,64},{1... | collective-permute-start | bytes 1572872 | tf_op jit(solution)/shard_map/ppermute | solution.py:227
  83.8 40.9 %collective-permute-start.7 = (bf16[1024,256]{1,0:T(8,128)(2,1)}, bf16[1024,256]{1,0:T(8,128)(2,1)}, u32[]{:S(2)}, u32[]{:S(2)}) collective-permute-start(bf16[1024,256]{1,0:T(8,128)(2,1)} %dynamic-slice_bitcast_fusion.3.refs_0_), channel_id=1, source_target_pairs={{0,32},{16,48},{32,0},{48,16},{64,96},{80,112},{96,64},{112,80},{1... | collective-permute-start | bytes 1572872 | tf_op jit(solution)/shard_map/ppermute | solution.py:227
  86.6 40.6 %collective-permute-start.8 = (bf16[1024,256]{1,0:T(8,128)(2,1)}, bf16[1024,256]{1,0:T(8,128)(2,1)}, u32[]{:S(2)}, u32[]{:S(2)}) collective-permute-start(bf16[1024,256]{1,0:T(8,128)(2,1)} %dynamic-slice_bitcast_fusion.3.refs_0_), channel_id=1, source_target_pairs={{0,48},{16,0},{32,16},{48,32},{64,112},{80,64},{96,80},{112,96},{1... | collective-permute-start | bytes 1572872 | tf_op jit(solution)/shard_map/ppermute | solution.py:227
  88.0 30.5 %collective-permute-start.10 = (bf16[3,384,128]{2,1,0:T(8,128)(2,1)}, bf16[3,384,128]{2,1,0:T(8,128)(2,1)S(1)}, u32[]{:S(2)}, u32[]{:S(2)}) collective-permute-start(bf16[3,384,128]{2,1,0:T(8,128)(2,1)} %get-tuple-element.18), channel_id=1, source_target_pairs={{0,2},{1,3},{2,4},{3,5},{4,6},{5,7},{6,8},{7,9},{8,10},{9,11},{10,... | collective-permute-start | bytes 884744 | tf_op jit(solution)/shard_map/ppermute | solution.py:231
  102.1 78.6 %copy-start.6 = (bf16[3,384,128]{2,1,0:T(8,128)(2,1)}, bf16[3,384,128]{2,1,0:T(8,128)(2,1)S(1)}, u32[]{:S(2)}) copy-start(bf16[3,384,128]{2,1,0:T(8,128)(2,1)S(1)} %collective-permute-done.9.refs_4_) | copy-start | bytes 884740
  102.2 18.2 %collective-permute-start.11 = (bf16[3,384,128]{2,1,0:T(8,128)(2,1)}, bf16[3,384,128]{2,1,0:T(8,128)(2,1)S(1)}, u32[]{:S(2)}, u32[]{:S(2)}) collective-permute-start(bf16[3,384,128]{2,1,0:T(8,128)(2,1)} %get-tuple-element.17), channel_id=1, source_target_pairs={{0,14},{1,15},{2,0},{3,1},{4,2},{5,3},{6,4},{7,5},{8,6},{9,7},{10,... | collective-permute-start | bytes 884744 | tf_op jit(solution)/shard_map/ppermute | solution.py:231
  118.5 62.3 %copy-start.8 = (bf16[3,384,128]{2,1,0:T(8,128)(2,1)}, bf16[3,384,128]{2,1,0:T(8,128)(2,1)S(1)}, u32[]{:S(2)}) copy-start(bf16[3,384,128]{2,1,0:T(8,128)(2,1)S(1)} %collective-permute-done.10.refs_5_) | copy-start | bytes 884740
  120.4 60.4 %copy-start.10 = (bf16[3,384,128]{2,1,0:T(8,128)(2,1)}, bf16[3,384,128]{2,1,0:T(8,128)(2,1)S(1)}, u32[]{:S(2)}) copy-start(bf16[3,384,128]{2,1,0:T(8,128)(2,1)S(1)} %collective-permute-done.11.refs_6_) | copy-start | bytes 884740
  131.9 59.8 %copy-start.47 = (s32[512]{0:T(512)S(1)}, s32[512]{0:T(512)}, u32[]{:S(2)}) copy-start(s32[512]{0:T(512)} %param.18) | copy-start | bytes 6148
  131.9 74.3 %copy-start.44 = (s32[512]{0:T(512)S(1)}, s32[512]{0:T(512)}, u32[]{:S(2)}) copy-start(s32[512]{0:T(512)} %param.19) | copy-start | bytes 6148
  131.9 74.6 %copy-start.48 = (bf16[1,256]{1,0:T(2,128)(2,1)S(1)}, bf16[1,256]{1,0:T(2,128)(2,1)}, u32[]{:S(2)}) copy-start(bf16[1,256]{1,0:T(2,128)(2,1)} %param.15) | copy-start | bytes 1540
  131.9 27.3 %collective-permute-start.15 = (bf16[3,384,128]{2,1,0:T(8,128)(2,1)}, bf16[3,384,128]{2,1,0:T(8,128)(2,1)S(1)}, u32[]{:S(2)}, u32[]{:S(2)}) collective-permute-start(bf16[3,384,128]{2,1,0:T(8,128)(2,1)} %get-tuple-element.16), channel_id=1, source_target_pairs={{0,9},{1,10},{2,11},{3,12},{4,13},{5,14},{6,15},{7,0},{8,1},{9,2},... | collective-permute-start | bytes 884744 | tf_op jit(solution)/shard_map/ppermute | solution.py:231
  137.9 33.2 %collective-permute-start.12 = (bf16[1024,256]{1,0:T(8,128)(2,1)}, bf16[1024,256]{1,0:T(8,128)(2,1)}, u32[]{:S(2)}, u32[]{:S(2)}) collective-permute-start(bf16[1024,256]{1,0:T(8,128)(2,1)} %dynamic-slice_bitcast_fusion.2.refs_4_), channel_id=1, source_target_pairs={{0,16},{16,32},{32,48},{48,0},{64,80},{80,96},{96,112},{112,64},{1... | collective-permute-start | bytes 1572872 | tf_op jit(solution)/shard_map/ppermute | solution.py:227
  139.9 33.7 %collective-permute-start.13 = (bf16[1024,256]{1,0:T(8,128)(2,1)}, bf16[1024,256]{1,0:T(8,128)(2,1)}, u32[]{:S(2)}, u32[]{:S(2)}) collective-permute-start(bf16[1024,256]{1,0:T(8,128)(2,1)} %dynamic-slice_bitcast_fusion.2.refs_4_), channel_id=1, source_target_pairs={{0,32},{16,48},{32,0},{48,16},{64,96},{80,112},{96,64},{112,80},{1... | collective-permute-start | bytes 1572872 | tf_op jit(solution)/shard_map/ppermute | solution.py:227
  143.0 33.1 %collective-permute-start.14 = (bf16[1024,256]{1,0:T(8,128)(2,1)}, bf16[1024,256]{1,0:T(8,128)(2,1)}, u32[]{:S(2)}, u32[]{:S(2)}) collective-permute-start(bf16[1024,256]{1,0:T(8,128)(2,1)} %dynamic-slice_bitcast_fusion.2.refs_4_), channel_id=1, source_target_pairs={{0,48},{16,0},{32,16},{48,32},{64,112},{80,64},{96,80},{112,96},{1... | collective-permute-start | bytes 1572872 | tf_op jit(solution)/shard_map/ppermute | solution.py:227
  144.3 20.7 %collective-permute-start.16 = (bf16[3,384,128]{2,1,0:T(8,128)(2,1)}, bf16[3,384,128]{2,1,0:T(8,128)(2,1)S(1)}, u32[]{:S(2)}, u32[]{:S(2)}) collective-permute-start(bf16[3,384,128]{2,1,0:T(8,128)(2,1)} %get-tuple-element.15), channel_id=1, source_target_pairs={{0,3},{1,4},{2,5},{3,6},{4,7},{5,8},{6,9},{7,10},{8,11},{9,12},{10... | collective-permute-start | bytes 884744 | tf_op jit(solution)/shard_map/ppermute | solution.py:231
  159.2 75.6 %copy-start.12 = (bf16[3,384,128]{2,1,0:T(8,128)(2,1)}, bf16[3,384,128]{2,1,0:T(8,128)(2,1)S(1)}, u32[]{:S(2)}) copy-start(bf16[3,384,128]{2,1,0:T(8,128)(2,1)S(1)} %collective-permute-done.15.refs_7_) | copy-start | bytes 884740
  159.2 10.1 %collective-permute-start.17 = (bf16[3,384,128]{2,1,0:T(8,128)(2,1)}, bf16[3,384,128]{2,1,0:T(8,128)(2,1)S(1)}, u32[]{:S(2)}, u32[]{:S(2)}) collective-permute-start(bf16[3,384,128]{2,1,0:T(8,128)(2,1)} %get-tuple-element.14), channel_id=1, source_target_pairs={{0,13},{1,14},{2,15},{3,0},{4,1},{5,2},{6,3},{7,4},{8,5},{9,6},{10... | collective-permute-start | bytes 884744 | tf_op jit(solution)/shard_map/ppermute | solution.py:231
  165.0 69.8 %copy-start.14 = (bf16[3,384,128]{2,1,0:T(8,128)(2,1)}, bf16[3,384,128]{2,1,0:T(8,128)(2,1)S(1)}, u32[]{:S(2)}) copy-start(bf16[3,384,128]{2,1,0:T(8,128)(2,1)S(1)} %collective-permute-done.16.refs_8_) | copy-start | bytes 884740
  169.3 65.5 %copy-start.16 = (bf16[3,384,128]{2,1,0:T(8,128)(2,1)}, bf16[3,384,128]{2,1,0:T(8,128)(2,1)S(1)}, u32[]{:S(2)}) copy-start(bf16[3,384,128]{2,1,0:T(8,128)(2,1)S(1)} %collective-permute-done.17.refs_9_) | copy-start | bytes 884740
  180.8 21.6 %collective-permute-start.21 = (bf16[3,384,128]{2,1,0:T(8,128)(2,1)}, bf16[3,384,128]{2,1,0:T(8,128)(2,1)S(1)}, u32[]{:S(2)}, u32[]{:S(2)}) collective-permute-start(bf16[3,384,128]{2,1,0:T(8,128)(2,1)} %get-tuple-element.13), channel_id=1, source_target_pairs={{0,6},{1,7},{2,8},{3,9},{4,10},{5,11},{6,12},{7,13},{8,14},{9,15},... | collective-permute-start | bytes 884744 | tf_op jit(solution)/shard_map/ppermute | solution.py:231
  185.9 98.6 %copy-start.31 = (bf16[1024,256]{1,0:T(8,128)(2,1)}, bf16[1024,256]{1,0:T(8,128)(2,1)S(1)}, u32[]{:S(2)}) copy-start(bf16[1024,256]{1,0:T(8,128)(2,1)S(1)} %dynamic-slice_bitcast_fusion.1.refs_8_) | copy-start | bytes 1572868
  185.9 40.4 %collective-permute-start.18 = (bf16[1024,256]{1,0:T(8,128)(2,1)S(1)}, bf16[1024,256]{1,0:T(8,128)(2,1)S(1)}, u32[]{:S(2)}, u32[]{:S(2)}) collective-permute-start(bf16[1024,256]{1,0:T(8,128)(2,1)S(1)} %dynamic-slice_bitcast_fusion.1.refs_8_), channel_id=1, source_target_pairs={{0,16},{16,32},{32,48},{48,0},{64,80},{80,96},{96,112},{112,64},{1... | collective-permute-start | bytes 1572872 | tf_op jit(solution)/shard_map/ppermute | solution.py:227
  187.5 40.7 %collective-permute-start.19 = (bf16[1024,256]{1,0:T(8,128)(2,1)S(1)}, bf16[1024,256]{1,0:T(8,128)(2,1)S(1)}, u32[]{:S(2)}, u32[]{:S(2)}) collective-permute-start(bf16[1024,256]{1,0:T(8,128)(2,1)S(1)} %dynamic-slice_bitcast_fusion.1.refs_8_), channel_id=1, source_target_pairs={{0,32},{16,48},{32,0},{48,16},{64,96},{80,112},{96,64},{112,80},{1... | collective-permute-start | bytes 1572872 | tf_op jit(solution)/shard_map/ppermute | solution.py:227
  190.2 39.9 %collective-permute-start.20 = (bf16[1024,256]{1,0:T(8,128)(2,1)S(1)}, bf16[1024,256]{1,0:T(8,128)(2,1)}, u32[]{:S(2)}, u32[]{:S(2)}) collective-permute-start(bf16[1024,256]{1,0:T(8,128)(2,1)S(1)} %dynamic-slice_bitcast_fusion.1.refs_8_), channel_id=1, source_target_pairs={{0,48},{16,0},{32,16},{48,32},{64,112},{80,64},{96,80},{112,96},{1... | collective-permute-start | bytes 1572872 | tf_op jit(solution)/shard_map/ppermute | solution.py:227
  191.7 23.3 %collective-permute-start.22 = (bf16[3,384,128]{2,1,0:T(8,128)(2,1)}, bf16[3,384,128]{2,1,0:T(8,128)(2,1)S(1)}, u32[]{:S(2)}, u32[]{:S(2)}) collective-permute-start(bf16[3,384,128]{2,1,0:T(8,128)(2,1)} %get-tuple-element.12), channel_id=1, source_target_pairs={{0,4},{1,5},{2,6},{3,7},{4,8},{5,9},{6,10},{7,11},{8,12},{9,13},{1... | collective-permute-start | bytes 884744 | tf_op jit(solution)/shard_map/ppermute | solution.py:231
  202.3 82.1 %copy-start.18 = (bf16[3,384,128]{2,1,0:T(8,128)(2,1)}, bf16[3,384,128]{2,1,0:T(8,128)(2,1)S(1)}, u32[]{:S(2)}) copy-start(bf16[3,384,128]{2,1,0:T(8,128)(2,1)S(1)} %collective-permute-done.21.refs_10_) | copy-start | bytes 884740
  202.3 22.1 %collective-permute-start.23 = (bf16[3,384,128]{2,1,0:T(8,128)(2,1)}, bf16[3,384,128]{2,1,0:T(8,128)(2,1)S(1)}, u32[]{:S(2)}, u32[]{:S(2)}) collective-permute-start(bf16[3,384,128]{2,1,0:T(8,128)(2,1)} %get-tuple-element.11), channel_id=1, source_target_pairs={{0,12},{1,13},{2,14},{3,15},{4,0},{5,1},{6,2},{7,3},{8,4},{9,5},{1... | collective-permute-start | bytes 884744 | tf_op jit(solution)/shard_map/ppermute | solution.py:231
  214.9 69.5 %copy-start.20 = (bf16[3,384,128]{2,1,0:T(8,128)(2,1)}, bf16[3,384,128]{2,1,0:T(8,128)(2,1)S(1)}, u32[]{:S(2)}) copy-start(bf16[3,384,128]{2,1,0:T(8,128)(2,1)S(1)} %collective-permute-done.22.refs_11_) | copy-start | bytes 884740
  224.5 60.0 %copy-start.22 = (bf16[3,384,128]{2,1,0:T(8,128)(2,1)}, bf16[3,384,128]{2,1,0:T(8,128)(2,1)S(1)}, u32[]{:S(2)}) copy-start(bf16[3,384,128]{2,1,0:T(8,128)(2,1)S(1)} %collective-permute-done.23.refs_12_) | copy-start | bytes 884740
  226.3 8.6 %copy-start.35 = (bf16[1024,256]{1,0:T(8,128)(2,1)}, bf16[1024,256]{1,0:T(8,128)(2,1)S(1)}, u32[]{:S(2)}) copy-start(bf16[1024,256]{1,0:T(8,128)(2,1)S(1)} %collective-permute-done.18.refs_9_) | copy-start | bytes 1572868
  228.2 4.4 %copy-start.36 = (bf16[1024,256]{1,0:T(8,128)(2,1)}, bf16[1024,256]{1,0:T(8,128)(2,1)S(1)}, u32[]{:S(2)}) copy-start(bf16[1024,256]{1,0:T(8,128)(2,1)S(1)} %collective-permute-done.19.refs_10_) | copy-start | bytes 1572868
  234.8 24.8 %collective-permute-start.27 = (bf16[3,384,128]{2,1,0:T(8,128)(2,1)}, bf16[3,384,128]{2,1,0:T(8,128)(2,1)S(1)}, u32[]{:S(2)}, u32[]{:S(2)}) collective-permute-start(bf16[3,384,128]{2,1,0:T(8,128)(2,1)} %get-tuple-element.10), channel_id=1, source_target_pairs={{0,10},{1,11},{2,12},{3,13},{4,14},{5,15},{6,0},{7,1},{8,2},{9,3},... | collective-permute-start | bytes 884744 | tf_op jit(solution)/shard_map/ppermute | solution.py:231
  236.0 48.5 %copy-start.32 = (bf16[1024,256]{1,0:T(8,128)(2,1)}, bf16[1024,256]{1,0:T(8,128)(2,1)S(1)}, u32[]{:S(2)}) copy-start(bf16[1024,256]{1,0:T(8,128)(2,1)S(1)} %dynamic-slice_bitcast_fusion.refs_12_) | copy-start | bytes 1572868
  236.0 42.7 %collective-permute-start.24 = (bf16[1024,256]{1,0:T(8,128)(2,1)S(1)}, bf16[1024,256]{1,0:T(8,128)(2,1)S(1)}, u32[]{:S(2)}, u32[]{:S(2)}) collective-permute-start(bf16[1024,256]{1,0:T(8,128)(2,1)S(1)} %dynamic-slice_bitcast_fusion.refs_12_), channel_id=1, source_target_pairs={{0,16},{16,32},{32,48},{48,0},{64,80},{80,96},{96,112},{112,64},{1... | collective-permute-start | bytes 1572872 | tf_op jit(solution)/shard_map/ppermute | solution.py:227
  238.1 42.5 %collective-permute-start.25 = (bf16[1024,256]{1,0:T(8,128)(2,1)S(1)}, bf16[1024,256]{1,0:T(8,128)(2,1)S(1)}, u32[]{:S(2)}, u32[]{:S(2)}) collective-permute-start(bf16[1024,256]{1,0:T(8,128)(2,1)S(1)} %dynamic-slice_bitcast_fusion.refs_12_), channel_id=1, source_target_pairs={{0,32},{16,48},{32,0},{48,16},{64,96},{80,112},{96,64},{112,80},{1... | collective-permute-start | bytes 1572872 | tf_op jit(solution)/shard_map/ppermute | solution.py:227
  240.2 42.3 %collective-permute-start.26 = (bf16[1024,256]{1,0:T(8,128)(2,1)S(1)}, bf16[1024,256]{1,0:T(8,128)(2,1)S(1)}, u32[]{:S(2)}, u32[]{:S(2)}) collective-permute-start(bf16[1024,256]{1,0:T(8,128)(2,1)S(1)} %dynamic-slice_bitcast_fusion.refs_12_), channel_id=1, source_target_pairs={{0,48},{16,0},{32,16},{48,32},{64,112},{80,64},{96,80},{112,96},{1... | collective-permute-start | bytes 1572872 | tf_op jit(solution)/shard_map/ppermute | solution.py:227
  241.5 20.8 %collective-permute-start.28 = (bf16[3,384,128]{2,1,0:T(8,128)(2,1)}, bf16[3,384,128]{2,1,0:T(8,128)(2,1)S(1)}, u32[]{:S(2)}, u32[]{:S(2)}) collective-permute-start(bf16[3,384,128]{2,1,0:T(8,128)(2,1)} %get-tuple-element.9), channel_id=1, source_target_pairs={{0,5},{1,6},{2,7},{3,8},{4,9},{5,10},{6,11},{7,12},{8,13},{9,14},{... | collective-permute-start | bytes 884744 | tf_op jit(solution)/shard_map/ppermute | solution.py:231
  259.7 16.5 %collective-permute-start.29 = (bf16[3,384,128]{2,1,0:T(8,128)(2,1)S(1)}, bf16[3,384,128]{2,1,0:T(8,128)(2,1)S(1)}, u32[]{:S(2)}, u32[]{:S(2)}) collective-permute-start(bf16[3,384,128]{2,1,0:T(8,128)(2,1)S(1)} %get-tuple-element.8), channel_id=1, source_target_pairs={{0,11},{1,12},{2,13},{3,14},{4,15},{5,0},{6,1},{7,2},{8,3},{9,4},{... | collective-permute-start | bytes 884744 | tf_op jit(solution)/shard_map/ppermute | solution.py:231
  278.7 3.8 %copy-start.37 = (bf16[1024,256]{1,0:T(8,128)(2,1)}, bf16[1024,256]{1,0:T(8,128)(2,1)S(1)}, u32[]{:S(2)}) copy-start(bf16[1024,256]{1,0:T(8,128)(2,1)S(1)} %collective-permute-done.24.refs_13_) | copy-start | bytes 1572868
  280.6 2.5 copy-start.38
  282.5 1.9 copy-start.39
  284.5 1.0 copy-start.1
  285.5 1.0 copy-start.3
  300.8 18.7 %copy-start.46 = (bf16[1024]{0:T(1024)(128)(2,1)S(1)}, bf16[1024]{0:T(1024)(128)(2,1)}, u32[]{:S(2)}) copy-start(bf16[1024]{0:T(1024)(128)(2,1)} %param.17) | copy-start | bytes 6148
  313.5 14.2 %all-to-all-start = ((bf16[16,24,256]{2,1,0:T(8,128)(2,1)}), bf16[16,24,256]{2,1,0:T(8,128)(2,1)S(1)}, u32[]{:S(2)}, u32[]{:S(2)}) async-start(bf16[16,24,256]{2,1,0:T(8,128)(2,1)} %bitcast.57), calls=%async_computation | async-start | bytes 393216 | tf_op jit(solution)/shard_map/all_to_all | solution.py:278
  (17 other events, 15.3 us)
Sparse Core Ops, SparseCore 0:
  9.2 158.3 all-gather.2

commit v9 on v7

--- a/solution.py
+++ b/solution.py
@@ -26,7 +26,7 @@
 
 
 QUARTERS = 4
-BACK = (0, 1, 15, 2, 14, 3, 13, 4, 12, 5, 11, 6, 10, 7, 9, 8)
+BACK = (0, 1, 7, 2, 6, 3, 5, 4)
 
 
 def pack_kernel(down, up, comp, over, out, sems):
@@ -47,8 +47,10 @@
     pieces, (base, sem) = refs[:-2], refs[-2:]
     shards, slot_most = len(pieces), pieces[0].shape[0]
     me = places[shards * slot_most]
+    z, core = me // 2, lax.rem(me, 2)
     for k in range(shards):
-        owner = lax.rem(me + shards - BACK[k], shards)
+        plane = lax.rem(z + 8 - BACK[k // 2], 8)
+        owner = 2 * plane + (core if k % 2 == 0 else 1 - core)
         for slot in range(slot_most):
             place = places[owner * slot_most + slot]
 
@@ -161,42 +163,47 @@
     columns = over_weight.shape[1]
     outputs = columns * shards
 
+    anywhere = pl.BlockSpec(memory_space=pl.ANY)
+
+    def whole(*shape):
+        return pl.BlockSpec(shape, lambda i, *_: (0,) * len(shape))
+
     parts = (
         cross_down[0].reshape(layers * step, rank),
         cross_up[0].reshape(layers * rank, step),
         comp_weight[0],
         over_weight.T,
     )
+    packed_rows = sum(part.size for part in parts) // step
     packed = pl.pallas_call(
         pack_kernel,
-        in_specs=[pl.BlockSpec(memory_space=pl.ANY)] * len(parts),
-        out_specs=pl.BlockSpec(memory_space=pl.ANY),
+        grid=(1,),
+        in_specs=[anywhere] * len(parts),
+        out_specs=whole(packed_rows, step),
         scratch_shapes=[pltpu.SemaphoreType.DMA((len(parts) + 1,))],
-        out_shape=jax.ShapeDtypeStruct((sum(p.size for p in parts) // step, step), BF16),
+        out_shape=jax.ShapeDtypeStruct((packed_rows, step), BF16),
         compiler_params=pltpu.CompilerParams(vmem_limit_bytes=58 * 2**20),
     )(*parts)
     weights = lax.all_gather(packed, "shard", axis=0)
 
-    by_slot = pooled[0].transpose(1, 0, 2).reshape(slot_most, shards, samples, emb)
-
-    def piece_for(to):
-        return lax.dynamic_index_in_dim(by_slot, to % 16, 1, keepdims=False)
-
-    pieces = [piece_for(shard)]
-    for k in BACK[1:]:
-        moves = [(i, (i + k) % 16) for i in range(16)]
-        pieces.append(lax.ppermute(piece_for(shard + k), "shard", moves))
+    z, core = shard // 2, shard % 2
+    by_slot = pooled[0].transpose(1, 0, 2).reshape(slot_most, 8, 2, samples, emb)
+    swap = [(i, i ^ 1) for i in range(16)]
+    pieces = []
+    for k in BACK:
+        both = lax.dynamic_index_in_dim(by_slot, (z + k) % 8, 1, keepdims=False)
+        if k:
+            moves = [(i, (i + 2 * k) % 16) for i in range(16)]
+            both = lax.ppermute(both, "shard", moves)
+        pieces.append(lax.dynamic_index_in_dim(both, core, 1, keepdims=False))
+        theirs = lax.dynamic_index_in_dim(both, 1 - core, 1, keepdims=False)
+        pieces.append(lax.ppermute(theirs, "shard", swap))
 
     slots = slot_order(table_tower, table_owner, tower_id, features // emb, slot_most)
     index = jnp.arange(shards * slot_most, dtype=jnp.int32)[:, None]
     turn = jnp.arange(1, slots.shape[0] + 1, dtype=jnp.int32)[None, :]
     places = jnp.sum(jnp.where(slots[None, :] == index, turn, 0), axis=1) - 1
     places = jnp.concatenate([places, shard[None]]).astype(jnp.int32)
-
-    anywhere = pl.BlockSpec(memory_space=pl.ANY)
-
-    def whole(*shape):
-        return pl.BlockSpec(shape, lambda i, *_: (0,) * len(shape))
 
     tables = pl.pallas_call(
         table_kernel,
@@ -231,7 +238,7 @@
             ],
         ),
         out_shape=jax.ShapeDtypeStruct((samples, outputs), BF16),
-        compiler_params=pltpu.CompilerParams(vmem_limit_bytes=58 * 2**20),
+        compiler_params=pltpu.CompilerParams(vmem_limit_bytes=36 * 2**20),
         cost_estimate=pl.CostEstimate(flops=8 * 10**9, bytes_accessed=24 * 10**6, transcendentals=0),
     )(tables, weights, cross_bias[0].astype(F32), comp_bias.astype(F32))
 

time: 295 us -> 258 us (0.87)
  Pallas kernels: 54.2 us -> 16.5 us
  starting transfers between devices: 40 us -> 22.9 us
  waiting for transfers between devices: 178 us -> 190 us
  local copies, waits for them, and re-layouts: 6.11 us -> 12.1 us
    pallas_call x1, Pallas kernels: 37.9 us -> 2.29 us  [on_device(): pl.pallas_call(pack_kernel, grid=(1,), in_specs=[anywhere] * len(parts),...]
    ppermute x15, starting transfers between devices: 32.9 us -> 15.9 us  [the longest x7 14 us: on_device(): both = lax.ppermute(both, 'shard', moves)]
    ppermute x15, waiting for transfers between devices: 122 us -> 136 us  [the longest x7 134 us: on_device(): both = lax.ppermute(both, 'shard', moves)]
    dynamic_slice x0 -> x8, local copies, waits for them, and re-layouts: none -> 4.51 us  [on_device(): both = lax.dynamic_index_in_dim(by_slot, (z + k) % 8, 1, keepdims=False)]
    squeeze x1 -> x8, local copies, waits for them, and re-layouts: 4.41 us -> 6.65 us  [on_device(): theirs = lax.dynamic_index_in_dim(both, 1 - core, 1, keepdims=False)]
  transfers between devices with their start and end apart: 17 -> 17, of which waited for: 10 -> 12; matrix products, arithmetic and copies ran while one was open for 2% -> 5% of each run, Pallas kernels for 1% -> 1%
where the time goes in v9:
time: 258 us
  waiting for transfers between devices  190 us (74%)
  starting transfers between devices  22.9 us (9%)
  Pallas kernels  16.5 us (6%)
  between operations  13.9 us (5%)
  local copies, waits for them, and re-layouts  12.1 us (5%)
    ppermute x7, waiting for transfers between devices, on_device(): both = lax.ppermute(both, 'shard', moves)  134 us
    all_gather x1, waiting for transfers between devices, on_device(): weights = lax.all_gather(packed, 'shard', axis=0)  38.8 us
    all_to_all x1, waiting for transfers between devices, on_device(): lax.all_to_all(partial.reshape(towers, samples // towers, outputs), 'towe...  15 us
    ppermute x7, starting transfers between devices, on_device(): both = lax.ppermute(both, 'shard', moves)  14 us
    pallas_call x1, Pallas kernels, on_device(): pl.pallas_call(tower_kernel, grid_spec=pl.GridSpec(grid=(1,), in_specs=[a...  12.4 us
    all_to_all x1, starting transfers between devices, on_device(): lax.all_to_all(partial.reshape(towers, samples // towers, outputs), 'towe...  7.04 us
    squeeze x8, local copies, waits for them, and re-layouts, on_device(): theirs = lax.dynamic_index_in_dim(both, 1 - core, 1, keepdims=False)  6.65 us
  transfers between devices with their start and end apart: 17, of which 12 were waited for; matrix products, arithmetic and copies ran while one was open for 5% of the time, Pallas kernels for 1%

profile of v9, /device:TPU:96, one launch (start us, length us, event | category | flops | bytes accessed | tf_op | source)
XLA Modules:
  0.0 257.6 jit_solution(13504922979806277979)
XLA Ops:
  6.5 0.0 all-gather.3.cloned.1.call-start
  6.5 2.3 shard_map.101
  8.8 0.0 all-gather.3.cloned.1.call-update
  9.0 2.6 constant_dynamic-slice_fusion
  11.6 0.0 copy-start.4
  11.6 0.0 copy-start.3
  11.6 0.0 copy-start.1
  11.6 0.9 copy.40
  12.5 4.0 %collective-permute-start.9 = (bf16[3,2,384,128]{3,2,0,1:T(8,128)(2,1)}, bf16[3,2,384,128]{3,2,0,1:T(8,128)(2,1)}, u32[]{:S(2)}, u32[]{:S(2)}) collective-permute-start(bf16[3,2,384,128]{3,2,0,1:T(8,128)(2,1)} %bitcast.73), channel_id=1, source_target_pairs={{0,6},{1,7},{2,8},{3,9},{4,10},{5,11},{6,12},{7,13},{8,14},{9,15},... | collective-permute-start | bytes 1769480 | tf_op jit(solution)/shard_map/ppermute | solution.py:197
  16.6 0.1 collective-permute-start.11
  16.7 4.3 %collective-permute-start.13 = (bf16[3,2,384,128]{3,2,0,1:T(8,128)(2,1)S(1)}, bf16[3,2,384,128]{3,2,0,1:T(8,128)(2,1)}, u32[]{:S(2)}, u32[]{:S(2)}) collective-permute-start(bf16[3,2,384,128]{3,2,0,1:T(8,128)(2,1)S(1)} %bitcast.83), channel_id=1, source_target_pairs={{0,8},{1,9},{2,10},{3,11},{4,12},{5,13},{6,14},{7,15},{8,0},{9,1},... | collective-permute-start | bytes 1769480 | tf_op jit(solution)/shard_map/ppermute | solution.py:197
  21.1 2.3 collective-permute-start.3
  23.4 0.1 collective-permute-start.5
  23.6 0.9 copy.41
  24.5 0.0 copy-done.4
  24.5 0.0 copy-done.3
  24.6 0.0 copy-done.1
  24.6 0.3 convert_reduce_fusion.2
  24.9 0.7 bitcast_convert_fusion.bias
  25.6 1.1 dynamic-slice_bitcast_fusion.14
  26.7 0.1 select_reduce_fusion
  26.9 0.1 select_reduce_fusion.1
  27.0 40.6 %collective-permute-done.9 = bf16[3,2,384,128]{3,2,0,1:T(8,128)(2,1)} collective-permute-done((bf16[3,2,384,128]{3,2,0,1:T(8,128)(2,1)}, bf16[3,2,384,128]{3,2,0,1:T(8,128)(2,1)}, u32[]{:S(2)}, u32[]{:S(2)}) %collective-permute-start.9) | collective-permute-done | bytes 589856 | tf_op jit(solution)/shard_map/ppermute | solution.py:197
  67.6 2.3 collective-permute-start.7
  69.9 1.1 dynamic-slice_bitcast_fusion.4
  71.0 3.5 %collective-permute-done.11 = bf16[3,2,384,128]{3,2,0,1:T(8,128)(2,1)} collective-permute-done((bf16[3,2,384,128]{3,2,0,1:T(8,128)(2,1)S(1)}, bf16[3,2,384,128]{3,2,0,1:T(8,128)(2,1)}, u32[]{:S(2)}, u32[]{:S(2)}) %collective-permute-start.11) | collective-permute-done | bytes 589856 | tf_op jit(solution)/shard_map/ppermute | solution.py:197
  74.4 0.9 collective-permute-start.1
  75.3 1.1 dynamic-slice_bitcast_fusion.2
  76.4 32.8 %collective-permute-done.13 = bf16[3,2,384,128]{3,2,0,1:T(8,128)(2,1)} collective-permute-done((bf16[3,2,384,128]{3,2,0,1:T(8,128)(2,1)S(1)}, bf16[3,2,384,128]{3,2,0,1:T(8,128)(2,1)}, u32[]{:S(2)}, u32[]{:S(2)}) %collective-permute-start.13) | collective-permute-done | bytes 589856 | tf_op jit(solution)/shard_map/ppermute | solution.py:197
  109.2 0.0 collective-permute-start
  109.2 1.1 dynamic-slice_bitcast_fusion
  110.3 26.0 %collective-permute-done.3 = bf16[3,2,384,128]{3,2,0,1:T(8,128)(2,1)} collective-permute-done((bf16[3,2,384,128]{3,2,0,1:T(8,128)(2,1)S(1)}, bf16[3,2,384,128]{3,2,0,1:T(8,128)(2,1)}, u32[]{:S(2)}, u32[]{:S(2)}) %collective-permute-start.3) | collective-permute-done | bytes 589856 | tf_op jit(solution)/shard_map/ppermute | solution.py:197
  136.3 0.0 collective-permute-start.10
  136.3 1.1 dynamic-slice_bitcast_fusion.10
  137.4 0.0 collective-permute-done.5
  137.5 0.6 collective-permute-start.12
  138.0 1.1 dynamic-slice_bitcast_fusion.8
  139.2 31.2 %collective-permute-done.7 = bf16[3,2,384,128]{3,2,0,1:T(8,128)(2,1)S(1)} collective-permute-done((bf16[3,2,384,128]{3,2,0,1:T(8,128)(2,1)}, bf16[3,2,384,128]{3,2,0,1:T(8,128)(2,1)S(1)}, u32[]{:S(2)}, u32[]{:S(2)}) %collective-permute-start.7) | collective-permute-done | bytes 589856 | tf_op jit(solution)/shard_map/ppermute | solution.py:197
  170.3 0.0 collective-permute-start.14
  170.4 0.0 collective-permute-done.1
  170.4 0.6 collective-permute-start.4
  171.0 0.0 collective-permute-done.refs_1_
  171.0 0.1 collective-permute-start.6
  171.1 0.0 collective-permute-done.10.refs_11_
  171.1 0.5 collective-permute-start.8
  171.6 0.0 collective-permute-done.12.refs_13_
  171.6 0.1 collective-permute-start.2
  171.7 0.1 pad_add_fusion.places
  171.8 0.1 collective-permute-done.14.refs_15_
  171.9 0.8 collective-permute-done.4.refs_5_
  172.8 0.4 collective-permute-done.6.refs_7_
  173.2 0.4 collective-permute-done.8.refs_9_
  173.6 0.4 collective-permute-done.2.refs_3_
  174.0 1.8 shard_map.100.tables
  175.9 38.8 %all-gather.3.cloned.1.call-done = bf16[37888,256]{1,0:T(8,128)(2,1)} async-done(((bf16[2368,256]{1,0:T(8,128)(2,1)}), bf16[37888,256]{1,0:T(8,128)(2,1)}) %all-gather.3.cloned.1.call-update) | async-done | bytes 19398672 | tf_op jit(solution)/shard_map/all_gather | solution.py:187
  214.7 0.0 copy-start.2
  214.7 12.4 %shard_map.102 = bf16[384,1024]{1,0:T(8,128)(2,1)S(1)} custom-call(bf16[384,4096]{1,0:T(8,128)(2,1)S(1)} %shard_map.100.tables, bf16[16,2368,256]{2,1,0:T(8,128)(2,1)} %bitcast.91, f32[2,4096]{1,0:T(2,128)S(1)} %bitcast_convert_fusion.bias, f32[1,256]{1,0:T(1,128)S(1)} %convert_element_type.34.comp_bias), custom_call_target="tpu_custom_call" | custom-call | flops 8000000000 | bytes 24000000 | tf_op jit(solution)/shard_map/pallas_call | solution.py:222
  227.1 0.0 copy-start
  227.1 0.9 copy-done
  227.9 7.0 %all-to-all-start = ((bf16[16,24,1024]{2,1,0:T(8,128)(2,1)}), bf16[16,24,1024]{2,1,0:T(8,128)(2,1)S(1)}, u32[]{:S(2)}, u32[]{:S(2)}) async-start(bf16[16,24,1024]{2,1,0:T(8,128)(2,1)} %bitcast.78), calls=%async_computation | async-start | bytes 1572864 | tf_op jit(solution)/shard_map/all_to_all | solution.py:245
  235.0 0.0 copy-done.2
  235.0 15.0 %all-to-all-done = bf16[16,24,1024]{2,1,0:T(8,128)(2,1)S(1)} async-done(((bf16[16,24,1024]{2,1,0:T(8,128)(2,1)}), bf16[16,24,1024]{2,1,0:T(8,128)(2,1)S(1)}, u32[]{:S(2)}, u32[]{:S(2)}) %all-to-all-start) | async-done | bytes 786464 | tf_op jit(solution)/shard_map/all_to_all | solution.py:245
  250.0 0.1 convert_reduce_fusion
  250.1 0.6 fusion.3
  (13 shorter events, 0.3 us)
Async XLA Ops:
  6.5 208.1 %all-gather.3.cloned.1.call-start = ((), (), s32[]{:S(2)}) async-start(), calls=%async_computation.1 | async-start | bytes 20611072 | tf_op jit(solution)/shard_map/all_gather | solution.py:187
  11.6 12.9 %copy-start.4 = (bf16[1,256]{1,0:T(2,128)(2,1)S(1)}, bf16[1,256]{1,0:T(2,128)(2,1)}, u32[]{:S(2)}) copy-start(bf16[1,256]{1,0:T(2,128)(2,1)} %param.15) | copy-start | bytes 1540
  11.6 13.0 %copy-start.3 = (s32[512]{0:T(512)S(1)}, s32[512]{0:T(512)}, u32[]{:S(2)}) copy-start(s32[512]{0:T(512)} %param.18) | copy-start | bytes 6148
  11.6 13.0 %copy-start.1 = (s32[512]{0:T(512)S(1)}, s32[512]{0:T(512)}, u32[]{:S(2)}) copy-start(s32[512]{0:T(512)} %param.19) | copy-start | bytes 6148
  12.5 55.1 %collective-permute-start.9 = (bf16[3,2,384,128]{3,2,0,1:T(8,128)(2,1)}, bf16[3,2,384,128]{3,2,0,1:T(8,128)(2,1)}, u32[]{:S(2)}, u32[]{:S(2)}) collective-permute-start(bf16[3,2,384,128]{3,2,0,1:T(8,128)(2,1)} %bitcast.73), channel_id=1, source_target_pairs={{0,6},{1,7},{2,8},{3,9},{4,10},{5,11},{6,12},{7,13},{8,14},{9,15},... | collective-permute-start | bytes 1769480 | tf_op jit(solution)/shard_map/ppermute | solution.py:197
  16.6 57.9 %collective-permute-start.11 = (bf16[3,2,384,128]{3,2,0,1:T(8,128)(2,1)S(1)}, bf16[3,2,384,128]{3,2,0,1:T(8,128)(2,1)}, u32[]{:S(2)}, u32[]{:S(2)}) collective-permute-start(bf16[3,2,384,128]{3,2,0,1:T(8,128)(2,1)S(1)} %bitcast.84), channel_id=1, source_target_pairs={{0,10},{1,11},{2,12},{3,13},{4,14},{5,15},{6,0},{7,1},{8,2},{9,3},... | collective-permute-start | bytes 1769480 | tf_op jit(solution)/shard_map/ppermute | solution.py:197
  16.7 92.5 %collective-permute-start.13 = (bf16[3,2,384,128]{3,2,0,1:T(8,128)(2,1)S(1)}, bf16[3,2,384,128]{3,2,0,1:T(8,128)(2,1)}, u32[]{:S(2)}, u32[]{:S(2)}) collective-permute-start(bf16[3,2,384,128]{3,2,0,1:T(8,128)(2,1)S(1)} %bitcast.83), channel_id=1, source_target_pairs={{0,8},{1,9},{2,10},{3,11},{4,12},{5,13},{6,14},{7,15},{8,0},{9,1},... | collective-permute-start | bytes 1769480 | tf_op jit(solution)/shard_map/ppermute | solution.py:197
  21.1 115.3 %collective-permute-start.3 = (bf16[3,2,384,128]{3,2,0,1:T(8,128)(2,1)S(1)}, bf16[3,2,384,128]{3,2,0,1:T(8,128)(2,1)}, u32[]{:S(2)}, u32[]{:S(2)}) collective-permute-start(bf16[3,2,384,128]{3,2,0,1:T(8,128)(2,1)S(1)} %bitcast.82), channel_id=1, source_target_pairs={{0,14},{1,15},{2,0},{3,1},{4,2},{5,3},{6,4},{7,5},{8,6},{9,7},{10,... | collective-permute-start | bytes 1769480 | tf_op jit(solution)/shard_map/ppermute | solution.py:197
  23.4 114.0 %collective-permute-start.5 = (bf16[3,2,384,128]{3,2,0,1:T(8,128)(2,1)S(1)}, bf16[3,2,384,128]{3,2,0,1:T(8,128)(2,1)}, u32[]{:S(2)}, u32[]{:S(2)}) collective-permute-start(bf16[3,2,384,128]{3,2,0,1:T(8,128)(2,1)S(1)} %bitcast.81), channel_id=1, source_target_pairs={{0,4},{1,5},{2,6},{3,7},{4,8},{5,9},{6,10},{7,11},{8,12},{9,13},{1... | collective-permute-start | bytes 1769480 | tf_op jit(solution)/shard_map/ppermute | solution.py:197
  67.6 102.7 %collective-permute-start.7 = (bf16[3,2,384,128]{3,2,0,1:T(8,128)(2,1)}, bf16[3,2,384,128]{3,2,0,1:T(8,128)(2,1)S(1)}, u32[]{:S(2)}, u32[]{:S(2)}) collective-permute-start(bf16[3,2,384,128]{3,2,0,1:T(8,128)(2,1)} %bitcast.86), channel_id=1, source_target_pairs={{0,12},{1,13},{2,14},{3,15},{4,0},{5,1},{6,2},{7,3},{8,4},{9,5},{1... | collective-permute-start | bytes 1769480 | tf_op jit(solution)/shard_map/ppermute | solution.py:197
  74.4 95.9 %collective-permute-start.1 = (bf16[3,2,384,128]{3,2,0,1:T(8,128)(2,1)S(1)}, bf16[3,2,384,128]{3,2,0,1:T(8,128)(2,1)S(1)}, u32[]{:S(2)}, u32[]{:S(2)}) collective-permute-start(bf16[3,2,384,128]{3,2,0,1:T(8,128)(2,1)S(1)} %bitcast.85), channel_id=1, source_target_pairs={{0,2},{1,3},{2,4},{3,5},{4,6},{5,7},{6,8},{7,9},{8,10},{9,11},{10,... | collective-permute-start | bytes 1769480 | tf_op jit(solution)/shard_map/ppermute | solution.py:197
  109.2 61.8 %collective-permute-start = (bf16[3,384,128]{2,1,0:T(8,128)(2,1)S(1)}, bf16[3,384,128]{2,1,0:T(8,128)(2,1)S(1)}, u32[]{:S(2)}, u32[]{:S(2)}) collective-permute-start(bf16[3,384,128]{2,1,0:T(8,128)(2,1)S(1)} %get-tuple-element.14), channel_id=1, source_target_pairs={{0,1},{1,0},{2,3},{3,2},{4,5},{5,4},{6,7},{7,6},{8,9},{9,8},{10,11... | collective-permute-start | bytes 884744 | tf_op jit(solution)/shard_map/ppermute | solution.py:200
  136.3 34.8 %collective-permute-start.10 = (bf16[3,384,128]{2,1,0:T(8,128)(2,1)S(1)}, bf16[3,384,128]{2,1,0:T(8,128)(2,1)S(1)}, u32[]{:S(2)}, u32[]{:S(2)}) collective-permute-start(bf16[3,384,128]{2,1,0:T(8,128)(2,1)S(1)} %get-tuple-element.20), channel_id=1, source_target_pairs={{0,1},{1,0},{2,3},{3,2},{4,5},{5,4},{6,7},{7,6},{8,9},{9,8},{10,11... | collective-permute-start | bytes 884744 | tf_op jit(solution)/shard_map/ppermute | solution.py:200
  137.5 34.2 %collective-permute-start.12 = (bf16[3,384,128]{2,1,0:T(8,128)(2,1)S(1)}, bf16[3,384,128]{2,1,0:T(8,128)(2,1)S(1)}, u32[]{:S(2)}, u32[]{:S(2)}) collective-permute-start(bf16[3,384,128]{2,1,0:T(8,128)(2,1)S(1)} %get-tuple-element.18), channel_id=1, source_target_pairs={{0,1},{1,0},{2,3},{3,2},{4,5},{5,4},{6,7},{7,6},{8,9},{9,8},{10,11... | collective-permute-start | bytes 884744 | tf_op jit(solution)/shard_map/ppermute | solution.py:200
  170.3 1.6 collective-permute-start.14
  170.4 2.4 collective-permute-start.4
  171.0 2.2 collective-permute-start.6
  171.1 2.5 collective-permute-start.8
  171.6 2.4 collective-permute-start.2
  214.7 20.3 %copy-start.2 = (bf16[1024]{0:T(1024)(128)(2,1)S(1)}, bf16[1024]{0:T(1024)(128)(2,1)}, u32[]{:S(2)}) copy-start(bf16[1024]{0:T(1024)(128)(2,1)} %param.17) | copy-start | bytes 6148
  227.1 0.9 copy-start
  227.9 22.1 %all-to-all-start = ((bf16[16,24,1024]{2,1,0:T(8,128)(2,1)}), bf16[16,24,1024]{2,1,0:T(8,128)(2,1)S(1)}, u32[]{:S(2)}, u32[]{:S(2)}) async-start(bf16[16,24,1024]{2,1,0:T(8,128)(2,1)} %bitcast.78), calls=%async_computation | async-start | bytes 1572864 | tf_op jit(solution)/shard_map/all_to_all | solution.py:245
Sparse Core Ops, SparseCore 0:
  9.2 205.4 all-gather.2

commit v10 on v9

--- a/solution.py
+++ b/solution.py
@@ -25,7 +25,7 @@
     return jnp.sum(jnp.where(picked, wanted[None, :], 0), axis=1)
 
 
-QUARTERS = 4
+PARTS = 8
 BACK = (0, 1, 7, 2, 6, 3, 5, 4)
 
 
@@ -71,13 +71,13 @@
     features = base.shape[1]
     shards, step, rank = down0.shape
     width = comp.shape[2]
-    block, half = shards // QUARTERS, rank // 2
+    block, half = shards // PARTS, rank // 2
 
     def bring(first, count, target, n):
         return pltpu.make_async_copy(weights.at[:, pl.ds(first, count), :], target, sems.at[n])
 
     early = []
-    for q in range(QUARTERS):
+    for q in range(PARTS):
         there, columns = pl.ds(q * block, block), pl.ds(q * block * step, block * step)
         early.append(
             pltpu.make_async_copy(tables.at[:, columns], base.at[:, columns], sems.at[3 * q])
@@ -90,20 +90,27 @@
                     sems.at[3 * q + 1 + h],
                 )
             )
-    n, at_up = 3 * QUARTERS, 4 * step
-    bring_up0 = bring(at_up, rank, up0, n)
+    n, at_up = 3 * PARTS, 4 * step
+    bring_up0 = []
+    for q in range(4):
+        there = pl.ds(q * shards // 4, shards // 4)
+        bring_up0.append(
+            pltpu.make_async_copy(
+                weights.at[there, pl.ds(at_up, rank), :], up0.at[there], sems.at[n + 5 + q]
+            )
+        )
     bring_down1 = [
         bring(2 * step * h + step, step, down1.at[:, :, pl.ds(h * half, half)], n + 1 + h)
         for h in range(2)
     ]
     bring_up1 = bring(at_up + rank, rank, up1, n + 3)
     bring_comp = bring(at_up + 2 * rank, step, comp, n + 4)
-    bring_over = bring(at_up + 2 * rank + step, over.shape[1], over, n + 5)
-    for copy in (*early, bring_up0, *bring_down1, bring_up1, bring_comp, bring_over):
+    bring_over = bring(at_up + 2 * rank + step, over.shape[1], over, n)
+    for copy in (*early, *bring_up0, *bring_down1, bring_up1, bring_comp, bring_over):
         copy.start()
 
     total = None
-    for q in range(QUARTERS):
+    for q in range(PARTS):
         for copy in early[3 * q : 3 * q + 3]:
             copy.wait()
         deep = block * step
@@ -114,8 +121,9 @@
         )
         total = part if total is None else total + part
     lowered = total.astype(BF16)
-    bring_up0.wait()
     for s in range(shards):
+        if s % (shards // 4) == 0:
+            bring_up0[s // (shards // 4)].wait()
         here = pl.ds(s * step, step)
         raised = jnp.dot(lowered, up0[s], preferred_element_type=F32)
         part = base[:, here].astype(F32)
@@ -234,7 +242,7 @@
                 pltpu.VMEM((shards, rank, step), BF16),
                 pltpu.VMEM((shards, step, width), BF16),
                 pltpu.VMEM((shards, columns, width), BF16),
-                pltpu.SemaphoreType.DMA((6 + 3 * QUARTERS,)),
+                pltpu.SemaphoreType.DMA((9 + 3 * PARTS,)),
             ],
         ),
         out_shape=jax.ShapeDtypeStruct((samples, outputs), BF16),

time: 258 us -> 258 us (level)
  no operation moved by 1% of the time
where the time goes in v10:
time: 258 us
  waiting for transfers between devices  190 us (74%)
  starting transfers between devices  22.9 us (9%)
  Pallas kernels  16.9 us (7%)
  between operations  13.9 us (5%)
  local copies, waits for them, and re-layouts  12.1 us (5%)
    ppermute x7, waiting for transfers between devices, on_device(): both = lax.ppermute(both, 'shard', moves)  134 us
    all_gather x1, waiting for transfers between devices, on_device(): weights = lax.all_gather(packed, 'shard', axis=0)  38.8 us
    all_to_all x1, waiting for transfers between devices, on_device(): lax.all_to_all(partial.reshape(towers, samples // towers, outputs), 'towe...  15 us
    ppermute x7, starting transfers between devices, on_device(): both = lax.ppermute(both, 'shard', moves)  14 us
    pallas_call x1, Pallas kernels, on_device(): pl.pallas_call(tower_kernel, grid_spec=pl.GridSpec(grid=(1,), in_specs=[a...  12.8 us
    all_to_all x1, starting transfers between devices, on_device(): lax.all_to_all(partial.reshape(towers, samples // towers, outputs), 'towe...  7.03 us
    squeeze x8, local copies, waits for them, and re-layouts, on_device(): theirs = lax.dynamic_index_in_dim(both, 1 - core, 1, keepdims=False)  6.65 us
  transfers between devices with their start and end apart: 17, of which 12 were waited for; matrix products, arithmetic and copies ran while one was open for 5% of the time, Pallas kernels for 1%

profile of v10, /device:TPU:96, one launch (start us, length us, event | category | flops | bytes accessed | tf_op | source)
XLA Modules:
  0.0 258.1 jit_solution(1986368345432109496)
XLA Ops:
  6.5 0.0 all-gather.3.cloned.1.call-start
  6.5 2.3 shard_map.101
  8.8 0.0 all-gather.3.cloned.1.call-update
  9.0 2.6 constant_dynamic-slice_fusion
  11.6 0.0 copy-start.4
  11.6 0.0 copy-start.3
  11.6 0.0 copy-start.1
  11.6 0.9 copy.40
  12.5 4.0 %collective-permute-start.9 = (bf16[3,2,384,128]{3,2,0,1:T(8,128)(2,1)}, bf16[3,2,384,128]{3,2,0,1:T(8,128)(2,1)}, u32[]{:S(2)}, u32[]{:S(2)}) collective-permute-start(bf16[3,2,384,128]{3,2,0,1:T(8,128)(2,1)} %bitcast.73), channel_id=1, source_target_pairs={{0,6},{1,7},{2,8},{3,9},{4,10},{5,11},{6,12},{7,13},{8,14},{9,15},... | collective-permute-start | bytes 1769480 | tf_op jit(solution)/shard_map/ppermute | solution.py:205
  16.6 0.1 collective-permute-start.11
  16.7 4.3 %collective-permute-start.13 = (bf16[3,2,384,128]{3,2,0,1:T(8,128)(2,1)S(1)}, bf16[3,2,384,128]{3,2,0,1:T(8,128)(2,1)}, u32[]{:S(2)}, u32[]{:S(2)}) collective-permute-start(bf16[3,2,384,128]{3,2,0,1:T(8,128)(2,1)S(1)} %bitcast.83), channel_id=1, source_target_pairs={{0,8},{1,9},{2,10},{3,11},{4,12},{5,13},{6,14},{7,15},{8,0},{9,1},... | collective-permute-start | bytes 1769480 | tf_op jit(solution)/shard_map/ppermute | solution.py:205
  21.1 2.3 collective-permute-start.3
  23.4 0.1 collective-permute-start.5
  23.6 0.9 copy.41
  24.5 0.0 copy-done.4
  24.5 0.0 copy-done.3
  24.6 0.0 copy-done.1
  24.6 0.3 convert_reduce_fusion.2
  24.9 0.7 bitcast_convert_fusion.bias
  25.6 1.1 dynamic-slice_bitcast_fusion.14
  26.7 0.1 select_reduce_fusion
  26.9 0.1 select_reduce_fusion.1
  27.0 40.6 %collective-permute-done.9 = bf16[3,2,384,128]{3,2,0,1:T(8,128)(2,1)} collective-permute-done((bf16[3,2,384,128]{3,2,0,1:T(8,128)(2,1)}, bf16[3,2,384,128]{3,2,0,1:T(8,128)(2,1)}, u32[]{:S(2)}, u32[]{:S(2)}) %collective-permute-start.9) | collective-permute-done | bytes 589856 | tf_op jit(solution)/shard_map/ppermute | solution.py:205
  67.6 2.3 collective-permute-start.7
  69.9 1.1 dynamic-slice_bitcast_fusion.4
  71.0 3.5 %collective-permute-done.11 = bf16[3,2,384,128]{3,2,0,1:T(8,128)(2,1)} collective-permute-done((bf16[3,2,384,128]{3,2,0,1:T(8,128)(2,1)S(1)}, bf16[3,2,384,128]{3,2,0,1:T(8,128)(2,1)}, u32[]{:S(2)}, u32[]{:S(2)}) %collective-permute-start.11) | collective-permute-done | bytes 589856 | tf_op jit(solution)/shard_map/ppermute | solution.py:205
  74.4 0.9 collective-permute-start.1
  75.3 1.1 dynamic-slice_bitcast_fusion.2
  76.4 32.8 %collective-permute-done.13 = bf16[3,2,384,128]{3,2,0,1:T(8,128)(2,1)} collective-permute-done((bf16[3,2,384,128]{3,2,0,1:T(8,128)(2,1)S(1)}, bf16[3,2,384,128]{3,2,0,1:T(8,128)(2,1)}, u32[]{:S(2)}, u32[]{:S(2)}) %collective-permute-start.13) | collective-permute-done | bytes 589856 | tf_op jit(solution)/shard_map/ppermute | solution.py:205
  109.2 0.0 collective-permute-start
  109.2 1.1 dynamic-slice_bitcast_fusion
  110.3 26.0 %collective-permute-done.3 = bf16[3,2,384,128]{3,2,0,1:T(8,128)(2,1)} collective-permute-done((bf16[3,2,384,128]{3,2,0,1:T(8,128)(2,1)S(1)}, bf16[3,2,384,128]{3,2,0,1:T(8,128)(2,1)}, u32[]{:S(2)}, u32[]{:S(2)}) %collective-permute-start.3) | collective-permute-done | bytes 589856 | tf_op jit(solution)/shard_map/ppermute | solution.py:205
  136.3 0.0 collective-permute-start.10
  136.3 1.1 dynamic-slice_bitcast_fusion.10
  137.4 0.0 collective-permute-done.5
  137.5 0.6 collective-permute-start.12
  138.0 1.1 dynamic-slice_bitcast_fusion.8
  139.2 31.2 %collective-permute-done.7 = bf16[3,2,384,128]{3,2,0,1:T(8,128)(2,1)S(1)} collective-permute-done((bf16[3,2,384,128]{3,2,0,1:T(8,128)(2,1)}, bf16[3,2,384,128]{3,2,0,1:T(8,128)(2,1)S(1)}, u32[]{:S(2)}, u32[]{:S(2)}) %collective-permute-start.7) | collective-permute-done | bytes 589856 | tf_op jit(solution)/shard_map/ppermute | solution.py:205
  170.3 0.0 collective-permute-start.14
  170.4 0.0 collective-permute-done.1
  170.4 0.6 collective-permute-start.4
  171.0 0.0 collective-permute-done.refs_1_
  171.0 0.1 collective-permute-start.6
  171.1 0.0 collective-permute-done.10.refs_11_
  171.1 0.5 collective-permute-start.8
  171.6 0.0 collective-permute-done.12.refs_13_
  171.6 0.1 collective-permute-start.2
  171.7 0.1 pad_add_fusion.places
  171.8 0.1 collective-permute-done.14.refs_15_
  171.9 0.8 collective-permute-done.4.refs_5_
  172.8 0.4 collective-permute-done.6.refs_7_
  173.2 0.4 collective-permute-done.8.refs_9_
  173.6 0.4 collective-permute-done.2.refs_3_
  174.0 1.8 shard_map.100.tables
  175.9 38.8 %all-gather.3.cloned.1.call-done = bf16[37888,256]{1,0:T(8,128)(2,1)} async-done(((bf16[2368,256]{1,0:T(8,128)(2,1)}), bf16[37888,256]{1,0:T(8,128)(2,1)}) %all-gather.3.cloned.1.call-update) | async-done | bytes 19398672 | tf_op jit(solution)/shard_map/all_gather | solution.py:195
  214.7 0.0 copy-start.2
  214.7 12.8 %shard_map.102 = bf16[384,1024]{1,0:T(8,128)(2,1)S(1)} custom-call(bf16[384,4096]{1,0:T(8,128)(2,1)S(1)} %shard_map.100.tables, bf16[16,2368,256]{2,1,0:T(8,128)(2,1)} %bitcast.91, f32[2,4096]{1,0:T(2,128)S(1)} %bitcast_convert_fusion.bias, f32[1,256]{1,0:T(1,128)S(1)} %convert_element_type.34.comp_bias), custom_call_target="tpu_custom_call" | custom-call | flops 8000000000 | bytes 24000000 | tf_op jit(solution)/shard_map/pallas_call | solution.py:230
  227.5 0.0 copy-start
  227.5 0.9 copy-done
  228.4 7.0 %all-to-all-start = ((bf16[16,24,1024]{2,1,0:T(8,128)(2,1)}), bf16[16,24,1024]{2,1,0:T(8,128)(2,1)S(1)}, u32[]{:S(2)}, u32[]{:S(2)}) async-start(bf16[16,24,1024]{2,1,0:T(8,128)(2,1)} %bitcast.78), calls=%async_computation | async-start | bytes 1572864 | tf_op jit(solution)/shard_map/all_to_all | solution.py:253
  235.4 0.0 copy-done.2
  235.4 15.0 %all-to-all-done = bf16[16,24,1024]{2,1,0:T(8,128)(2,1)S(1)} async-done(((bf16[16,24,1024]{2,1,0:T(8,128)(2,1)}), bf16[16,24,1024]{2,1,0:T(8,128)(2,1)S(1)}, u32[]{:S(2)}, u32[]{:S(2)}) %all-to-all-start) | async-done | bytes 786464 | tf_op jit(solution)/shard_map/all_to_all | solution.py:253
  250.5 0.1 convert_reduce_fusion
  250.6 0.6 fusion.3
  (13 shorter events, 0.3 us)
Async XLA Ops:
  6.5 208.1 %all-gather.3.cloned.1.call-start = ((), (), s32[]{:S(2)}) async-start(), calls=%async_computation.1 | async-start | bytes 20611072 | tf_op jit(solution)/shard_map/all_gather | solution.py:195
  11.6 12.9 %copy-start.4 = (bf16[1,256]{1,0:T(2,128)(2,1)S(1)}, bf16[1,256]{1,0:T(2,128)(2,1)}, u32[]{:S(2)}) copy-start(bf16[1,256]{1,0:T(2,128)(2,1)} %param.15) | copy-start | bytes 1540
  11.6 13.0 %copy-start.3 = (s32[512]{0:T(512)S(1)}, s32[512]{0:T(512)}, u32[]{:S(2)}) copy-start(s32[512]{0:T(512)} %param.18) | copy-start | bytes 6148
  11.6 13.0 %copy-start.1 = (s32[512]{0:T(512)S(1)}, s32[512]{0:T(512)}, u32[]{:S(2)}) copy-start(s32[512]{0:T(512)} %param.19) | copy-start | bytes 6148
  12.5 55.1 %collective-permute-start.9 = (bf16[3,2,384,128]{3,2,0,1:T(8,128)(2,1)}, bf16[3,2,384,128]{3,2,0,1:T(8,128)(2,1)}, u32[]{:S(2)}, u32[]{:S(2)}) collective-permute-start(bf16[3,2,384,128]{3,2,0,1:T(8,128)(2,1)} %bitcast.73), channel_id=1, source_target_pairs={{0,6},{1,7},{2,8},{3,9},{4,10},{5,11},{6,12},{7,13},{8,14},{9,15},... | collective-permute-start | bytes 1769480 | tf_op jit(solution)/shard_map/ppermute | solution.py:205
  16.6 57.9 %collective-permute-start.11 = (bf16[3,2,384,128]{3,2,0,1:T(8,128)(2,1)S(1)}, bf16[3,2,384,128]{3,2,0,1:T(8,128)(2,1)}, u32[]{:S(2)}, u32[]{:S(2)}) collective-permute-start(bf16[3,2,384,128]{3,2,0,1:T(8,128)(2,1)S(1)} %bitcast.84), channel_id=1, source_target_pairs={{0,10},{1,11},{2,12},{3,13},{4,14},{5,15},{6,0},{7,1},{8,2},{9,3},... | collective-permute-start | bytes 1769480 | tf_op jit(solution)/shard_map/ppermute | solution.py:205
  16.7 92.5 %collective-permute-start.13 = (bf16[3,2,384,128]{3,2,0,1:T(8,128)(2,1)S(1)}, bf16[3,2,384,128]{3,2,0,1:T(8,128)(2,1)}, u32[]{:S(2)}, u32[]{:S(2)}) collective-permute-start(bf16[3,2,384,128]{3,2,0,1:T(8,128)(2,1)S(1)} %bitcast.83), channel_id=1, source_target_pairs={{0,8},{1,9},{2,10},{3,11},{4,12},{5,13},{6,14},{7,15},{8,0},{9,1},... | collective-permute-start | bytes 1769480 | tf_op jit(solution)/shard_map/ppermute | solution.py:205
  21.1 115.3 %collective-permute-start.3 = (bf16[3,2,384,128]{3,2,0,1:T(8,128)(2,1)S(1)}, bf16[3,2,384,128]{3,2,0,1:T(8,128)(2,1)}, u32[]{:S(2)}, u32[]{:S(2)}) collective-permute-start(bf16[3,2,384,128]{3,2,0,1:T(8,128)(2,1)S(1)} %bitcast.82), channel_id=1, source_target_pairs={{0,14},{1,15},{2,0},{3,1},{4,2},{5,3},{6,4},{7,5},{8,6},{9,7},{10,... | collective-permute-start | bytes 1769480 | tf_op jit(solution)/shard_map/ppermute | solution.py:205
  23.4 114.0 %collective-permute-start.5 = (bf16[3,2,384,128]{3,2,0,1:T(8,128)(2,1)S(1)}, bf16[3,2,384,128]{3,2,0,1:T(8,128)(2,1)}, u32[]{:S(2)}, u32[]{:S(2)}) collective-permute-start(bf16[3,2,384,128]{3,2,0,1:T(8,128)(2,1)S(1)} %bitcast.81), channel_id=1, source_target_pairs={{0,4},{1,5},{2,6},{3,7},{4,8},{5,9},{6,10},{7,11},{8,12},{9,13},{1... | collective-permute-start | bytes 1769480 | tf_op jit(solution)/shard_map/ppermute | solution.py:205
  67.6 102.7 %collective-permute-start.7 = (bf16[3,2,384,128]{3,2,0,1:T(8,128)(2,1)}, bf16[3,2,384,128]{3,2,0,1:T(8,128)(2,1)S(1)}, u32[]{:S(2)}, u32[]{:S(2)}) collective-permute-start(bf16[3,2,384,128]{3,2,0,1:T(8,128)(2,1)} %bitcast.86), channel_id=1, source_target_pairs={{0,12},{1,13},{2,14},{3,15},{4,0},{5,1},{6,2},{7,3},{8,4},{9,5},{1... | collective-permute-start | bytes 1769480 | tf_op jit(solution)/shard_map/ppermute | solution.py:205
  74.4 95.9 %collective-permute-start.1 = (bf16[3,2,384,128]{3,2,0,1:T(8,128)(2,1)S(1)}, bf16[3,2,384,128]{3,2,0,1:T(8,128)(2,1)S(1)}, u32[]{:S(2)}, u32[]{:S(2)}) collective-permute-start(bf16[3,2,384,128]{3,2,0,1:T(8,128)(2,1)S(1)} %bitcast.85), channel_id=1, source_target_pairs={{0,2},{1,3},{2,4},{3,5},{4,6},{5,7},{6,8},{7,9},{8,10},{9,11},{10,... | collective-permute-start | bytes 1769480 | tf_op jit(solution)/shard_map/ppermute | solution.py:205
  109.2 61.8 %collective-permute-start = (bf16[3,384,128]{2,1,0:T(8,128)(2,1)S(1)}, bf16[3,384,128]{2,1,0:T(8,128)(2,1)S(1)}, u32[]{:S(2)}, u32[]{:S(2)}) collective-permute-start(bf16[3,384,128]{2,1,0:T(8,128)(2,1)S(1)} %get-tuple-element.14), channel_id=1, source_target_pairs={{0,1},{1,0},{2,3},{3,2},{4,5},{5,4},{6,7},{7,6},{8,9},{9,8},{10,11... | collective-permute-start | bytes 884744 | tf_op jit(solution)/shard_map/ppermute | solution.py:208
  136.3 34.8 %collective-permute-start.10 = (bf16[3,384,128]{2,1,0:T(8,128)(2,1)S(1)}, bf16[3,384,128]{2,1,0:T(8,128)(2,1)S(1)}, u32[]{:S(2)}, u32[]{:S(2)}) collective-permute-start(bf16[3,384,128]{2,1,0:T(8,128)(2,1)S(1)} %get-tuple-element.20), channel_id=1, source_target_pairs={{0,1},{1,0},{2,3},{3,2},{4,5},{5,4},{6,7},{7,6},{8,9},{9,8},{10,11... | collective-permute-start | bytes 884744 | tf_op jit(solution)/shard_map/ppermute | solution.py:208
  137.5 34.2 %collective-permute-start.12 = (bf16[3,384,128]{2,1,0:T(8,128)(2,1)S(1)}, bf16[3,384,128]{2,1,0:T(8,128)(2,1)S(1)}, u32[]{:S(2)}, u32[]{:S(2)}) collective-permute-start(bf16[3,384,128]{2,1,0:T(8,128)(2,1)S(1)} %get-tuple-element.18), channel_id=1, source_target_pairs={{0,1},{1,0},{2,3},{3,2},{4,5},{5,4},{6,7},{7,6},{8,9},{9,8},{10,11... | collective-permute-start | bytes 884744 | tf_op jit(solution)/shard_map/ppermute | solution.py:208
  170.3 1.6 collective-permute-start.14
  170.4 2.4 collective-permute-start.4
  171.0 2.2 collective-permute-start.6
  171.1 2.5 collective-permute-start.8
  171.6 2.4 collective-permute-start.2
  214.7 20.7 %copy-start.2 = (bf16[1024]{0:T(1024)(128)(2,1)S(1)}, bf16[1024]{0:T(1024)(128)(2,1)}, u32[]{:S(2)}) copy-start(bf16[1024]{0:T(1024)(128)(2,1)} %param.17) | copy-start | bytes 6148
  227.5 0.9 copy-start
  228.4 22.1 %all-to-all-start = ((bf16[16,24,1024]{2,1,0:T(8,128)(2,1)}), bf16[16,24,1024]{2,1,0:T(8,128)(2,1)S(1)}, u32[]{:S(2)}, u32[]{:S(2)}) async-start(bf16[16,24,1024]{2,1,0:T(8,128)(2,1)} %bitcast.78), calls=%async_computation | async-start | bytes 1572864 | tf_op jit(solution)/shard_map/all_to_all | solution.py:253
Sparse Core Ops, SparseCore 0:
  9.2 205.4 all-gather.2

commit v11 on v9

--- a/solution.py
+++ b/solution.py
@@ -25,7 +25,7 @@
     return jnp.sum(jnp.where(picked, wanted[None, :], 0), axis=1)
 
 
-QUARTERS = 4
+PARTS = 2
 BACK = (0, 1, 7, 2, 6, 3, 5, 4)
 
 
@@ -71,13 +71,13 @@
     features = base.shape[1]
     shards, step, rank = down0.shape
     width = comp.shape[2]
-    block, half = shards // QUARTERS, rank // 2
+    block, half = shards // PARTS, rank // 2
 
     def bring(first, count, target, n):
         return pltpu.make_async_copy(weights.at[:, pl.ds(first, count), :], target, sems.at[n])
 
     early = []
-    for q in range(QUARTERS):
+    for q in range(PARTS):
         there, columns = pl.ds(q * block, block), pl.ds(q * block * step, block * step)
         early.append(
             pltpu.make_async_copy(tables.at[:, columns], base.at[:, columns], sems.at[3 * q])
@@ -90,7 +90,7 @@
                     sems.at[3 * q + 1 + h],
                 )
             )
-    n, at_up = 3 * QUARTERS, 4 * step
+    n, at_up = 3 * PARTS, 4 * step
     bring_up0 = bring(at_up, rank, up0, n)
     bring_down1 = [
         bring(2 * step * h + step, step, down1.at[:, :, pl.ds(h * half, half)], n + 1 + h)
@@ -103,7 +103,7 @@
         copy.start()
 
     total = None
-    for q in range(QUARTERS):
+    for q in range(PARTS):
         for copy in early[3 * q : 3 * q + 3]:
             copy.wait()
         deep = block * step
@@ -234,7 +234,7 @@
                 pltpu.VMEM((shards, rank, step), BF16),
                 pltpu.VMEM((shards, step, width), BF16),
                 pltpu.VMEM((shards, columns, width), BF16),
-                pltpu.SemaphoreType.DMA((6 + 3 * QUARTERS,)),
+                pltpu.SemaphoreType.DMA((6 + 3 * PARTS,)),
             ],
         ),
         out_shape=jax.ShapeDtypeStruct((samples, outputs), BF16),

time: 258 us -> 259 us (level)
  no operation moved by 1% of the time
where the time goes in v11:
time: 259 us; the launch traced here: 258 us
  waiting for transfers between devices  190 us (73%)
  starting transfers between devices  22.9 us (9%)
  Pallas kernels  17 us (7%)
  between operations  13.9 us (5%)
  local copies, waits for them, and re-layouts  12.1 us (5%)
    ppermute x7, waiting for transfers between devices, on_device(): both = lax.ppermute(both, 'shard', moves)  134 us
    all_gather x1, waiting for transfers between devices, on_device(): weights = lax.all_gather(packed, 'shard', axis=0)  38.8 us
    all_to_all x1, waiting for transfers between devices, on_device(): lax.all_to_all(partial.reshape(towers, samples // towers, outputs), 'towe...  15 us
    ppermute x7, starting transfers between devices, on_device(): both = lax.ppermute(both, 'shard', moves)  14 us
    pallas_call x1, Pallas kernels, on_device(): pl.pallas_call(tower_kernel, grid_spec=pl.GridSpec(grid=(1,), in_specs=[a...  12.9 us
    all_to_all x1, starting transfers between devices, on_device(): lax.all_to_all(partial.reshape(towers, samples // towers, outputs), 'towe...  7.03 us
    squeeze x8, local copies, waits for them, and re-layouts, on_device(): theirs = lax.dynamic_index_in_dim(both, 1 - core, 1, keepdims=False)  6.65 us
  transfers between devices with their start and end apart: 17, of which 12 were waited for; matrix products, arithmetic and copies ran while one was open for 5% of the time, Pallas kernels for 1%

profile of v11, /device:TPU:96, one launch (start us, length us, event | category | flops | bytes accessed | tf_op | source)
XLA Modules:
  0.0 258.2 jit_solution(14564061303887292639)
XLA Ops:
  6.5 0.0 all-gather.3.cloned.1.call-start
  6.5 2.3 shard_map.101
  8.8 0.0 all-gather.3.cloned.1.call-update
  9.0 2.6 constant_dynamic-slice_fusion
  11.6 0.0 copy-start.4
  11.6 0.0 copy-start.3
  11.6 0.0 copy-start.1
  11.6 0.9 copy.40
  12.5 4.0 %collective-permute-start.9 = (bf16[3,2,384,128]{3,2,0,1:T(8,128)(2,1)}, bf16[3,2,384,128]{3,2,0,1:T(8,128)(2,1)}, u32[]{:S(2)}, u32[]{:S(2)}) collective-permute-start(bf16[3,2,384,128]{3,2,0,1:T(8,128)(2,1)} %bitcast.73), channel_id=1, source_target_pairs={{0,6},{1,7},{2,8},{3,9},{4,10},{5,11},{6,12},{7,13},{8,14},{9,15},... | collective-permute-start | bytes 1769480 | tf_op jit(solution)/shard_map/ppermute | solution.py:197
  16.6 0.1 collective-permute-start.11
  16.7 4.3 %collective-permute-start.13 = (bf16[3,2,384,128]{3,2,0,1:T(8,128)(2,1)S(1)}, bf16[3,2,384,128]{3,2,0,1:T(8,128)(2,1)}, u32[]{:S(2)}, u32[]{:S(2)}) collective-permute-start(bf16[3,2,384,128]{3,2,0,1:T(8,128)(2,1)S(1)} %bitcast.83), channel_id=1, source_target_pairs={{0,8},{1,9},{2,10},{3,11},{4,12},{5,13},{6,14},{7,15},{8,0},{9,1},... | collective-permute-start | bytes 1769480 | tf_op jit(solution)/shard_map/ppermute | solution.py:197
  21.1 2.3 collective-permute-start.3
  23.4 0.1 collective-permute-start.5
  23.6 0.9 copy.41
  24.5 0.0 copy-done.4
  24.5 0.0 copy-done.3
  24.6 0.0 copy-done.1
  24.6 0.3 convert_reduce_fusion.2
  24.9 0.7 bitcast_convert_fusion.bias
  25.6 1.1 dynamic-slice_bitcast_fusion.14
  26.7 0.1 select_reduce_fusion
  26.9 0.1 select_reduce_fusion.1
  27.0 40.6 %collective-permute-done.9 = bf16[3,2,384,128]{3,2,0,1:T(8,128)(2,1)} collective-permute-done((bf16[3,2,384,128]{3,2,0,1:T(8,128)(2,1)}, bf16[3,2,384,128]{3,2,0,1:T(8,128)(2,1)}, u32[]{:S(2)}, u32[]{:S(2)}) %collective-permute-start.9) | collective-permute-done | bytes 589856 | tf_op jit(solution)/shard_map/ppermute | solution.py:197
  67.6 2.3 collective-permute-start.7
  69.9 1.1 dynamic-slice_bitcast_fusion.4
  71.0 3.5 %collective-permute-done.11 = bf16[3,2,384,128]{3,2,0,1:T(8,128)(2,1)} collective-permute-done((bf16[3,2,384,128]{3,2,0,1:T(8,128)(2,1)S(1)}, bf16[3,2,384,128]{3,2,0,1:T(8,128)(2,1)}, u32[]{:S(2)}, u32[]{:S(2)}) %collective-permute-start.11) | collective-permute-done | bytes 589856 | tf_op jit(solution)/shard_map/ppermute | solution.py:197
  74.4 0.9 collective-permute-start.1
  75.3 1.1 dynamic-slice_bitcast_fusion.2
  76.4 32.8 %collective-permute-done.13 = bf16[3,2,384,128]{3,2,0,1:T(8,128)(2,1)} collective-permute-done((bf16[3,2,384,128]{3,2,0,1:T(8,128)(2,1)S(1)}, bf16[3,2,384,128]{3,2,0,1:T(8,128)(2,1)}, u32[]{:S(2)}, u32[]{:S(2)}) %collective-permute-start.13) | collective-permute-done | bytes 589856 | tf_op jit(solution)/shard_map/ppermute | solution.py:197
  109.2 0.0 collective-permute-start
  109.2 1.1 dynamic-slice_bitcast_fusion
  110.3 26.0 %collective-permute-done.3 = bf16[3,2,384,128]{3,2,0,1:T(8,128)(2,1)} collective-permute-done((bf16[3,2,384,128]{3,2,0,1:T(8,128)(2,1)S(1)}, bf16[3,2,384,128]{3,2,0,1:T(8,128)(2,1)}, u32[]{:S(2)}, u32[]{:S(2)}) %collective-permute-start.3) | collective-permute-done | bytes 589856 | tf_op jit(solution)/shard_map/ppermute | solution.py:197
  136.3 0.0 collective-permute-start.10
  136.3 1.1 dynamic-slice_bitcast_fusion.10
  137.4 0.0 collective-permute-done.5
  137.5 0.6 collective-permute-start.12
  138.0 1.1 dynamic-slice_bitcast_fusion.8
  139.2 31.2 %collective-permute-done.7 = bf16[3,2,384,128]{3,2,0,1:T(8,128)(2,1)S(1)} collective-permute-done((bf16[3,2,384,128]{3,2,0,1:T(8,128)(2,1)}, bf16[3,2,384,128]{3,2,0,1:T(8,128)(2,1)S(1)}, u32[]{:S(2)}, u32[]{:S(2)}) %collective-permute-start.7) | collective-permute-done | bytes 589856 | tf_op jit(solution)/shard_map/ppermute | solution.py:197
  170.3 0.0 collective-permute-start.14
  170.4 0.0 collective-permute-done.1
  170.4 0.6 collective-permute-start.4
  171.0 0.0 collective-permute-done.refs_1_
  171.0 0.1 collective-permute-start.6
  171.1 0.0 collective-permute-done.10.refs_11_
  171.1 0.5 collective-permute-start.8
  171.6 0.0 collective-permute-done.12.refs_13_
  171.6 0.1 collective-permute-start.2
  171.7 0.1 pad_add_fusion.places
  171.8 0.1 collective-permute-done.14.refs_15_
  171.9 0.8 collective-permute-done.4.refs_5_
  172.8 0.4 collective-permute-done.6.refs_7_
  173.2 0.4 collective-permute-done.8.refs_9_
  173.6 0.4 collective-permute-done.2.refs_3_
  174.0 1.8 shard_map.100.tables
  175.9 38.8 %all-gather.3.cloned.1.call-done = bf16[37888,256]{1,0:T(8,128)(2,1)} async-done(((bf16[2368,256]{1,0:T(8,128)(2,1)}), bf16[37888,256]{1,0:T(8,128)(2,1)}) %all-gather.3.cloned.1.call-update) | async-done | bytes 19398672 | tf_op jit(solution)/shard_map/all_gather | solution.py:187
  214.7 0.0 copy-start.2
  214.7 12.9 %shard_map.102 = bf16[384,1024]{1,0:T(8,128)(2,1)S(1)} custom-call(bf16[384,4096]{1,0:T(8,128)(2,1)S(1)} %shard_map.100.tables, bf16[16,2368,256]{2,1,0:T(8,128)(2,1)} %bitcast.91, f32[2,4096]{1,0:T(2,128)S(1)} %bitcast_convert_fusion.bias, f32[1,256]{1,0:T(1,128)S(1)} %convert_element_type.34.comp_bias), custom_call_target="tpu_custom_call" | custom-call | flops 8000000000 | bytes 24000000 | tf_op jit(solution)/shard_map/pallas_call | solution.py:222
  227.6 0.0 copy-start
  227.6 0.9 copy-done
  228.5 7.0 %all-to-all-start = ((bf16[16,24,1024]{2,1,0:T(8,128)(2,1)}), bf16[16,24,1024]{2,1,0:T(8,128)(2,1)S(1)}, u32[]{:S(2)}, u32[]{:S(2)}) async-start(bf16[16,24,1024]{2,1,0:T(8,128)(2,1)} %bitcast.78), calls=%async_computation | async-start | bytes 1572864 | tf_op jit(solution)/shard_map/all_to_all | solution.py:245
  235.5 0.0 copy-done.2
  235.6 15.0 %all-to-all-done = bf16[16,24,1024]{2,1,0:T(8,128)(2,1)S(1)} async-done(((bf16[16,24,1024]{2,1,0:T(8,128)(2,1)}), bf16[16,24,1024]{2,1,0:T(8,128)(2,1)S(1)}, u32[]{:S(2)}, u32[]{:S(2)}) %all-to-all-start) | async-done | bytes 786464 | tf_op jit(solution)/shard_map/all_to_all | solution.py:245
  250.6 0.1 convert_reduce_fusion
  250.7 0.6 fusion.3
  (13 shorter events, 0.3 us)
Async XLA Ops:
  6.5 208.1 %all-gather.3.cloned.1.call-start = ((), (), s32[]{:S(2)}) async-start(), calls=%async_computation.1 | async-start | bytes 20611072 | tf_op jit(solution)/shard_map/all_gather | solution.py:187
  11.6 12.9 %copy-start.4 = (bf16[1,256]{1,0:T(2,128)(2,1)S(1)}, bf16[1,256]{1,0:T(2,128)(2,1)}, u32[]{:S(2)}) copy-start(bf16[1,256]{1,0:T(2,128)(2,1)} %param.15) | copy-start | bytes 1540
  11.6 13.0 %copy-start.3 = (s32[512]{0:T(512)S(1)}, s32[512]{0:T(512)}, u32[]{:S(2)}) copy-start(s32[512]{0:T(512)} %param.18) | copy-start | bytes 6148
  11.6 13.0 %copy-start.1 = (s32[512]{0:T(512)S(1)}, s32[512]{0:T(512)}, u32[]{:S(2)}) copy-start(s32[512]{0:T(512)} %param.19) | copy-start | bytes 6148
  12.5 55.1 %collective-permute-start.9 = (bf16[3,2,384,128]{3,2,0,1:T(8,128)(2,1)}, bf16[3,2,384,128]{3,2,0,1:T(8,128)(2,1)}, u32[]{:S(2)}, u32[]{:S(2)}) collective-permute-start(bf16[3,2,384,128]{3,2,0,1:T(8,128)(2,1)} %bitcast.73), channel_id=1, source_target_pairs={{0,6},{1,7},{2,8},{3,9},{4,10},{5,11},{6,12},{7,13},{8,14},{9,15},... | collective-permute-start | bytes 1769480 | tf_op jit(solution)/shard_map/ppermute | solution.py:197
  16.6 57.9 %collective-permute-start.11 = (bf16[3,2,384,128]{3,2,0,1:T(8,128)(2,1)S(1)}, bf16[3,2,384,128]{3,2,0,1:T(8,128)(2,1)}, u32[]{:S(2)}, u32[]{:S(2)}) collective-permute-start(bf16[3,2,384,128]{3,2,0,1:T(8,128)(2,1)S(1)} %bitcast.84), channel_id=1, source_target_pairs={{0,10},{1,11},{2,12},{3,13},{4,14},{5,15},{6,0},{7,1},{8,2},{9,3},... | collective-permute-start | bytes 1769480 | tf_op jit(solution)/shard_map/ppermute | solution.py:197
  16.7 92.5 %collective-permute-start.13 = (bf16[3,2,384,128]{3,2,0,1:T(8,128)(2,1)S(1)}, bf16[3,2,384,128]{3,2,0,1:T(8,128)(2,1)}, u32[]{:S(2)}, u32[]{:S(2)}) collective-permute-start(bf16[3,2,384,128]{3,2,0,1:T(8,128)(2,1)S(1)} %bitcast.83), channel_id=1, source_target_pairs={{0,8},{1,9},{2,10},{3,11},{4,12},{5,13},{6,14},{7,15},{8,0},{9,1},... | collective-permute-start | bytes 1769480 | tf_op jit(solution)/shard_map/ppermute | solution.py:197
  21.1 115.3 %collective-permute-start.3 = (bf16[3,2,384,128]{3,2,0,1:T(8,128)(2,1)S(1)}, bf16[3,2,384,128]{3,2,0,1:T(8,128)(2,1)}, u32[]{:S(2)}, u32[]{:S(2)}) collective-permute-start(bf16[3,2,384,128]{3,2,0,1:T(8,128)(2,1)S(1)} %bitcast.82), channel_id=1, source_target_pairs={{0,14},{1,15},{2,0},{3,1},{4,2},{5,3},{6,4},{7,5},{8,6},{9,7},{10,... | collective-permute-start | bytes 1769480 | tf_op jit(solution)/shard_map/ppermute | solution.py:197
  23.4 114.0 %collective-permute-start.5 = (bf16[3,2,384,128]{3,2,0,1:T(8,128)(2,1)S(1)}, bf16[3,2,384,128]{3,2,0,1:T(8,128)(2,1)}, u32[]{:S(2)}, u32[]{:S(2)}) collective-permute-start(bf16[3,2,384,128]{3,2,0,1:T(8,128)(2,1)S(1)} %bitcast.81), channel_id=1, source_target_pairs={{0,4},{1,5},{2,6},{3,7},{4,8},{5,9},{6,10},{7,11},{8,12},{9,13},{1... | collective-permute-start | bytes 1769480 | tf_op jit(solution)/shard_map/ppermute | solution.py:197
  67.6 102.7 %collective-permute-start.7 = (bf16[3,2,384,128]{3,2,0,1:T(8,128)(2,1)}, bf16[3,2,384,128]{3,2,0,1:T(8,128)(2,1)S(1)}, u32[]{:S(2)}, u32[]{:S(2)}) collective-permute-start(bf16[3,2,384,128]{3,2,0,1:T(8,128)(2,1)} %bitcast.86), channel_id=1, source_target_pairs={{0,12},{1,13},{2,14},{3,15},{4,0},{5,1},{6,2},{7,3},{8,4},{9,5},{1... | collective-permute-start | bytes 1769480 | tf_op jit(solution)/shard_map/ppermute | solution.py:197
  74.4 95.9 %collective-permute-start.1 = (bf16[3,2,384,128]{3,2,0,1:T(8,128)(2,1)S(1)}, bf16[3,2,384,128]{3,2,0,1:T(8,128)(2,1)S(1)}, u32[]{:S(2)}, u32[]{:S(2)}) collective-permute-start(bf16[3,2,384,128]{3,2,0,1:T(8,128)(2,1)S(1)} %bitcast.85), channel_id=1, source_target_pairs={{0,2},{1,3},{2,4},{3,5},{4,6},{5,7},{6,8},{7,9},{8,10},{9,11},{10,... | collective-permute-start | bytes 1769480 | tf_op jit(solution)/shard_map/ppermute | solution.py:197
  109.2 61.8 %collective-permute-start = (bf16[3,384,128]{2,1,0:T(8,128)(2,1)S(1)}, bf16[3,384,128]{2,1,0:T(8,128)(2,1)S(1)}, u32[]{:S(2)}, u32[]{:S(2)}) collective-permute-start(bf16[3,384,128]{2,1,0:T(8,128)(2,1)S(1)} %get-tuple-element.14), channel_id=1, source_target_pairs={{0,1},{1,0},{2,3},{3,2},{4,5},{5,4},{6,7},{7,6},{8,9},{9,8},{10,11... | collective-permute-start | bytes 884744 | tf_op jit(solution)/shard_map/ppermute | solution.py:200
  136.3 34.8 %collective-permute-start.10 = (bf16[3,384,128]{2,1,0:T(8,128)(2,1)S(1)}, bf16[3,384,128]{2,1,0:T(8,128)(2,1)S(1)}, u32[]{:S(2)}, u32[]{:S(2)}) collective-permute-start(bf16[3,384,128]{2,1,0:T(8,128)(2,1)S(1)} %get-tuple-element.20), channel_id=1, source_target_pairs={{0,1},{1,0},{2,3},{3,2},{4,5},{5,4},{6,7},{7,6},{8,9},{9,8},{10,11... | collective-permute-start | bytes 884744 | tf_op jit(solution)/shard_map/ppermute | solution.py:200
  137.5 34.2 %collective-permute-start.12 = (bf16[3,384,128]{2,1,0:T(8,128)(2,1)S(1)}, bf16[3,384,128]{2,1,0:T(8,128)(2,1)S(1)}, u32[]{:S(2)}, u32[]{:S(2)}) collective-permute-start(bf16[3,384,128]{2,1,0:T(8,128)(2,1)S(1)} %get-tuple-element.18), channel_id=1, source_target_pairs={{0,1},{1,0},{2,3},{3,2},{4,5},{5,4},{6,7},{7,6},{8,9},{9,8},{10,11... | collective-permute-start | bytes 884744 | tf_op jit(solution)/shard_map/ppermute | solution.py:200
  170.3 1.6 collective-permute-start.14
  170.4 2.4 collective-permute-start.4
  171.0 2.2 collective-permute-start.6
  171.1 2.5 collective-permute-start.8
  171.6 2.4 collective-permute-start.2
  214.7 20.9 %copy-start.2 = (bf16[1024]{0:T(1024)(128)(2,1)S(1)}, bf16[1024]{0:T(1024)(128)(2,1)}, u32[]{:S(2)}) copy-start(bf16[1024]{0:T(1024)(128)(2,1)} %param.17) | copy-start | bytes 6148
  227.6 0.9 copy-start
  228.5 22.1 %all-to-all-start = ((bf16[16,24,1024]{2,1,0:T(8,128)(2,1)}), bf16[16,24,1024]{2,1,0:T(8,128)(2,1)S(1)}, u32[]{:S(2)}, u32[]{:S(2)}) async-start(bf16[16,24,1024]{2,1,0:T(8,128)(2,1)} %bitcast.78), calls=%async_computation | async-start | bytes 1572864 | tf_op jit(solution)/shard_map/all_to_all | solution.py:245
Sparse Core Ops, SparseCore 0:
  9.2 205.4 all-gather.2
